TPU v7x, 32 devices: a whole 2x2x4 slice. The times are simulated.
32 devices in a mesh: dp: 8 (over z, x), mp: 4 (over y, core).
Axes of the slice: x: 2, y: 2, z: 4, core: 2. Of those that a mesh axis runs over, the one named last changes fastest.
Arguments:
- encoder_input: bfloat16 [8, 1024, 768], P('dp'), may hold values from -6 to 6
- decoder_input: bfloat16 [8, 1024, 768], P('dp'), may hold values from -6 to 6
- encoder_lengths: int32 [8, 8], P('dp'), may hold values from 1 to 384, 1024 in all within a row
- decoder_lengths: int32 [8, 8], P('dp'), may hold values from 1 to 384, 1024 in all within a row
- encoder_buckets: int32 [2047], replicated, may hold values from 0 to 31
- decoder_buckets: int32 [1024], replicated, may hold values from 0 to 31
- encoder_attn_gain: float32 [768], replicated, may hold values from 0.5 to 1.5
- encoder_query: bfloat16 [768, 768], P(None, 'mp'), may hold values from -0.21875 to 0.21875
- encoder_key: bfloat16 [768, 768], P(None, 'mp'), may hold values from -0.21875 to 0.21875
- encoder_value: bfloat16 [768, 768], P(None, 'mp'), may hold values from -0.21875 to 0.21875
- encoder_output: bfloat16 [768, 768], P('mp'), may hold values from -0.75 to 0.75
- encoder_bias: float32 [32, 12], P(None, 'mp'), may hold values from -4 to 4
- encoder_ffn_gain: float32 [768], replicated, may hold values from 0.5 to 1.5
- encoder_ffn_in: bfloat16 [768, 3072], P(None, 'mp'), may hold values from -0.21875 to 0.21875
- encoder_ffn_out: bfloat16 [3072, 768], P('mp'), may hold values from -0.109375 to 0.109375
- decoder_attn_gain: float32 [768], replicated, may hold values from 0.5 to 1.5
- decoder_query: bfloat16 [768, 768], P(None, 'mp'), may hold values from -0.21875 to 0.21875
- decoder_key: bfloat16 [768, 768], P(None, 'mp'), may hold values from -0.21875 to 0.21875
- decoder_value: bfloat16 [768, 768], P(None, 'mp'), may hold values from -0.21875 to 0.21875
- decoder_output: bfloat16 [768, 768], P('mp'), may hold values from -0.75 to 0.75
- decoder_bias: float32 [32, 12], P(None, 'mp'), may hold values from -4 to 4
- cross_gain: float32 [768], replicated, may hold values from 0.5 to 1.5
- cross_query: bfloat16 [768, 768], P(None, 'mp'), may hold values from -0.21875 to 0.21875
- cross_key: bfloat16 [768, 768], P(None, 'mp'), may hold values from -0.21875 to 0.21875
- cross_value: bfloat16 [768, 768], P(None, 'mp'), may hold values from -0.21875 to 0.21875
- cross_output: bfloat16 [768, 768], P('mp'), may hold values from -0.75 to 0.75
- decoder_ffn_gain: float32 [768], replicated, may hold values from 0.5 to 1.5
- decoder_ffn_in: bfloat16 [768, 3072], P(None, 'mp'), may hold values from -0.21875 to 0.21875
- decoder_ffn_out: bfloat16 [3072, 768], P('mp'), may hold values from -0.109375 to 0.109375
- encoder_cotangent: bfloat16 [8, 1024, 768], P('dp'), may hold values from -6 to 6
- decoder_cotangent: bfloat16 [8, 1024, 768], P('dp'), may hold values from -6 to 6
Outputs:
- encoder_result: bfloat16 [8, 1024, 768], P('dp')
- decoder_result: bfloat16 [8, 1024, 768], P('dp')
- encoder_input_grad: float32 [8, 1024, 768], P('dp')
- decoder_input_grad: float32 [8, 1024, 768], P('dp')
- encoder_attn_gain_grad: float32 [768], replicated
- encoder_query_grad: float32 [768, 768], P(None, 'mp')
- encoder_key_grad: float32 [768, 768], P(None, 'mp')
- encoder_value_grad: float32 [768, 768], P(None, 'mp')
- encoder_output_grad: float32 [768, 768], P('mp')
- encoder_bias_grad: float32 [32, 12], P(None, 'mp')
- encoder_ffn_gain_grad: float32 [768], replicated
- encoder_ffn_in_grad: float32 [768, 3072], P(None, 'mp')
- encoder_ffn_out_grad: float32 [3072, 768], P('mp')
- decoder_attn_gain_grad: float32 [768], replicated
- decoder_query_grad: float32 [768, 768], P(None, 'mp')
- decoder_key_grad: float32 [768, 768], P(None, 'mp')
- decoder_value_grad: float32 [768, 768], P(None, 'mp')
- decoder_output_grad: float32 [768, 768], P('mp')
- decoder_bias_grad: float32 [32, 12], P(None, 'mp')
- cross_gain_grad: float32 [768], replicated
- cross_query_grad: float32 [768, 768], P(None, 'mp')
- cross_key_grad: float32 [768, 768], P(None, 'mp')
- cross_value_grad: float32 [768, 768], P(None, 'mp')
- cross_output_grad: float32 [768, 768], P('mp')
- decoder_ffn_gain_grad: float32 [768], replicated
- decoder_ffn_in_grad: float32 [768, 3072], P(None, 'mp')
- decoder_ffn_out_grad: float32 [3072, 768], P('mp')
Inputs may be any that keep to these rules, and one draw needn't show every extreme that they name: `encoder_lengths`: each sequence's 8 source document lengths sum to 1024, and one of them is exactly 384. `decoder_lengths`: each sequence's 8 target document lengths sum to 1024, and one of them is exactly 384.
All inputs are finite; a program needn't handle non-finite values.
Results may differ from a plain program's by a relative error of at most 0.029.
Values sent between devices are 32-bit elements; how exact they have to be, the bound alone decides.
A program may use at most 320 MiB of HBM per device.

v0:
```python
import jax
import jax.numpy as jnp
from jax import lax
from jax.sharding import PartitionSpec as P

DK = 64


EPS = 1e-06
NEG = -1e30
HIGHEST = lax.Precision.HIGHEST


def rms_norm(stream, gain):
    return stream * lax.rsqrt(jnp.mean(stream * stream, axis=-1, keepdims=True) + EPS) * gain


def gelu_tanh(value):
    return jax.nn.gelu(value, approximate=True)


def doc_ids(lengths, seq_len):
    ends = jnp.cumsum(lengths, axis=-1)
    places = lax.broadcasted_iota(
        jnp.int32, lengths.shape[:-1] + (seq_len, lengths.shape[-1]), lengths.ndim - 1
    )
    return jnp.sum((places >= ends[..., None, :]).astype(jnp.int32), axis=-1)


def distance_table(buckets, table):
    onehot = (buckets[:, None] == jnp.arange(table.shape[0], dtype=jnp.int32)[None, :]).astype(
        jnp.float32
    )
    return jnp.dot(onehot, table, precision=HIGHEST)


def table_grad(buckets, table, grad_dist):
    _, pullback = jax.vjp(lambda values: distance_table(buckets, values), table)
    return pullback(grad_dist)[0]


def signed_dist(dist, keys, causal):
    if causal:
        before = jnp.broadcast_to(dist[:1], (keys - 1, dist.shape[1]))
        return jnp.concatenate([before, dist], axis=0)
    return dist


def bias_rows(dist, start, count, keys, causal):
    whole = signed_dist(dist, keys, causal)
    blank = jnp.zeros((1, whole.shape[1]), whole.dtype)
    padded = jnp.concatenate([blank, whole, blank], axis=0)
    length = padded.shape[0]
    reverse = jnp.transpose(padded[::-1], (1, 0))
    tiled = jnp.tile(reverse, (1, count))[:, : count * (length - 1)]
    skewed = tiled.reshape(reverse.shape[0], count, length - 1)
    offset = keys - start
    return skewed[:, :, offset : offset + keys]


def project(left, right):
    return jnp.dot(left, right, preferred_element_type=jnp.float32)


def project_back(left, right):
    return jnp.einsum("rk,dk->rd", left, right, preferred_element_type=jnp.float32)


def project_weight(left, right):
    return jnp.einsum("ra,rb->ab", left, right, preferred_element_type=jnp.float32)


def reduce_branch(values, weight):
    count = values.shape[0] // lax.axis_size("mp")

    def term(start, rows):
        return project(values, weight)

    share = lax.psum_scatter(
        term(jnp.int32(0), lax.axis_size("mp") * count), "mp", scatter_dimension=0, tiled=True
    )
    return lax.all_gather(share, "mp", axis=0, tiled=True)


def reduce_grad(term, total):
    share = lax.psum_scatter(
        term(jnp.int32(0), lax.axis_size("mp") * (total // lax.axis_size("mp"))),
        "mp",
        scatter_dimension=0,
        tiled=True,
    )
    return lax.all_gather(share, "mp", axis=0, tiled=True)


def norm_grad(stream, gain, grad_normed):
    _, pullback = jax.vjp(rms_norm, stream, gain)
    return pullback(grad_normed)


def block_scores(query_block, key_rows, dist, start, query_docs, key_docs, causal):
    count = query_block.shape[0]
    keys = key_rows.shape[0]
    scores = jnp.einsum(
        "qhd,khd->hqk", query_block, key_rows, preferred_element_type=jnp.float32
    ) * DK ** (-0.5)
    if dist is not None:
        scores = scores + bias_rows(dist, start, count, keys, causal)
    allowed = query_docs[start : start + count, None] == key_docs[None, :]
    if causal:
        rows = start + lax.broadcasted_iota(jnp.int32, (count, keys), 0)
        cols = lax.broadcasted_iota(jnp.int32, (count, keys), 1)
        allowed = allowed & (cols <= rows)
    return jnp.where(allowed[None], scores, NEG)


def attention_forward(queries, key_rows, value_rows, dist, query_docs, key_docs, causal):
    seq = queries.shape[0]
    span = min(512, seq)
    outputs = []
    logsums = []
    for start in range(0, seq, span):
        scores = block_scores(
            queries[start : start + span], key_rows, dist, start, query_docs, key_docs, causal
        )
        top = jnp.max(scores, axis=-1, keepdims=True)
        total = jnp.sum(jnp.exp(scores - top), axis=-1, keepdims=True)
        logsum = top + jnp.log(total)
        attn_probs = jnp.exp(scores - logsum).astype(jnp.bfloat16)
        outputs.append(
            jnp.einsum("hqk,khd->qhd", attn_probs, value_rows, preferred_element_type=jnp.float32)
        )
        logsums.append(logsum)
    attended = jnp.concatenate(outputs, axis=0).reshape(seq, -1).astype(jnp.bfloat16)
    return (attended, jnp.concatenate(logsums, axis=1))


def attention_backward(
    queries, key_rows, value_rows, dist, query_docs, key_docs, causal, logsum, grad_attended
):
    seq = queries.shape[0]
    keys = key_rows.shape[0]
    span = min(512, seq)
    scale = DK ** (-0.5)
    grad_keys = jnp.zeros(key_rows.shape, jnp.float32)
    grad_values = jnp.zeros(value_rows.shape, jnp.float32)
    grad_dist = None if dist is None else jnp.zeros(dist.shape, jnp.float32)
    query_parts = []
    for start in range(0, seq, span):
        query_block = queries[start : start + span]
        out_block = grad_attended[start : start + span]
        scores = block_scores(query_block, key_rows, dist, start, query_docs, key_docs, causal)
        attn_probs = jnp.exp(scores - logsum[:, start : start + span])
        grad_probs = jnp.einsum(
            "qhd,khd->hqk", out_block, value_rows, preferred_element_type=jnp.float32
        )
        inner = jnp.sum(attn_probs * grad_probs, axis=-1, keepdims=True)
        grad_scores = (attn_probs * (grad_probs - inner)).astype(jnp.bfloat16)
        query_parts.append(
            jnp.einsum("hqk,khd->qhd", grad_scores, key_rows, preferred_element_type=jnp.float32)
            * scale
        )
        grad_keys = (
            grad_keys
            + jnp.einsum(
                "hqk,qhd->khd", grad_scores, query_block, preferred_element_type=jnp.float32
            )
            * scale
        )
        grad_values = grad_values + jnp.einsum(
            "hqk,qhd->khd",
            attn_probs.astype(jnp.bfloat16),
            out_block,
            preferred_element_type=jnp.float32,
        )
        if dist is not None:
            _, pullback = jax.vjp(lambda table: bias_rows(table, start, span, keys, causal), dist)
            grad_dist = grad_dist + pullback(grad_scores.astype(jnp.float32))[0]
    grad_queries = jnp.concatenate(query_parts, axis=0).astype(jnp.bfloat16)
    return (
        grad_queries,
        grad_keys.astype(jnp.bfloat16),
        grad_values.astype(jnp.bfloat16),
        grad_dist,
    )


def attention_inner(normed, memory, w_query, w_key, w_value, dist, query_docs, key_docs, causal):
    batch, seq = query_docs.shape
    keys = key_docs.shape[1]
    heads = w_query.shape[1] // DK
    queries = project(normed, w_query).astype(jnp.bfloat16).reshape(batch, seq, heads, DK)
    key_rows = project(memory, w_key).astype(jnp.bfloat16).reshape(batch, keys, heads, DK)
    value_rows = project(memory, w_value).astype(jnp.bfloat16).reshape(batch, keys, heads, DK)
    result = attention_forward(
        queries[0], key_rows[0], value_rows[0], dist, query_docs[0], key_docs[0], causal
    )
    attended = result[0]
    logsums = [result[1]]
    return (queries, key_rows, value_rows, attended, logsums)


def attention_grads(grad_stream, inner, normed, memory, w_out, dist, query_docs, key_docs, causal):
    queries, key_rows, value_rows, attended, logsums = inner
    batch, seq, heads, _ = queries.shape
    grad_branch = grad_stream.astype(jnp.bfloat16)
    grad_w_out = project_weight(attended, grad_branch)
    grad_attended = (
        project_back(grad_branch, w_out).astype(jnp.bfloat16).reshape(batch, seq, heads, DK)
    )
    grad_dist = None if dist is None else jnp.zeros(dist.shape, jnp.float32)
    result = attention_backward(
        queries[0],
        key_rows[0],
        value_rows[0],
        dist,
        query_docs[0],
        key_docs[0],
        causal,
        logsums[0],
        grad_attended[0],
    )
    query_list = result[0].reshape(seq, heads * DK)
    key_list = result[1].reshape(-1, heads * DK)
    value_list = result[2].reshape(-1, heads * DK)
    if dist is not None:
        grad_dist = result[3]
    grad_w_query = project_weight(normed, query_list)
    grad_w_key = project_weight(memory, key_list)
    grad_w_value = project_weight(memory, value_list)
    return (
        query_list,
        key_list,
        value_list,
        grad_w_query,
        grad_w_key,
        grad_w_value,
        grad_w_out,
        grad_dist,
    )


def self_input_grad(grad_queries, grad_keys, grad_values, w_query, w_key, w_value):

    def term(start, rows):
        return (
            project_back(grad_queries, w_query)
            + project_back(grad_keys, w_key)
            + project_back(grad_values, w_value)
        )

    return reduce_grad(term, grad_queries.shape[0])


def ffn_grads(grad_stream, normed_ffn, hidden, active, w_in, w_out):
    grad_branch = grad_stream.astype(jnp.bfloat16)
    grad_w_out = project_weight(active, grad_branch)
    grad_active = project_back(grad_branch, w_out)
    _, pullback = jax.vjp(gelu_tanh, hidden)
    grad_hidden = pullback(grad_active)[0].astype(jnp.bfloat16)
    grad_w_in = project_weight(normed_ffn, grad_hidden)

    def term(start, rows):
        return project_back(grad_hidden, w_in)

    grad_normed = reduce_grad(term, grad_hidden.shape[0])
    return (grad_normed, grad_w_in, grad_w_out)


def body(
    encoder_input,
    decoder_input,
    encoder_lengths,
    decoder_lengths,
    encoder_buckets,
    decoder_buckets,
    encoder_attn_gain,
    encoder_query,
    encoder_key,
    encoder_value,
    encoder_output,
    encoder_bias,
    encoder_ffn_gain,
    encoder_ffn_in,
    encoder_ffn_out,
    decoder_attn_gain,
    decoder_query,
    decoder_key,
    decoder_value,
    decoder_output,
    decoder_bias,
    cross_gain,
    cross_query,
    cross_key,
    cross_value,
    cross_output,
    decoder_ffn_gain,
    decoder_ffn_in,
    decoder_ffn_out,
    encoder_cotangent,
    decoder_cotangent,
):
    batch, seq, width = encoder_input.shape
    flat = batch * seq
    enc_docs = doc_ids(encoder_lengths, seq)
    dec_docs = doc_ids(decoder_lengths, seq)
    enc_dist = distance_table(encoder_buckets, encoder_bias)
    dec_dist = distance_table(decoder_buckets, decoder_bias)
    enc_start = encoder_input.astype(jnp.float32).reshape(flat, width)
    dec_start = decoder_input.astype(jnp.float32).reshape(flat, width)
    normed_attn = rms_norm(enc_start, encoder_attn_gain).astype(jnp.bfloat16)
    inner = attention_inner(
        normed_attn,
        normed_attn,
        encoder_query,
        encoder_key,
        encoder_value,
        enc_dist,
        enc_docs,
        enc_docs,
        False,
    )
    middle = enc_start + reduce_branch(inner[3], encoder_output)
    normed_ffn = rms_norm(middle, encoder_ffn_gain).astype(jnp.bfloat16)
    hidden = project(normed_ffn, encoder_ffn_in)
    active = gelu_tanh(hidden).astype(jnp.bfloat16)
    enc_saved = (normed_attn, inner, middle, normed_ffn, hidden, active)
    enc_final = enc_saved[2] + reduce_branch(enc_saved[5], encoder_ffn_out)
    memory = enc_final.astype(jnp.bfloat16)
    normed_self = rms_norm(dec_start, decoder_attn_gain).astype(jnp.bfloat16)
    inner_self = attention_inner(
        normed_self,
        normed_self,
        decoder_query,
        decoder_key,
        decoder_value,
        dec_dist,
        dec_docs,
        dec_docs,
        True,
    )
    middle_one = dec_start + reduce_branch(inner_self[3], decoder_output)
    normed_cross = rms_norm(middle_one, cross_gain).astype(jnp.bfloat16)
    inner_cross = attention_inner(
        normed_cross, memory, cross_query, cross_key, cross_value, None, dec_docs, enc_docs, False
    )
    middle_two = middle_one + reduce_branch(inner_cross[3], cross_output)
    normed_ffn = rms_norm(middle_two, decoder_ffn_gain).astype(jnp.bfloat16)
    hidden = project(normed_ffn, decoder_ffn_in)
    active = gelu_tanh(hidden).astype(jnp.bfloat16)
    dec_saved = (
        normed_self,
        inner_self,
        middle_one,
        normed_cross,
        inner_cross,
        middle_two,
        normed_ffn,
        hidden,
        active,
    )
    dec_final = dec_saved[5] + reduce_branch(dec_saved[8], decoder_ffn_out)
    (
        normed_self,
        inner_self,
        middle_one,
        normed_cross,
        inner_cross,
        middle_two,
        normed_ffn,
        hidden,
        active,
    ) = dec_saved
    grad_stream = decoder_cotangent.astype(jnp.float32).reshape(flat, width)
    grad_normed, dec_ffn_in_grad, dec_ffn_out_grad = ffn_grads(
        grad_stream, normed_ffn, hidden, active, decoder_ffn_in, decoder_ffn_out
    )
    grad_middle, dec_ffn_gain_grad = norm_grad(middle_two, decoder_ffn_gain, grad_normed)
    grad_stream = grad_stream + grad_middle
    cross_parts = attention_grads(
        grad_stream,
        inner_cross,
        normed_cross,
        memory,
        cross_output,
        None,
        dec_docs,
        enc_docs,
        False,
    )
    grad_cq, grad_ck, grad_cv = (cross_parts[0], cross_parts[1], cross_parts[2])

    def cross_term(start, rows):
        return jnp.concatenate(
            [
                project_back(grad_cq, cross_query),
                project_back(grad_ck, cross_key) + project_back(grad_cv, cross_value),
            ],
            axis=1,
        )

    joined = reduce_grad(cross_term, flat)
    grad_middle, cross_gain_grad = norm_grad(middle_one, cross_gain, joined[:, :width])
    grad_memory = joined[:, width:]
    grad_stream = grad_stream + grad_middle
    self_parts = attention_grads(
        grad_stream,
        inner_self,
        normed_self,
        normed_self,
        decoder_output,
        dec_dist,
        dec_docs,
        dec_docs,
        True,
    )
    grad_normed = self_input_grad(
        self_parts[0], self_parts[1], self_parts[2], decoder_query, decoder_key, decoder_value
    )
    grad_middle, dec_attn_gain_grad = norm_grad(dec_start, decoder_attn_gain, grad_normed)
    decoder_input_grad = grad_stream + grad_middle
    dec_bias_grad = table_grad(decoder_buckets, decoder_bias, self_parts[7])
    dec_grads = (
        dec_attn_gain_grad,
        self_parts[3],
        self_parts[4],
        self_parts[5],
        self_parts[6],
        dec_bias_grad,
        cross_gain_grad,
        cross_parts[3],
        cross_parts[4],
        cross_parts[5],
        cross_parts[6],
        dec_ffn_gain_grad,
        dec_ffn_in_grad,
        dec_ffn_out_grad,
    )
    normed_attn, inner_enc, middle_enc, normed_ffn, hidden, active = enc_saved
    grad_stream = encoder_cotangent.astype(jnp.float32).reshape(flat, width) + grad_memory
    grad_normed, enc_ffn_in_grad, enc_ffn_out_grad = ffn_grads(
        grad_stream, normed_ffn, hidden, active, encoder_ffn_in, encoder_ffn_out
    )
    grad_middle, enc_ffn_gain_grad = norm_grad(middle_enc, encoder_ffn_gain, grad_normed)
    grad_stream = grad_stream + grad_middle
    enc_parts = attention_grads(
        grad_stream,
        inner_enc,
        normed_attn,
        normed_attn,
        encoder_output,
        enc_dist,
        enc_docs,
        enc_docs,
        False,
    )
    grad_normed = self_input_grad(
        enc_parts[0], enc_parts[1], enc_parts[2], encoder_query, encoder_key, encoder_value
    )
    grad_middle, enc_attn_gain_grad = norm_grad(enc_start, encoder_attn_gain, grad_normed)
    encoder_input_grad = grad_stream + grad_middle
    enc_bias_grad = table_grad(encoder_buckets, encoder_bias, enc_parts[7])
    enc_grads = (
        enc_attn_gain_grad,
        enc_parts[3],
        enc_parts[4],
        enc_parts[5],
        enc_parts[6],
        enc_bias_grad,
        enc_ffn_gain_grad,
        enc_ffn_in_grad,
        enc_ffn_out_grad,
    )
    summed = lax.psum(
        (
            enc_grads[0],
            enc_grads[1],
            enc_grads[2],
            enc_grads[3],
            enc_grads[4],
            enc_grads[5],
            enc_grads[6],
            enc_grads[7],
            enc_grads[8],
            dec_grads[0],
            dec_grads[1],
            dec_grads[2],
            dec_grads[3],
            dec_grads[4],
            dec_grads[5],
            dec_grads[6],
            dec_grads[7],
            dec_grads[8],
            dec_grads[9],
            dec_grads[10],
            dec_grads[11],
            dec_grads[12],
            dec_grads[13],
        ),
        "dp",
    )
    encoder_result = enc_final.astype(jnp.bfloat16).reshape(batch, seq, width)
    decoder_result = dec_final.astype(jnp.bfloat16).reshape(batch, seq, width)
    return (
        encoder_result,
        decoder_result,
        encoder_input_grad.reshape(batch, seq, width),
        decoder_input_grad.reshape(batch, seq, width),
        summed[0],
        summed[1],
        summed[2],
        summed[3],
        summed[4],
        summed[5],
        summed[6],
        summed[7],
        summed[8],
        summed[9],
        summed[10],
        summed[11],
        summed[12],
        summed[13],
        summed[14],
        summed[15],
        summed[16],
        summed[17],
        summed[18],
        summed[19],
        summed[20],
        summed[21],
        summed[22],
    )


def solution(mesh):
    return jax.shard_map(
        body,
        mesh=mesh,
        in_specs=(
            P("dp", None, None),
            P("dp", None, None),
            P("dp", None),
            P("dp", None),
            P(),
            P(),
            P(),
            P(None, "mp"),
            P(None, "mp"),
            P(None, "mp"),
            P("mp", None),
            P(None, "mp"),
            P(),
            P(None, "mp"),
            P("mp", None),
            P(),
            P(None, "mp"),
            P(None, "mp"),
            P(None, "mp"),
            P("mp", None),
            P(None, "mp"),
            P(),
            P(None, "mp"),
            P(None, "mp"),
            P(None, "mp"),
            P("mp", None),
            P(),
            P(None, "mp"),
            P("mp", None),
            P("dp", None, None),
            P("dp", None, None),
        ),
        out_specs=(
            P("dp", None, None),
            P("dp", None, None),
            P("dp", None, None),
            P("dp", None, None),
            P(),
            P(None, "mp"),
            P(None, "mp"),
            P(None, "mp"),
            P("mp", None),
            P(None, "mp"),
            P(),
            P(None, "mp"),
            P("mp", None),
            P(),
            P(None, "mp"),
            P(None, "mp"),
            P(None, "mp"),
            P("mp", None),
            P(None, "mp"),
            P(),
            P(None, "mp"),
            P(None, "mp"),
            P(None, "mp"),
            P("mp", None),
            P(),
            P(None, "mp"),
            P("mp", None),
        ),
        check_vma=False,
    )
```

profile of v0, /device:TPU:0, one launch (start us, length us, event | category | flops | bytes accessed | tf_op | source)
XLA Modules:
  0.0 1597.4 jit_solution(11811310894968948851)
XLA Ops:
  27.0 21.5 %reshape.743 = f32[3147264]{0:T(1024)} reshape(f32[3,512,2049]{2,1,0:T(8,128)} %tile.8) | data formatting | bytes 25178112
  48.5 18.9 %tile.9 = f32[3,1049088]{1,0:T(4,128)} reshape(f32[3147264]{0:T(1024)} %reshape.743) | data formatting | bytes 25178112 | tf_op jit(solution)/shard_map/tile | solution.py:55
  67.4 14.6 slice.193
  82.1 17.6 %copy.86 = f32[1,3,512,2048]{3,2,1,0:T(8,128)} copy(f32[1,3,512,2048]{3,1,2,0:T(4,128)} %bitcast.348) | data formatting | bytes 25165824
  122.0 38.0 %reduce-scatter.11.cloned.1.call-done = f32[256,768]{1,0:T(8,128)} async-done(((f32[1024,768]{1,0:T(8,128)}), f32[256,768]{1,0:T(8,128)}) %reduce-scatter.11.cloned.1.call-update) | async-done | bytes 786448 | tf_op jit(solution)/shard_map/reduce_scatter | solution.py:79
  160.1 5.7 tile.10
  165.7 21.7 %reshape.745 = f32[3147264]{0:T(1024)} reshape(f32[3,512,2049]{2,1,0:T(8,128)} %tile.10) | data formatting | bytes 25178112
  187.4 18.9 %tile.11 = f32[3,1049088]{1,0:T(4,128)} reshape(f32[3147264]{0:T(1024)} %reshape.745) | data formatting | bytes 25178112 | tf_op jit(solution)/shard_map/tile | solution.py:55
  206.3 14.6 slice.201
  221.0 17.6 %copy.85 = f32[1,3,512,2048]{3,2,1,0:T(8,128)} copy(f32[1,3,512,2048]{3,1,2,0:T(4,128)} %bitcast.349) | data formatting | bytes 25165824
  268.6 28.0 %reduce-scatter.15.cloned.1.call-done = f32[256,768]{1,0:T(8,128)} async-done(((f32[1024,768]{1,0:T(8,128)}), f32[256,768]{1,0:T(8,128)}) %reduce-scatter.15.cloned.1.call-update) | async-done | bytes 786448 | tf_op jit(solution)/shard_map/reduce_scatter | solution.py:79
  296.7 40.9 %reduce-scatter.13.cloned.1.call-done = f32[256,768]{1,0:T(8,128)} async-done(((f32[1024,768]{1,0:T(8,128)}), f32[256,768]{1,0:T(8,128)}) %reduce-scatter.13.cloned.1.call-update) | async-done | bytes 786448 | tf_op jit(solution)/shard_map/reduce_scatter | solution.py:79
  338.1 29.6 %all-gather.15.cloned.1.call-done = f32[1024,768]{1,0:T(8,128)} async-done(((f32[256,768]{1,0:T(8,128)}), f32[1024,768]{1,0:T(8,128)}) %all-gather.15.cloned.1.call-update) | async-done | bytes 3145744 | tf_op jit(solution)/shard_map/all_gather | solution.py:82
  372.5 25.1 %all-gather.13.cloned.1.call-done = f32[1024,768]{1,0:T(8,128)} async-done(((f32[256,768]{1,0:T(8,128)}), f32[1024,768]{1,0:T(8,128)}) %all-gather.13.cloned.1.call-update) | async-done | bytes 3145744 | tf_op jit(solution)/shard_map/all_gather | solution.py:82
  414.9 38.0 %reduce-scatter.17.cloned.1.call-done = f32[256,768]{1,0:T(8,128)} async-done(((f32[1024,768]{1,0:T(8,128)}), f32[256,768]{1,0:T(8,128)}) %reduce-scatter.17.cloned.1.call-update) | async-done | bytes 786448 | tf_op jit(solution)/shard_map/reduce_scatter | solution.py:79
  453.2 29.9 %all-gather.17.cloned.1.call-done = f32[1024,768]{1,0:T(8,128)} async-done(((f32[256,768]{1,0:T(8,128)}), f32[1024,768]{1,0:T(8,128)}) %all-gather.17.cloned.1.call-update) | async-done | bytes 3145744 | tf_op jit(solution)/shard_map/all_gather | solution.py:82
  503.9 31.3 %reduce-scatter.21.cloned.1.call-done = f32[256,768]{1,0:T(8,128)} async-done(((f32[1024,768]{1,0:T(8,128)}), f32[256,768]{1,0:T(8,128)}) %reduce-scatter.21.cloned.1.call-update) | async-done | bytes 786448 | tf_op jit(solution)/shard_map/reduce_scatter | solution.py:86
  535.3 40.5 %reduce-scatter.19.cloned.1.call-done = f32[256,768]{1,0:T(8,128)} async-done(((f32[1024,768]{1,0:T(8,128)}), f32[256,768]{1,0:T(8,128)}) %reduce-scatter.19.cloned.1.call-update) | async-done | bytes 786448 | tf_op jit(solution)/shard_map/reduce_scatter | solution.py:79
  576.0 29.9 %all-gather.21.cloned.1.call-done = f32[1024,768]{1,0:T(8,128)} async-done(((f32[256,768]{1,0:T(8,128)}), f32[1024,768]{1,0:T(8,128)}) %all-gather.21.cloned.1.call-update) | async-done | bytes 3145744 | tf_op jit(solution)/shard_map/all_gather | solution.py:92
  610.1 25.8 %all-gather.19.cloned.1.call-done = f32[1024,768]{1,0:T(8,128)} async-done(((f32[256,768]{1,0:T(8,128)}), f32[1024,768]{1,0:T(8,128)}) %all-gather.19.cloned.1.call-update) | async-done | bytes 3145744 | tf_op jit(solution)/shard_map/all_gather | solution.py:82
  635.8 5.8 fusion.52
  648.9 6.2 multiply_reduce_fusion.5
  659.5 7.9 multiply_convert_fusion.4
  681.4 58.5 %reduce-scatter.23.cloned.1.call-done = f32[256,1536]{1,0:T(8,128)} async-done(((f32[1024,1536]{1,0:T(8,128)}), f32[256,1536]{1,0:T(8,128)}) %reduce-scatter.23.cloned.1.call-update) | async-done | bytes 1572880 | tf_op jit(solution)/shard_map/reduce_scatter | solution.py:86
  739.9 47.8 %all-gather.23.cloned.1.call-done = f32[1024,1536]{1,0:T(8,128)} async-done(((f32[256,1536]{1,0:T(8,128)}), f32[1024,1536]{1,0:T(8,128)}) %all-gather.23.cloned.1.call-update) | async-done | bytes 6291472 | tf_op jit(solution)/shard_map/all_gather | solution.py:92
  787.8 6.4 fusion.44
  799.7 38.0 %reduce-scatter.25.cloned.1.call-done = f32[256,768]{1,0:T(8,128)} async-done(((f32[1024,768]{1,0:T(8,128)}), f32[256,768]{1,0:T(8,128)}) %reduce-scatter.25.cloned.1.call-update) | async-done | bytes 786448 | tf_op jit(solution)/shard_map/reduce_scatter | solution.py:86
  861.2 6.5 all-gather.25.cloned.1.call-done
  872.5 7.0 fusion.56
  914.5 12.1 copy.79
  947.1 11.2 pad_convert_fusion.3
  961.6 11.6 copy.80
  973.3 10.4 pad_convert_fusion.2
  986.9 11.5 copy.81
  998.5 10.4 pad_convert_fusion.1
  1012.3 12.0 copy.82
  1036.1 10.4 pad_convert_fusion
  1046.6 36.8 %reshape.753 = f32[3147264]{0:T(1024)} reshape(f32[3,1049088]{1,0:T(4,128)} %pad_convert_fusion.1) | data formatting | bytes 25178112
  1083.3 20.6 %reshape.734 = f32[3,512,2049]{2,1,0:T(8,128)} reshape(f32[3147264]{0:T(1024)} %reshape.753) | data formatting | bytes 25178112 | tf_op jit(solution)/shard_map/transpose(jvp())/reshape | solution.py:55
  1109.6 36.8 %reshape.751 = f32[3147264]{0:T(1024)} reshape(f32[3,1049088]{1,0:T(4,128)} %pad_convert_fusion) | data formatting | bytes 25178112
  1146.4 20.6 %reshape.736 = f32[3,512,2049]{2,1,0:T(8,128)} reshape(f32[3147264]{0:T(1024)} %reshape.751) | data formatting | bytes 25178112 | tf_op jit(solution)/shard_map/transpose(jvp())/reshape | solution.py:55
  1167.0 5.8 reduce_sum.412
  1173.0 36.2 %reshape.747 = f32[3147264]{0:T(1024)} reshape(f32[3,1049088]{1,0:T(4,128)} %pad_convert_fusion.3) | data formatting | bytes 25178112
  1209.2 20.6 %reshape.730 = f32[3,512,2049]{2,1,0:T(8,128)} reshape(f32[3147264]{0:T(1024)} %reshape.747) | data formatting | bytes 25178112 | tf_op jit(solution)/shard_map/transpose(jvp())/reshape | solution.py:55
  1237.2 36.6 %reshape.749 = f32[3147264]{0:T(1024)} reshape(f32[3,1049088]{1,0:T(4,128)} %pad_convert_fusion.2) | data formatting | bytes 25178112
  1273.7 20.5 %reshape.732 = f32[3,512,2049]{2,1,0:T(8,128)} reshape(f32[3147264]{0:T(1024)} %reshape.749) | data formatting | bytes 25178112 | tf_op jit(solution)/shard_map/transpose(jvp())/reshape | solution.py:55
  1312.7 37.7 %all-reduce.10 = (f32[768]{0:T(1024)}, f32[32,3]{0,1:T(4,128)}, f32[768]{0:T(1024)}, f32[768]{0:T(1024)}, f32[32,3]{0,1:T(4,128)}, /*index=5*/f32[768]{0:T(1024)}, f32[768]{0:T(1024)}) all-reduce(f32[768]{0:T(1024)S(1)} %get-tuple-element.35, f32[32,3]{0,1:T(4,128)S(1)} %fusion.92, ...), channel_id=1, replica_groups=mesh['dp'=8,'mp'=4] {'dp'}, use_global_device_ids=true, to_apply=%region_43.44 | all-reduce | flops 4032 | bytes 32256 | tf_op jit(solution)/shard_map/psum | solution.py:473
  1359.4 212.0 %all-reduce.14.cloned.1.call-done = (f32[768,192]{0,1:T(8,128)}, f32[768,192]{0,1:T(8,128)}, f32[768,192]{0,1:T(8,128)}, f32[192,768]{1,0:T(8,128)}, f32[768,768...) async-done(((f32[768,192]{0,1:T(8,128)}, ...) | async-done | bytes 16515088 | tf_op jit(solution)/shard_map/psum | solution.py:473
  (613 shorter events, 314.6 us)
Async XLA Ops:
  7.2 479.2 %copy-start = (bf16[768,768]{1,0:T(8,128)(2,1)S(1)}, bf16[768,768]{1,0:T(8,128)(2,1)}, u32[]{:S(2)}) copy-start(bf16[768,768]{1,0:T(8,128)(2,1)} %param.58) | copy-start | bytes 3538948
  7.2 152.7 %reduce-scatter.11.cloned.1.call-start = ((), (), s32[]{:S(2)}) async-start(), calls=%async_computation.10 | async-start | bytes 3932160 | tf_op jit(solution)/shard_map/reduce_scatter | solution.py:79
  17.3 85.6 %copy-start.60 = (bf16[512,192]{0,1:T(8,128)(2,1)}, bf16[512,192]{0,1:T(8,128)(2,1)S(1)}, u32[]{:S(2)}) copy-start(bf16[512,192]{0,1:T(8,128)(2,1)S(1)} %get-tuple-element.81) | copy-start | bytes 589828
  119.2 139.5 %all-gather.11.cloned.1.call-start = ((), (), s32[]{:S(2)}) async-start(), calls=%async_computation.11 | async-start | bytes 3932160 | tf_op jit(solution)/shard_map/all_gather | solution.py:82
  121.9 43.9 %copy-start.132 = (f32[1024]{0:T(1024)}, f32[1024]{0:T(1024)S(1)}, u32[]{:S(2)}) copy-start(f32[1024]{0:T(1024)S(1)} %fusion.34) | copy-start | bytes 12292
  160.0 136.6 %reduce-scatter.15.cloned.1.call-start = ((), (), s32[]{:S(2)}) async-start(), calls=%async_computation.14 | async-start | bytes 3932160 | tf_op jit(solution)/shard_map/reduce_scatter | solution.py:79
  160.0 91.8 %copy-start.128 = (f32[1024]{0:T(1024)}, f32[1024]{0:T(1024)S(1)}, u32[]{:S(2)}) copy-start(f32[1024]{0:T(1024)S(1)} %fusion.141) | copy-start | bytes 12292
  221.0 17.6 %copy-start.134 = (f32[768]{0:T(1024)S(1)}, f32[768]{0:T(1024)}, u32[]{:S(2)}) copy-start(f32[768]{0:T(1024)} %param.46) | copy-start | bytes 9220
  258.6 79.0 %reduce-scatter.13.cloned.1.call-start = ((), (), s32[]{:S(2)}) async-start(), calls=%async_computation.12 | async-start | bytes 3932160 | tf_op jit(solution)/shard_map/reduce_scatter | solution.py:79
  268.6 99.1 %all-gather.15.cloned.1.call-start = ((), (), s32[]{:S(2)}) async-start(), calls=%async_computation.15 | async-start | bytes 3932160 | tf_op jit(solution)/shard_map/all_gather | solution.py:82
  296.6 101.1 %all-gather.13.cloned.1.call-start = ((), (), s32[]{:S(2)}) async-start(), calls=%async_computation.13 | async-start | bytes 3932160 | tf_op jit(solution)/shard_map/all_gather | solution.py:82
  337.6 34.1 %copy-start.125 = (f32[768]{0:T(1024)S(1)}, f32[768]{0:T(1024)}, u32[]{:S(2)}) copy-start(f32[768]{0:T(1024)} %param.52) | copy-start | bytes 9220
  337.6 115.4 %reduce-scatter.17.cloned.1.call-start = ((), (), s32[]{:S(2)}) async-start(), calls=%async_computation.16 | async-start | bytes 3932160 | tf_op jit(solution)/shard_map/reduce_scatter | solution.py:79
  372.5 32.9 %copy-start.70 = (bf16[512,192]{0,1:T(8,128)(2,1)}, bf16[512,192]{0,1:T(8,128)(2,1)S(1)}, u32[]{:S(2)}) copy-start(bf16[512,192]{0,1:T(8,128)(2,1)S(1)} %get-tuple-element.76) | copy-start | bytes 589828
  372.5 28.3 %copy-start.110 = (bf16[768,192]{0,1:T(8,128)(2,1)S(1)}, bf16[768,192]{0,1:T(8,128)(2,1)}, u32[]{:S(2)}) copy-start(bf16[768,192]{0,1:T(8,128)(2,1)} %param.54) | copy-start | bytes 884740
  372.5 29.0 %copy-start.112 = (bf16[768,192]{0,1:T(8,128)(2,1)S(1)}, bf16[768,192]{0,1:T(8,128)(2,1)}, u32[]{:S(2)}) copy-start(bf16[768,192]{0,1:T(8,128)(2,1)} %param.55) | copy-start | bytes 884740
  414.9 68.2 %all-gather.17.cloned.1.call-start = ((), (), s32[]{:S(2)}) async-start(), calls=%async_computation.17 | async-start | bytes 3932160 | tf_op jit(solution)/shard_map/all_gather | solution.py:82
  453.0 33.4 %copy-start.141 = (f32[768]{0:T(1024)S(1)}, f32[768]{0:T(1024)}, u32[]{:S(2)}) copy-start(f32[768]{0:T(1024)} %param.57) | copy-start | bytes 9220
  453.0 82.2 %reduce-scatter.21.cloned.1.call-start = ((), (), s32[]{:S(2)}) async-start(), calls=%async_computation.20 | async-start | bytes 3932160 | tf_op jit(solution)/shard_map/reduce_scatter | solution.py:86
  497.1 78.6 %reduce-scatter.19.cloned.1.call-start = ((), (), s32[]{:S(2)}) async-start(), calls=%async_computation.18 | async-start | bytes 3932160 | tf_op jit(solution)/shard_map/reduce_scatter | solution.py:79
  503.8 102.0 %all-gather.21.cloned.1.call-start = ((), (), s32[]{:S(2)}) async-start(), calls=%async_computation.21 | async-start | bytes 3932160 | tf_op jit(solution)/shard_map/all_gather | solution.py:92
  535.2 100.6 %all-gather.19.cloned.1.call-start = ((), (), s32[]{:S(2)}) async-start(), calls=%async_computation.19 | async-start | bytes 3932160 | tf_op jit(solution)/shard_map/all_gather | solution.py:82
  575.7 164.1 %reduce-scatter.23.cloned.1.call-start = ((), (), s32[]{:S(2)}) async-start(), calls=%async_computation.22 | async-start | bytes 7864320 | tf_op jit(solution)/shard_map/reduce_scatter | solution.py:86
  610.1 31.5 %copy-start.80 = (bf16[192,768]{1,0:T(8,128)(2,1)S(1)}, bf16[192,768]{1,0:T(8,128)(2,1)}, u32[]{:S(2)}) copy-start(bf16[192,768]{1,0:T(8,128)(2,1)} %param.56) | copy-start | bytes 884740
  642.3 12.8 copy-start.95
  643.3 11.8 slice-start.10
  681.3 106.5 %copy-start.146 = (bf16[768,768]{1,0:T(8,128)(2,1)S(1)}, bf16[768,768]{1,0:T(8,128)(2,1)}, u32[]{:S(2)}) copy-start(bf16[768,768]{1,0:T(8,128)(2,1)} %param.45) | copy-start | bytes 3538948
  681.3 106.4 %all-gather.23.cloned.1.call-start = ((), (), s32[]{:S(2)}) async-start(), calls=%async_computation.23 | async-start | bytes 7864320 | tf_op jit(solution)/shard_map/all_gather | solution.py:92
  739.9 97.9 %reduce-scatter.25.cloned.1.call-start = ((), (), s32[]{:S(2)}) async-start(), calls=%async_computation.24 | async-start | bytes 3932160 | tf_op jit(solution)/shard_map/reduce_scatter | solution.py:86
  799.7 68.1 %all-gather.25.cloned.1.call-start = ((), (), s32[]{:S(2)}) async-start(), calls=%async_computation.25 | async-start | bytes 3932160 | tf_op jit(solution)/shard_map/all_gather | solution.py:92
  837.8 135.4 %reduce-scatter.29.cloned.1.call-start = ((), (), s32[]{:S(2)}) async-start(), calls=%async_computation.28 | async-start | bytes 3932160 | tf_op jit(solution)/shard_map/reduce_scatter | solution.py:86
  838.3 14.2 slice-start.20
  898.6 99.8 %reduce-scatter.27.cloned.1.call-start = ((), (), s32[]{:S(2)}) async-start(), calls=%async_computation.26 | async-start | bytes 3932160 | tf_op jit(solution)/shard_map/reduce_scatter | solution.py:86
  914.4 12.1 copy-start.41
  947.0 359.0 %all-gather.29.cloned.1.call-start = ((), (), s32[]{:S(2)}) async-start(), calls=%async_computation.29 | async-start | bytes 3932160 | tf_op jit(solution)/shard_map/all_gather | solution.py:92
  947.1 11.2 copy-start.14
  973.2 336.0 %all-gather.27.cloned.1.call-start = ((), (), s32[]{:S(2)}) async-start(), calls=%async_computation.27 | async-start | bytes 3932160 | tf_op jit(solution)/shard_map/all_gather | solution.py:92
  998.5 572.9 %all-reduce.14.cloned.1.call-start = ((), (), s32[]{:S(2)}) async-start(), calls=%async_computation.30 | async-start | bytes 33030144 | tf_op jit(solution)/shard_map/psum | solution.py:473
  998.5 10.4 copy-start.12
  1012.3 12.0 copy-start.31
  1012.3 12.0 copy-start.88
  1012.3 12.0 copy-start.90
  1012.3 12.0 copy-start.129
  1012.3 12.0 copy-start.135
  1294.3 10.7 copy-start.150
  1294.3 11.1 copy-start.148
  1309.2 41.2 %copy-start.133 = (f32[1024]{0:T(1024)S(1)}, f32[1024]{0:T(1024)}, u32[]{:S(2)}) copy-start(f32[1024]{0:T(1024)} %copy-done.132) | copy-start | bytes 12292
  1309.2 41.2 %copy-start.131 = (f32[1024]{0:T(1024)S(1)}, f32[1024]{0:T(1024)}, u32[]{:S(2)}) copy-start(f32[1024]{0:T(1024)} %copy-done.130) | copy-start | bytes 12292
  (155 other events, 551.7 us)
Sparse Core Ops, SparseCore 0:
  119.3 40.6 reduce-scatter.10
  161.6 28.5 all-gather.10
  258.7 37.8 reduce-scatter.14
  299.6 37.9 reduce-scatter.12
  339.0 28.5 all-gather.14
  369.1 28.5 all-gather.12
  415.0 37.9 reduce-scatter.16
  454.5 28.5 all-gather.16
  497.2 37.9 reduce-scatter.20
  537.7 37.9 reduce-scatter.18
  577.3 28.5 all-gather.20
  607.3 28.5 all-gather.18
  681.5 58.3 reduce-scatter.22
  741.3 46.3 all-gather.22
  799.8 37.9 reduce-scatter.24
  839.2 28.5 all-gather.24
  898.8 37.9 reduce-scatter.28
  947.1 37.3 reduce-scatter.26
  986.1 28.5 all-gather.28
  1016.0 28.5 all-gather.26
  1053.3 518.0 all-reduce.13
where the time goes:
time: 1600 us
  waiting for transfers between devices  720 us (45%)
  local copies, waits for them, and re-layouts  501 us (31%)
  matrix products  171 us (11%)
  other arithmetic  149 us (9%)
  blocking collectives  37.7 us (2%)
  between operations  16.8 us (1%)
    unnamed x402, local copies, waits for them, and re-layouts  337 us
    psum x1, waiting for transfers between devices, body(): lax.psum((enc_grads[0], enc_grads[1], enc_grads[2], enc_grads[3], enc_gra...  212 us
    reduce_scatter x5, waiting for transfers between devices, reduce_branch(): lax.psum_scatter(term(jnp.int32(0), lax.axis_size('mp') * count), 'mp', s...  185 us
    reduce_scatter x5, waiting for transfers between devices, reduce_grad(): lax.psum_scatter(term(jnp.int32(0), lax.axis_size('mp') * (total // lax.a...  128 us
    all_gather x5, waiting for transfers between devices, reduce_branch(): return lax.all_gather(share, 'mp', axis=0, tiled=True)  110 us
    all_gather x5, waiting for transfers between devices, reduce_grad(): return lax.all_gather(share, 'mp', axis=0, tiled=True)  84.3 us
    reshape x4, local copies, waits for them, and re-layouts, bias_rows(): tiled = jnp.tile(reverse, (1, count))[:, :count * (length - 1)]  82.3 us
    another operation x4, local copies, waits for them, and re-layouts, bias_rows(): tiled = jnp.tile(reverse, (1, count))[:, :count * (length - 1)]  49.2 us
  transfers between devices with their start and end apart: 21, of which 16 were waited for; matrix products, arithmetic and copies ran while one was open for 35% of the time, Pallas kernels for 0%

commit v1 on v0

v1 whole, which is shorter than its diff:
```python
import functools

import jax
import jax.numpy as jnp
from jax import lax
from jax.experimental import pallas as pl
from jax.experimental.pallas import tpu as pltpu
from jax.sharding import PartitionSpec as P

DK = 64
EPS = 1e-06
NEG = -1e30
HIGHEST = lax.Precision.HIGHEST
TILE = 128
BQ = 256
KC = 128
SPEEDUP = 1 << 20
VMEM_BYTES = 60 * 1024 * 1024


def doc_ends(lens_ref):
    ends = []
    total = jnp.int32(0)
    for j in range(lens_ref.shape[1]):
        total = total + lens_ref[0, j]
        ends.append(total)
    return ends


def docs_at(places, ends):
    result = jnp.zeros(places.shape, jnp.int32)
    for end in ends:
        result = result + (places >= end).astype(jnp.int32)
    return result


def key_range(ql_ref, q_ends, kl_ref, block, causal):
    first = block * BQ
    last = first + BQ - 1
    low = jnp.int32(0)
    high = jnp.int32(0)
    for j, end in enumerate(q_ends):
        low = low + jnp.where(end <= first, kl_ref[0, j], 0)
        high = high + jnp.where(end - ql_ref[0, j] <= last, kl_ref[0, j], 0)
    if causal:
        high = jnp.minimum(high, first + BQ)
    return low // KC, (high + KC - 1) // KC


def bucket_hits(buckets_ref, count):
    ids = lax.broadcasted_iota(jnp.int32, (count, buckets_ref.shape[1]), 0)
    return ids == buckets_ref[...]


def make_tiles(buckets_ref, table_ref, tiles_ref):
    hits = bucket_hits(buckets_ref, table_ref.shape[0])
    width = buckets_ref.shape[1]
    for h in range(tiles_ref.shape[0]):
        row = jnp.sum(jnp.where(hits, table_ref[:, h : h + 1], 0.0), axis=0, keepdims=True)
        row = jnp.where(buckets_ref[...] < 0, NEG, row)
        for k in range(tiles_ref.shape[1] // TILE):
            start = width - 2 * TILE - k * TILE
            window = jnp.broadcast_to(row[:, start : start + 2 * TILE], (TILE, 2 * TILE))
            skewed = pltpu.roll(window, 0, 1, stride=1, stride_axis=0)
            tiles_ref[h, k * TILE : (k + 1) * TILE, :] = skewed[:, TILE:]


def sum_tiles(buckets_ref, grad_tiles_ref, grad_table_ref):
    count = grad_table_ref.shape[0]
    width = buckets_ref.shape[1]
    hits = bucket_hits(buckets_ref, count)
    blocks = grad_tiles_ref.shape[1] // TILE
    blank = jnp.zeros((8, TILE), jnp.float32)
    for h in range(grad_tiles_ref.shape[0]):
        halves = []
        for k in range(blocks):
            total = jnp.zeros((8, 2 * TILE), jnp.float32)
            for a in range(0, TILE, 8):
                piece = grad_tiles_ref[h, k * TILE + a : k * TILE + a + 8, :]
                wide = jnp.concatenate([blank, piece], axis=1)
                total = total + pltpu.roll(wide, (2 * TILE - a) % (2 * TILE), 1)
            halves.append(total)
        parts = []
        for m in range(width // TILE):
            upper = halves[blocks - 1 - m][:, :TILE] if m < blocks else None
            lower = halves[blocks - m][:, TILE:] if m >= 1 else None
            part = upper if lower is None else lower if upper is None else upper + lower
            parts.append(part)
        group = jnp.concatenate(parts, axis=1)
        row = group[0:1]
        for b in range(1, 8):
            row = row + pltpu.roll(group[b : b + 1], width - b, 1)
        grad_table_ref[:, h : h + 1] = jnp.sum(jnp.where(hits, row, 0.0), axis=1, keepdims=True)


def tile_rows(tiles_ref, h, block, chunk, keys):
    parts = []
    for t in range(BQ // TILE):
        start = keys - TILE - TILE * (block * (BQ // TILE) + t) + chunk * KC
        parts.append(tiles_ref[h, pl.ds(pl.multiple_of(start, TILE), KC), :])
    return jnp.concatenate(parts, axis=1)


def head_mask(h, width):
    lane = lax.broadcasted_iota(jnp.int32, (1, width), 1)
    return ((lane >= h * DK) & (lane < (h + 1) * DK)).astype(jnp.bfloat16)


def dot_last(left, right):
    return lax.dot_general(
        left, right, (((1,), (1,)), ((), ())), preferred_element_type=jnp.float32
    )


def dot(left, right):
    return jnp.dot(left, right, preferred_element_type=jnp.float32)


def flip(value):
    return jnp.transpose(value.astype(jnp.float32)).astype(value.dtype)


ROWS = 256


def ref_norm(stream, gain):
    scale = lax.rsqrt(jnp.mean(stream * stream, axis=-1, keepdims=True) + EPS)
    return stream * scale * gain


def norm_back(stream, gain, grad_normed):
    scale = lax.rsqrt(jnp.mean(stream * stream, axis=-1, keepdims=True) + EPS)
    unit = stream * scale
    scaled = gain * grad_normed
    grad = scale * (scaled - unit * jnp.mean(scaled * unit, axis=-1, keepdims=True))
    return grad, jnp.sum(grad_normed * unit, axis=0, keepdims=True)


GELU_SCALE = 0.7978845608028654
GELU_CUBE = 0.044715


def gelu_parts(value):
    square = value * value
    curve = jnp.tanh(GELU_SCALE * (value + GELU_CUBE * value * square))
    active = 0.5 * value * (1.0 + curve)
    slope = 0.5 * (1.0 + curve) + 0.5 * value * (1.0 - curve * curve) * GELU_SCALE * (
        1.0 + 3.0 * GELU_CUBE * square
    )
    return active, slope


def block_rows(index):
    return pl.ds(pl.multiple_of(index * ROWS, ROWS), ROWS)


def attend_block(block, causal, biased, ql_ref, kl_ref, q_block, k_ref, vt_ref, kd_ref, s_ref, o_acc, tiles_ref, lse_ref):
    keys, width = k_ref.shape
    heads = width // DK
    q_ends = doc_ends(ql_ref)
    q_docs = docs_at(block * BQ + lax.broadcasted_iota(jnp.int32, (1, BQ), 1), q_ends)
    queries = q_block * jnp.bfloat16(DK ** (-0.5))
    masked = [queries * head_mask(h, width) for h in range(heads)]
    low, high = key_range(ql_ref, q_ends, kl_ref, block, causal)

    def first(chunk, tops):
        rows = pl.ds(pl.multiple_of(chunk * KC, KC), KC)
        docs = jnp.concatenate([kd_ref[rows, :]] * (BQ // TILE), axis=1)
        allowed = docs == q_docs
        fresh = []
        for h in range(heads):
            scores = dot_last(k_ref[rows, :], masked[h])
            if biased:
                scores = scores + tile_rows(tiles_ref, h, block, chunk, keys)
            scores = jnp.where(allowed, scores, NEG)
            s_ref[h, rows, :] = scores
            fresh.append(jnp.maximum(tops[h], jnp.max(scores, axis=0, keepdims=True)))
        return tuple(fresh)

    tops = lax.fori_loop(
        low, high, first, tuple(jnp.full((1, BQ), NEG, jnp.float32) for _ in range(heads))
    )
    o_acc[...] = jnp.zeros_like(o_acc)

    def second(chunk, totals):
        rows = pl.ds(pl.multiple_of(chunk * KC, KC), KC)
        fresh = []
        for h in range(heads):
            probs = jnp.exp(s_ref[h, rows, :] - tops[h])
            fresh.append(totals[h] + jnp.sum(probs, axis=0, keepdims=True))
            o_acc[h * DK : (h + 1) * DK, :] += dot(
                vt_ref[h * DK : (h + 1) * DK, rows], probs.astype(jnp.bfloat16)
            )
        return tuple(fresh)

    totals = lax.fori_loop(
        low, high, second, tuple(jnp.zeros((1, BQ), jnp.float32) for _ in range(heads))
    )
    outs = []
    for h in range(heads):
        lse_ref[h : h + 1, :] = tops[h] + jnp.log(totals[h])
        outs.append(o_acc[h * DK : (h + 1) * DK, :] / totals[h])
    return jnp.concatenate(outs, axis=0).astype(jnp.bfloat16).astype(jnp.float32)


def put_out(out, o_ref, ot_ref):
    o_ref[...] = jnp.transpose(out).astype(jnp.bfloat16)
    ot_ref[...] = out


def order_pieces(me, own, far, sib, sibfar, target_ref):
    other = lax.rem(me + 2, 4)
    beside = me + 1 - 2 * lax.rem(me, 2)
    target_ref[me] = own
    target_ref[other] = far
    target_ref[beside] = sib
    target_ref[lax.rem(beside + 2, 4)] = sibfar


def order_weights(me, refs, target_ref):
    order_pieces(me, *[ref[...].astype(jnp.bfloat16) for ref in refs], target_ref)


def out_product(me, refs, lanes, weights_ref, pieces_ref):
    order_pieces(me, *[ref[:, lanes] for ref in refs], pieces_ref)
    total = None
    for m in range(4):
        left = jnp.transpose(pieces_ref[m]).astype(jnp.bfloat16)
        product = dot(left, weights_ref[m])
        total = product if total is None else total + product
    return total


def self_forward_kernel(causal, *refs):
    ql_ref, x_ref, gain_ref, wq_ref, wk_ref, wv_ref, buckets_ref, table_ref = refs[:8]
    n_ref, q_ref, k_ref, v_ref, o_ref, lse_ref = refs[8:14]
    ot_ref = refs[14]
    vt_ref, kd_ref, s_ref, o_acc, tiles_ref = refs[15:]
    block = pl.program_id(0)
    keys = k_ref.shape[0]

    @pl.when(block == 0)
    def _():
        for b in range(keys // ROWS):
            rows = slice(b * ROWS, (b + 1) * ROWS)
            normed = ref_norm(x_ref[rows, :].astype(jnp.float32), gain_ref[...]).astype(
                jnp.bfloat16
            )
            n_ref[rows, :] = normed
            q_ref[rows, :] = dot_last(normed, wq_ref[...]).astype(jnp.bfloat16)
            k_ref[rows, :] = dot_last(normed, wk_ref[...]).astype(jnp.bfloat16)
            value = dot_last(normed, wv_ref[...])
            v_ref[rows, :] = value.astype(jnp.bfloat16)
            vt_ref[:, rows] = jnp.transpose(value).astype(jnp.bfloat16)
        kd_ref[...] = docs_at(
            lax.broadcasted_iota(jnp.int32, (keys, TILE), 0), doc_ends(ql_ref)
        )
        make_tiles(buckets_ref, table_ref, tiles_ref)

    out = attend_block(
        block, causal, True, ql_ref, ql_ref, q_ref[block_rows(block), :],
        k_ref, vt_ref, kd_ref, s_ref, o_acc, tiles_ref, lse_ref,
    )
    put_out(out, o_ref, ot_ref)


def cross_forward_kernel(*refs):
    me_ref, ql_ref, kl_ref, y0_ref = refs[:4]
    dec_pieces, dec_weights = refs[4:8], refs[8:12]
    x1_ref, enc_sum_ref, gain_ref, wq_ref, wk_ref, wv_ref = refs[12:18]
    y1_ref, n_ref, memory_ref, q_ref, k_ref, v_ref, o_ref, lse_ref, ot_ref = refs[18:27]
    vt_ref, kd_ref, s_ref, o_acc, weights_ref, pieces_ref = refs[27:]
    block = pl.program_id(0)
    keys = k_ref.shape[0]
    me = me_ref[0]

    @pl.when(block == 0)
    def _():
        for b in range(keys // ROWS):
            rows = slice(b * ROWS, (b + 1) * ROWS)
            memory = (x1_ref[rows, :] + enc_sum_ref[rows, :]).astype(jnp.bfloat16)
            memory_ref[rows, :] = memory
            k_ref[rows, :] = dot_last(memory, wk_ref[...]).astype(jnp.bfloat16)
            value = dot_last(memory, wv_ref[...])
            v_ref[rows, :] = value.astype(jnp.bfloat16)
            vt_ref[:, rows] = jnp.transpose(value).astype(jnp.bfloat16)
        kd_ref[...] = docs_at(
            lax.broadcasted_iota(jnp.int32, (keys, TILE), 0), doc_ends(kl_ref)
        )
        order_weights(me, dec_weights, weights_ref)

    summed = out_product(me, dec_pieces, slice(None), weights_ref, pieces_ref)
    stream = y0_ref[...].astype(jnp.float32) + summed
    y1_ref[...] = stream
    normed = ref_norm(stream, gain_ref[...]).astype(jnp.bfloat16)
    n_ref[...] = normed
    queries = dot_last(normed, wq_ref[...]).astype(jnp.bfloat16)
    q_ref[...] = queries
    out = attend_block(
        block, False, False, ql_ref, kl_ref, queries,
        k_ref, vt_ref, kd_ref, s_ref, o_acc, None, lse_ref,
    )
    put_out(out, o_ref, ot_ref)


def ffn_forward_kernel(*refs):
    me_ref, x_ref = refs[:2]
    pieces, weights = refs[2:6], refs[6:10]
    gain_ref, wi_ref, wo_ref, x1_ref, n_ref, hid_ref, act_ref, part_ref = refs[10:18]
    weights_ref, pieces_ref = refs[18:]
    me = me_ref[0]

    @pl.when(pl.program_id(0) == 0)
    def _():
        order_weights(me, weights, weights_ref)

    summed = out_product(me, pieces, slice(None), weights_ref, pieces_ref)
    stream = x_ref[...].astype(jnp.float32) + summed
    x1_ref[...] = stream
    normed = ref_norm(stream, gain_ref[...]).astype(jnp.bfloat16)
    n_ref[...] = normed
    hidden = dot(normed, wi_ref[...])
    hid_ref[...] = hidden
    active = gelu_parts(hidden)[0].astype(jnp.bfloat16)
    act_ref[...] = active
    part_ref[...] = dot(active, wo_ref[...])


def ffn_both_kernel(*refs):
    me_ref, y_ref = refs[:2]
    pieces, weights = refs[2:6], refs[6:10]
    gain_ref, wi_ref, wo_ref, cot_ref = refs[10:14]
    y2_ref, n_ref, act_ref, dhid_ref, part_ref, out_part_ref, weights_ref, pieces_ref = refs[14:]
    me = me_ref[0]

    @pl.when(pl.program_id(0) == 0)
    def _():
        order_weights(me, weights, weights_ref)

    summed = out_product(me, pieces, slice(None), weights_ref, pieces_ref)
    stream = y_ref[...] + summed
    y2_ref[...] = stream
    normed = ref_norm(stream, gain_ref[...]).astype(jnp.bfloat16)
    n_ref[...] = normed
    active, slope = gelu_parts(dot(normed, wi_ref[...]))
    active = active.astype(jnp.bfloat16)
    act_ref[...] = active
    grad = (slope * dot_last(cot_ref[...], wo_ref[...])).astype(jnp.bfloat16)
    dhid_ref[...] = grad
    part_ref[...] = dot_last(grad, wi_ref[...])
    out_part_ref[...] = dot(active, wo_ref[...])


def ffn_backward_kernel(cot_ref, sum_ref, hid_ref, wi_ref, wo_ref, x_ref, g_ref, dhid_ref, part_ref):
    stream = cot_ref[...].astype(jnp.float32) + sum_ref[...]
    x_ref[...] = stream
    branch = stream.astype(jnp.bfloat16)
    g_ref[...] = branch
    slope = gelu_parts(hid_ref[...])[1]
    grad = (slope * dot_last(branch, wo_ref[...])).astype(jnp.bfloat16)
    dhid_ref[...] = grad
    part_ref[...] = dot_last(grad, wi_ref[...])


def half_rows(core, block, mine_ref, sib_ref):
    local = block_rows(lax.rem(block, 2))
    return jnp.where(block // 2 == core, mine_ref[local, :], sib_ref[local, :])


def piece_rows(core, block, refs):
    near, far, near_sib, far_sib = refs
    return half_rows(core, block, near, near_sib) + half_rows(core, block, far, far_sib)


def closing_kernel(x0_ref, eb_ref, egain_ref, z_ref, y0_ref, sb_ref, dgain_ref, s_ref, y2_ref, l_ref,
                   enc_ref, dec_ref, result_ref):
    for start, stream, gain, summed, out in (
        (x0_ref, eb_ref, egain_ref, z_ref, enc_ref), (y0_ref, sb_ref, dgain_ref, s_ref, dec_ref)
    ):
        grad, _ = norm_back(start[...].astype(jnp.float32), gain[...], summed[...])
        out[...] = stream[...] + grad
    result_ref[...] = (y2_ref[...] + l_ref[...]).astype(result_ref.dtype)


def attention_back_kernel(causal, biased, pieces, *refs):
    refs = list(refs)
    take = lambda n: [refs.pop(0) for _ in range(n)]
    core_ref, ql_ref, kl_ref = take(3)
    base_ref, stream_ref = take(2)
    dn_refs = take(pieces)
    gain_ref, wo_ref, q_ref, k_ref, v_ref, o_ref, lse_ref, wq_ref, wk_ref, wv_ref = take(10)
    buckets_ref, table_ref, x0_ref = take(3) if biased else (None, None, None)
    x_ref, g_ref, dq_ref, dk_ref, dv_ref, gain_grad_ref = take(6)
    if biased:
        dtable_ref, own_gain_ref = take(2)
    part_ref = take(1)[0]
    memory_part_ref = None if biased else take(1)[0]
    kt_ref, kd_ref, dq_acc, dk_acc, dv_acc = take(5)
    tiles_ref, grad_ref = take(2) if biased else (None, None)
    block = pl.program_id(0)
    keys, width = k_ref.shape
    heads = width // DK
    core = core_ref[0]
    q_ends = doc_ends(ql_ref)
    scale = jnp.bfloat16(DK ** (-0.5))

    @pl.when(block == 0)
    def _():
        kt_ref[...] = flip(k_ref[...])
        kd_ref[...] = docs_at(
            lax.broadcasted_iota(jnp.int32, (keys, TILE), 0), doc_ends(kl_ref)
        )
        dk_acc[...] = jnp.zeros_like(dk_acc)
        dv_acc[...] = jnp.zeros_like(dv_acc)
        gain_grad_ref[...] = jnp.zeros_like(gain_grad_ref)
        if biased:
            make_tiles(buckets_ref, table_ref, tiles_ref)
            grad_ref[...] = jnp.zeros_like(grad_ref)

    if pieces == 1:
        grad_normed = dn_refs[0][...]
    else:
        grad_normed = piece_rows(core, block, dn_refs)
    grad_in, gain_grad = norm_back(stream_ref[...], gain_ref[...], grad_normed)
    gain_grad_ref[...] += gain_grad
    grad_stream = base_ref[...].astype(jnp.float32) + grad_in
    x_ref[...] = grad_stream
    branch = grad_stream.astype(jnp.bfloat16)
    g_ref[...] = branch
    grads = dot_last(branch, wo_ref[...]).astype(jnp.bfloat16)

    q_docs = docs_at(block * BQ + lax.broadcasted_iota(jnp.int32, (1, BQ), 1), q_ends)
    queries = q_ref[...] * scale
    product = grads.astype(jnp.float32) * o_ref[...].astype(jnp.float32)
    pick = jnp.concatenate(
        [head_mask(h, width).astype(jnp.float32) for h in range(heads)]
        + [jnp.zeros((8 - heads, width), jnp.float32)],
        axis=0,
    )
    inner = lax.dot_general(
        pick,
        product,
        (((1,), (1,)), ((), ())),
        precision=HIGHEST,
        preferred_element_type=jnp.float32,
    )
    q_masked = [queries * head_mask(h, width) for h in range(heads)]
    g_masked = [grads * head_mask(h, width) for h in range(heads)]
    low, high = key_range(ql_ref, q_ends, kl_ref, block, causal)
    dq_acc[...] = jnp.zeros_like(dq_acc)

    @pl.loop(low, high)
    def _(chunk):
        rows = pl.ds(pl.multiple_of(chunk * KC, KC), KC)
        docs = jnp.concatenate([kd_ref[rows, :]] * (BQ // TILE), axis=1)
        allowed = docs == q_docs
        dk = dk_acc[rows, :]
        dv = dv_acc[rows, :]
        for h in range(heads):
            scores = dot_last(k_ref[rows, :], q_masked[h])
            if biased:
                scores = scores + tile_rows(tiles_ref, h, block, chunk, keys)
            scores = jnp.where(allowed, scores, NEG)
            probs = jnp.exp(scores - lse_ref[h : h + 1, :])
            grad_probs = dot_last(v_ref[rows, :], g_masked[h])
            grad_scores = (probs * (grad_probs - inner[h : h + 1, :])).astype(jnp.bfloat16)
            dv = dv + dot(probs.astype(jnp.bfloat16), g_masked[h])
            dk = dk + dot(grad_scores, q_masked[h])
            dq_acc[h * DK : (h + 1) * DK, :] += dot(
                kt_ref[h * DK : (h + 1) * DK, rows], grad_scores
            )
            if biased:
                for t in range(BQ // TILE):
                    start = keys - TILE - TILE * (block * (BQ // TILE) + t) + chunk * KC
                    piece = pl.ds(pl.multiple_of(start, TILE), KC)
                    grad_ref[h, piece, :] += grad_scores[:, t * TILE : (t + 1) * TILE].astype(
                        jnp.float32
                    )
        dk_acc[rows, :] = dk
        dv_acc[rows, :] = dv

    dq = (jnp.transpose(dq_acc[...]) * DK ** (-0.5)).astype(jnp.bfloat16)
    dq_ref[block_rows(block), :] = dq

    @pl.when(block == pl.num_programs(0) - 1)
    def _():
        dk_ref[...] = dk_acc[...].astype(jnp.bfloat16)
        dv_ref[...] = dv_acc[...].astype(jnp.bfloat16)
        own_gain = jnp.zeros(gain_grad_ref.shape, jnp.float32)
        for b in range(keys // ROWS):
            rows = slice(b * ROWS, (b + 1) * ROWS)
            from_q = dot(dq_ref[rows, :], wq_ref[...])
            from_kv = dot(dk_ref[rows, :], wk_ref[...]) + dot(
                dv_ref[rows, :], wv_ref[...]
            )
            if not biased:
                part_ref[rows, :] = from_q
                memory_part_ref[rows, :] = from_kv
                continue
            total = from_q + from_kv
            part_ref[rows, :] = total
            start = x0_ref[rows, :].astype(jnp.float32)
            unit = start * lax.rsqrt(jnp.mean(start * start, axis=-1, keepdims=True) + EPS)
            own_gain = own_gain + jnp.sum(total * unit, axis=0, keepdims=True)
        if biased:
            own_gain_ref[...] = own_gain
            sum_tiles(buckets_ref, grad_ref, dtable_ref)


def whole(shape):
    return pl.BlockSpec(shape, lambda *_: (0,) * len(shape), pipeline_mode=pl.Buffered(1))


def rows_spec(width):
    return pl.BlockSpec((BQ, width), lambda i: (i, 0))


def lanes_spec():
    return pl.BlockSpec((8, BQ), lambda i: (0, i))


SMEM_SPEC = pl.BlockSpec(memory_space=pltpu.SMEM)
BF16, F32 = jnp.bfloat16, jnp.float32


def call(kernel, name, grid, inputs, outputs, scratch, flops, exps=0):
    def size(shape, dtype):
        count = 1
        for dim in shape:
            count *= dim
        return count * jnp.dtype(dtype).itemsize

    moved = sum(size(a.shape, a.dtype) for a, _ in inputs) + sum(size(s, d) for s, d, _ in outputs)
    return pl.pallas_call(
        kernel,
        grid=grid,
        in_specs=[spec for _, spec in inputs],
        out_specs=[spec for _, _, spec in outputs],
        out_shape=[jax.ShapeDtypeStruct(shape, dtype) for shape, dtype, _ in outputs],
        scratch_shapes=scratch,
        compiler_params=pltpu.CompilerParams(
            dimension_semantics=("arbitrary",) * len(grid), vmem_limit_bytes=VMEM_BYTES
        ),
        cost_estimate=pl.CostEstimate(flops=flops // SPEEDUP, bytes_accessed=moved // SPEEDUP, transcendentals=exps // SPEEDUP),
        name=name,
    )(*[a for a, _ in inputs])


def full(array):
    return (array, whole(array.shape))


def attention_scratch(width, keys, biased):
    heads = width // DK
    scratch = [
        pltpu.VMEM((width, keys), BF16),
        pltpu.VMEM((keys, TILE), jnp.int32),
        pltpu.VMEM((heads, keys, BQ), F32),
        pltpu.VMEM((width, BQ), F32),
    ]
    if biased:
        scratch.append(pltpu.VMEM((heads, 2 * keys - TILE, TILE), F32))
    return scratch


def transposed_spec(width):
    return pl.BlockSpec((width, BQ), lambda i: (0, i))


def self_forward(lens, x, gain, wq, wk, wv, bias, causal, name):
    seq, model = x.shape
    width = wq.shape[0]
    inputs = [(lens, SMEM_SPEC)]
    inputs += [full(a) for a in (x, gain, wq, wk, wv, bias[0], bias[1])]
    outputs = [((seq, model), BF16, whole((seq, model)))]
    outputs += [((seq, width), BF16, whole((seq, width)))] * 3
    outputs += [((seq, width), BF16, rows_spec(width)), ((8, seq), F32, lanes_spec())]
    outputs.append(((width, seq), F32, transposed_spec(width)))
    result = call(
        functools.partial(self_forward_kernel, causal), name, (seq // BQ,), inputs, outputs,
        attention_scratch(width, seq, True), 6 * seq * model * width + 2 * seq * seq * width,
        seq * seq,
    )
    return result[:6], result[6]


def order_scratch(width, model, rows):
    return [pltpu.VMEM((4, width, model), BF16), pltpu.VMEM((4, width, rows), F32)]


def piece_inputs(pieces, weights):
    width = pieces[0].shape[0]
    return [(a, transposed_spec(width)) for a in pieces] + [full(a) for a in weights]


def cross_forward(me, ql, kl, y0, pieces, weights, x1, enc_sum, gain, wq, wk, wv):
    seq, model = y0.shape
    width = wq.shape[0]
    inputs = [(me, SMEM_SPEC), (ql, SMEM_SPEC), (kl, SMEM_SPEC), (y0, rows_spec(model))]
    inputs += piece_inputs(pieces, weights)
    inputs += [full(a) for a in (x1, enc_sum, gain, wq, wk, wv)]
    outputs = [
        ((seq, model), F32, rows_spec(model)),
        ((seq, model), BF16, rows_spec(model)),
        ((seq, model), BF16, whole((seq, model))),
        ((seq, width), BF16, rows_spec(width)),
        ((seq, width), BF16, whole((seq, width))),
        ((seq, width), BF16, whole((seq, width))),
        ((seq, width), BF16, rows_spec(width)),
        ((8, seq), F32, lanes_spec()),
        ((width, seq), F32, transposed_spec(width)),
    ]
    scratch = attention_scratch(width, seq, False) + order_scratch(width, model, ROWS)
    result = call(
        cross_forward_kernel, "cross_forward", (seq // BQ,), inputs, outputs, scratch,
        14 * seq * model * width + 2 * seq * seq * width, seq * seq,
    )
    return result[:8], result[8]


def row_outputs(seq, *kinds):
    return [((seq, width), dtype, rows_spec(width)) for width, dtype in kinds]


def ffn_forward(me, x, pieces, weights, gain, wi, wo):
    seq, model = x.shape
    units = wi.shape[1]
    inputs = [(me, SMEM_SPEC), (x, rows_spec(model))] + piece_inputs(pieces, weights)
    inputs += [full(a) for a in (gain, wi, wo)]
    outputs = row_outputs(seq, (model, F32), (model, BF16), (units, F32), (units, BF16), (model, F32))
    return call(
        ffn_forward_kernel, "ffn_forward", (seq // ROWS,), inputs, outputs,
        order_scratch(weights[0].shape[0], model, ROWS), 6 * seq * model * units, seq * units,
    )


def ffn_both(me, y, pieces, weights, gain, wi, wo, cot):
    seq, model = y.shape
    units = wi.shape[1]
    inputs = [(me, SMEM_SPEC), (y, rows_spec(model))] + piece_inputs(pieces, weights)
    inputs += [full(a) for a in (gain, wi, wo)] + [(cot, rows_spec(model))]
    outputs = row_outputs(
        seq, (model, F32), (model, BF16), (units, BF16), (units, BF16), (model, F32), (model, F32)
    )
    return call(
        ffn_both_kernel, "ffn_both", (seq // ROWS,), inputs, outputs,
        order_scratch(weights[0].shape[0], model, ROWS), 10 * seq * model * units, seq * units,
    )


def ffn_backward(cot, summed, hid, wi, wo):
    seq, units = hid.shape
    model = wi.shape[0]
    inputs = [(cot, rows_spec(model)), (summed, rows_spec(model)), (hid, rows_spec(units))]
    inputs += [full(wi), full(wo)]
    outputs = row_outputs(seq, (model, F32), (model, BF16), (units, BF16), (model, F32))
    return call(
        ffn_backward_kernel, "ffn_backward", (seq // ROWS,), inputs, outputs, [],
        4 * seq * model * units, seq * units,
    )


def closing(x0, eb, enc_gain, enc_sum, y0, sb, dec_gain, dec_sum, y2, last):
    seq, model = x0.shape
    inputs = [
        full(a) if a.shape[0] == 1 else (a, rows_spec(model))
        for a in (x0, eb, enc_gain, enc_sum, y0, sb, dec_gain, dec_sum, y2, last)
    ]
    return call(
        closing_kernel, "closing", (seq // ROWS,), inputs,
        row_outputs(seq, (model, F32), (model, F32), (model, BF16)), [], 20 * seq * model,
    )


def dot_rows(left, right):
    return lax.dot_general(
        left, right, (((0,), (0,)), ((), ())), preferred_element_type=jnp.float32
    )


def attention_weights_kernel(dq_ref, dk_ref, dv_ref, o_ref, n_ref, m_ref, g_ref, out_ref):
    count = dq_ref.shape[1]
    pairs = ((dq_ref, n_ref), (dk_ref, m_ref), (dv_ref, m_ref), (o_ref, g_ref))
    for i, (left, right) in enumerate(pairs):
        out_ref[i * count : (i + 1) * count, :] = dot_rows(left[...], right[...])


def attention_weights(grads, attended, normed, memory):
    seq, model = normed.shape
    width = attended.shape[1]
    inputs = [full(a) for a in (*grads[2:5], attended, normed, memory, grads[1])]
    outputs = [((4 * width, model), F32, whole((4 * width, model)))]
    return call(
        attention_weights_kernel, "attention_weights", (1,), inputs, outputs, [],
        8 * seq * model * width,
    )[0]


def attention_back(
    core, ql, kl, base, stream, dn, gain, wo, kept, wq, wk, wv, bias, x0, causal, name
):
    q, k, v, o, lse = kept
    seq, width = q.shape
    model = wo.shape[1]
    heads = width // DK
    biased = bias is not None
    inputs = [(core, SMEM_SPEC), (ql, SMEM_SPEC), (kl, SMEM_SPEC)]
    inputs += [(base, rows_spec(model)), (stream, rows_spec(model))]
    inputs += [(dn[0], rows_spec(model))] if len(dn) == 1 else [full(a) for a in dn]
    inputs += [full(gain), full(wo)]
    inputs += [(q, rows_spec(width)), full(k), full(v), (o, rows_spec(width)), (lse, lanes_spec())]
    inputs += [full(wq), full(wk), full(wv)]
    if biased:
        inputs += [full(bias[0]), full(bias[1]), full(x0)]
    outputs = [((seq, model), F32, rows_spec(model)), ((seq, model), BF16, rows_spec(model))]
    outputs += [((seq, width), BF16, whole((seq, width)))] * 3
    outputs.append(((1, model), F32, whole((1, model))))
    if biased:
        outputs.append((bias[1].shape, F32, whole(bias[1].shape)))
        outputs.append(((1, model), F32, whole((1, model))))
    outputs.append(((seq, model), F32, whole((seq, model))))
    if not biased:
        outputs.append(((seq, model), F32, whole((seq, model))))
    scratch = [
        pltpu.VMEM((width, seq), BF16),
        pltpu.VMEM((seq, TILE), jnp.int32),
        pltpu.VMEM((width, BQ), F32),
        pltpu.VMEM((seq, width), F32),
        pltpu.VMEM((seq, width), F32),
    ]
    if biased:
        scratch += [pltpu.VMEM((heads, 2 * seq - TILE, TILE), F32)] * 2
    result = call(
        functools.partial(attention_back_kernel, causal, biased, len(dn)),
        name, (seq // BQ,), inputs,
        outputs, scratch, 8 * seq * model * width + 5 * seq * seq * width, seq * seq,
    )
    return result[:6], result[6:]


MESH_ID = pl.DeviceIdType.MESH
MB_PER_ROW = 0.768 * 4 / 1000
RATES = (2.0, 21.0, 21.3, 21.5, 44.0)
DEPTH = 2


class Copies:
    def __init__(self, send_sem, recv_sem):
        self.send_sem, self.recv_sem = send_sem, recv_sem
        self.all, self.steps, self.first = [], [], []

    def copy(self, source, target, axis, index, link, rows, stage=0):
        i = len(self.all)

        def make():
            return pltpu.make_async_remote_copy(
                src_ref=source,
                dst_ref=target,
                send_sem=self.send_sem.at[i],
                recv_sem=self.recv_sem.at[i],
                device_id={axis: index},
                device_id_type=MESH_ID,
            )

        self.all.append((make, link, rows, stage))
        return i

    def step(self, waits, work, starts):
        self.steps.append((waits, work, starts))

    def start(self, i):
        make, link, rows, _ = self.all[i]
        self.made[i] = make()
        self.made[i].start()
        begin = max(self.now, self.free.get(link, 0.0))
        if link == 4:
            half = 22.0 * rows * MB_PER_ROW
            begin = max(begin, self.free.get(3, 0.0) - half)
            self.free[3] = max(self.free.get(3, 0.0), begin) + half
        self.free[link] = begin + RATES[link] * rows * MB_PER_ROW
        self.arrive[i] = self.free[link] + 1.0

    def fill(self):
        for i in sorted(self.pending, key=lambda i: (-self.all[i][3], i)):
            link = self.all[i][1]
            busy = sum(self.all[j][1] == link and self.arrive[j] > self.now for j in self.made)
            if busy < DEPTH or link < 2:
                self.pending.remove(i)
                self.start(i)

    def run(self):
        self.now, self.free, self.arrive, self.made = 0.0, {}, {}, {}
        self.pending = list(self.first)
        left = list(self.steps)
        self.fill()
        while left:
            ready = [s for s in left if all(i in self.made for i in s[0])]
            step = min(ready, key=lambda s: max([self.arrive[i] for i in s[0]], default=0.0))
            left.remove(step)
            for i in step[0]:
                self.made[i].wait_recv()
                self.now = max(self.now, self.arrive[i])
            if step[1] is not None:
                step[1]()
            self.pending += step[2]
            self.fill()
        for made in self.made.values():
            made.wait_send()


def mp_partners():
    me = lax.axis_index("mp")
    core = lax.rem(me, 2)
    return core, me + 1 - 2 * core, lax.rem(me + 2, 4)


def dp_side(bit):
    return lax.rem(lax.axis_index("dp") // (1 << bit), 2)


def dp_partner(bit):
    return lax.axis_index("dp") + (1 << bit) * (1 - 2 * dp_side(bit))


def greet(bits):
    barrier = pltpu.get_barrier_semaphore()
    _, beside, across = mp_partners()
    ids = [{"mp": beside}, {"mp": across}] + [{"dp": dp_partner(bit)} for bit in bits]
    for device_id in ids:
        pl.semaphore_signal(barrier, inc=1, device_id=device_id, device_id_type=MESH_ID)
    pl.semaphore_wait(barrier, len(ids))


def rows_at(start, count):
    return pl.ds(pl.multiple_of(start, 8), count)


def mp_job(copies, part_ref, near_ref, far_ref, out_ref, chunks, finish=None, far=True):
    core, beside, across = mp_partners()
    count = part_ref.shape[0] // (2 * chunks)

    def one(k):
        mine = rows_at((2 * k + core) * count, count)
        other = rows_at((2 * k + 1 - core) * count, count)
        first = copies.copy(part_ref.at[other, :], near_ref.at[k], "mp", beside, 0, count)
        copies.first.append(first)

        def add_near():
            near_ref[k] = part_ref[mine, :] + near_ref[k]

        second = copies.copy(near_ref.at[k], far_ref.at[k], "mp", across, 1, count)
        copies.step([first], add_near, [second])

        def add_far():
            out_ref[mine, :] = near_ref[k] + far_ref[k]
            if finish is not None:
                finish(mine)

        third = copies.copy(out_ref.at[mine, :], out_ref.at[mine, :], "mp", beside, 0, count)
        copies.step([second], add_far, [third])
        copies.step([third], None if finish is None else lambda: finish(other), [])

    for k in range(chunks):
        one(k)


def near_job(copies, part_ref, land_ref, out_ref):
    core, beside, _ = mp_partners()
    count = part_ref.shape[0] // 2
    mine = rows_at(core * count, count)
    other = rows_at((1 - core) * count, count)
    first = copies.copy(part_ref.at[other, :], land_ref, "mp", beside, 0, count)
    copies.first.append(first)

    def add():
        out_ref[...] = part_ref[mine, :] + land_ref[...]

    copies.step([first], add, [])


LINKS = (2, 3, 4)


def scatter_job(copies, part_ref, land_refs, bits, base, rows, store, got_ref=None):
    start, count, waits, work = base, rows, None, None
    source, origin = part_ref, 0
    for level, bit in enumerate(bits):
        count = count // 2
        side = dp_side(bit)
        keep = start + side * count
        give = start + (1 - side) * count
        land = land_refs[level]
        place = base // rows * count
        landing = slice(place, place + count)
        got = land
        if level == 0 and got_ref is not None:
            made, got = None, got_ref
        else:
            made = copies.copy(
                source.at[rows_at(give - origin, count), :], land.at[landing, :], "dp",
                dp_partner(bit), LINKS[min(bit, 2)], count, level,
            )
            if level == 0:
                copies.first.append(made)
            else:
                copies.step(waits, work, [made])

        def work(
            source=source, origin=origin, keep=keep, land=land, got=got, landing=landing, count=count
        ):
            land[landing, :] = source[rows_at(keep - origin, count), :] + got[landing, :]

        waits = [] if made is None else [made]
        source, origin, start = land, keep - place, keep

    def last(add=work, land=land, landing=landing, start=start, count=count):
        add()
        store(start, count, land[landing, :])

    return waits, last


def gather_job(copies, out_ref, bits, base, rows, waits, work):
    count = rows >> len(bits)
    start, size = base, rows
    for bit in bits:
        size = size // 2
        start = start + dp_side(bit) * size
    for level, bit in enumerate(reversed(bits)):
        held = rows_at(start, count)
        made = copies.copy(
            out_ref.at[held, :], out_ref.at[held, :], "dp", dp_partner(bit),
            LINKS[min(bit, 2)], count, len(bits) + level,
        )
        if waits is None:
            work()
            copies.first.append(made)
        else:
            copies.step(waits, work, [made])
        waits, work = [made], None
        start = start - dp_side(bit) * count
        count = count * 2
    copies.step(waits, None, [])


def small_job(copies, small_ref, land_ref, held_ref, out_ref, bits, shared):
    core, beside, across = mp_partners()
    hops = [("mp", beside, 0), ("mp", across, 1)]
    hops += [("dp", dp_partner(bit), LINKS[min(bit, 2)]) for bit in bits]
    count = small_ref.shape[0]
    first_rows = lax.broadcasted_iota(jnp.int32, small_ref.shape, 0) < shared
    source, waits, work = small_ref, None, None
    for i, (axis, index, link) in enumerate(hops):
        made = copies.copy(source, land_ref.at[i], axis, index, link, count)
        if i == 0:
            copies.first.append(made)
        else:
            copies.step(waits, work, [made])

        def work(i=i, source=source, last=i == len(hops) - 1):
            got = land_ref[i]
            if i < 2:
                got = jnp.where(first_rows, got, 0.0)
            target = out_ref if last else held_ref.at[i]
            target[...] = source[...] + got

        waits, source = [made], held_ref.at[i]
    copies.step(waits, work, [])


CHUNKS = 4
PIECES = 4


def sums(number, parts=(), near=(), scatter=(), gather=(), units=(), turns=(), halves=(), small=None, shared=0):
    bits = list(range((lax.axis_size("dp") - 1).bit_length()))
    turned = bits[1:] + bits[:1]
    dp = bool(scatter or gather or units or small is not None)
    smalls = [] if small is None else [small]
    inputs = [*parts, *near, *scatter, *gather, *units, *smalls, *halves]
    model = inputs[0].shape[1]
    shares = lax.axis_size("dp")
    outputs = [(a.shape, F32) for a in parts]
    outputs += [((a.shape[0] // 2, model), F32) for a in near]
    outputs += [((a.shape[0] // shares, model), F32) for a in scatter]
    outputs += [((a.shape[0] * shares, model), F32) for a in gather]
    outputs += [(a.shape, F32) for a in (*units, *smalls)]
    lands = []
    for a in parts:
        lands += [pltpu.VMEM((CHUNKS, a.shape[0] // (2 * CHUNKS), model), F32)] * 2
    for a in near:
        lands.append(pltpu.VMEM((a.shape[0] // 2, model), F32))
    for a in (*scatter, *units):
        lands += [pltpu.VMEM((a.shape[0] >> (i + 1), model), F32) for i in range(len(bits))]
    for a in smalls:
        lands += [pltpu.VMEM((2 + len(bits), *a.shape), F32)] * 2
    count, ends = len(inputs), len(inputs) + len(outputs)
    total = 3 * CHUNKS * len(parts) + len(near) + len(smalls) * (2 + len(bits))
    total += len(bits) * PIECES * (len(scatter) + len(gather) + 2 * len(units))

    def kernel(*refs):
        ins, outs = list(refs[:count]), list(refs[count:ends])
        scratch = list(refs[ends:-2])
        half_refs = [None] * (len(units) - len(halves)) + ins[count - len(halves) :]
        greet(bits if dp else [])
        copies = Copies(refs[-2], refs[-1])
        for _ in parts:
            mp_job(copies, ins.pop(0), scratch.pop(0), scratch.pop(0), outs.pop(0), CHUNKS)
        for _ in near:
            near_job(copies, ins.pop(0), scratch.pop(0), outs.pop(0))
        for a in scatter:
            part_ref, out_ref = ins.pop(0), outs.pop(0)
            land_refs = [scratch.pop(0) for _ in bits]
            rows = a.shape[0] // PIECES
            for piece in range(PIECES):

                def keep(start, count, value, piece=piece, out_ref=out_ref):
                    out_ref[piece * count : (piece + 1) * count, :] = value

                waits, work = scatter_job(
                    copies, part_ref, land_refs, bits, piece * rows, rows, keep
                )
                copies.step(waits, work, [])
        for a in gather:
            part_ref, out_ref = ins.pop(0), outs.pop(0)
            rows = a.shape[0] * shares // PIECES
            for piece in range(PIECES):
                start, size = piece * rows, rows
                for bit in bits:
                    size = size // 2
                    start = start + dp_side(bit) * size

                def put(start=start, size=size, piece=piece, part_ref=part_ref, out_ref=out_ref):
                    out_ref[rows_at(start, size), :] = part_ref[
                        piece * size : (piece + 1) * size, :
                    ]

                gather_job(copies, out_ref, bits, piece * rows, rows, None, put)
        for a, half_ref in zip(units, half_refs):
            part_ref, out_ref = ins.pop(0), outs.pop(0)
            land_refs = [scratch.pop(0) for _ in bits]
            rows = a.shape[0] // PIECES
            for piece in range(PIECES):

                def keep(start, count, value, out_ref=out_ref):
                    out_ref[rows_at(start, count), :] = value

                order = turned if piece in turns else bits
                waits, work = scatter_job(
                    copies, part_ref, land_refs, order, piece * rows, rows, keep, half_ref
                )
                gather_job(copies, out_ref, order, piece * rows, rows, waits, work)
        if small is not None:
            small_job(copies, ins[0], scratch[0], scratch[1], outs[0], bits, shared)
        copies.run()

    result = pl.pallas_call(
        kernel,
        in_specs=[whole(a.shape) for a in inputs],
        out_specs=[whole(shape) for shape, _ in outputs],
        out_shape=[jax.ShapeDtypeStruct(shape, dtype) for shape, dtype in outputs],
        grid=(1,),
        scratch_shapes=lands
        + [pltpu.SemaphoreType.DMA((total,)), pltpu.SemaphoreType.DMA((total,))],
        compiler_params=pltpu.CompilerParams(
            collective_id=number, has_side_effects=True, vmem_limit_bytes=VMEM_BYTES
        ),
        cost_estimate=pl.CostEstimate(flops=1, bytes_accessed=1, transcendentals=0),
        name="sums",
    )(*inputs)
    groups = []
    for group in (parts, near, scatter, gather, units, smalls):
        groups.append(list(result[: len(group)]))
        result = result[len(group) :]
    return groups


def first_half(unit):
    rows = unit.shape[0] // (2 * PIECES)
    pieces = unit.reshape(PIECES, 2, rows, unit.shape[1])
    other = 1 - lax.rem(lax.axis_index("dp"), 2)
    return lax.dynamic_index_in_dim(pieces, other, 1, False).reshape(PIECES * rows, -1)


def first_swap(value):
    pairs = [(i, i ^ 1) for i in range(lax.axis_size("dp"))]
    return lax.ppermute(value, "dp", pairs)


def shares_fit(rows):
    return rows % (8 * PIECES * lax.axis_size("dp")) == 0


CORE_SWAP = [(0, 1), (1, 0), (2, 3), (3, 2)]
CHIP_SWAP = [(0, 2), (2, 0), (1, 3), (3, 1)]


def core_swap(value):
    return lax.ppermute(value, "mp", CORE_SWAP)


def chip_swap(value):
    return lax.ppermute(value, "mp", CHIP_SWAP)


def part(value, start, rows):
    return lax.dynamic_slice_in_dim(value, start, rows, axis=0)


class Chain:
    def __init__(self):
        self.token = None

    def tie(self, value):
        if self.token is None:
            return value
        value, _ = lax.optimization_barrier((value, self.token))
        return value

    def mark(self, value):
        self.token = value


class Wire:
    def __init__(self, chain, swap):
        self.chain, self.swap = chain, swap

    def send(self, value):
        self.value = self.swap(self.chain.tie(value))

    def wait(self):
        self.value = self.chain.tie(self.value)
        self.chain.mark(self.value)
        return self.value


class Gather:
    def __init__(self, chain):
        self.chain = chain
        self.y, self.s, self.r = [Wire(chain, swap) for swap in (chip_swap, core_swap, core_swap)]

    def put(self, own):
        self.own = own

    def sy(self):
        self.y.send(self.own)

    def wy(self):
        self.y.wait()

    def ss(self):
        self.s.send(self.own)

    def ws(self):
        self.s.wait()

    def sr(self):
        self.r.send(self.y.value)

    def wr(self):
        self.r.wait()

    def pieces(self):
        return (self.own, self.y.value, self.s.value, self.r.value)


def project_weight(left, right):
    return lax.dot_general(
        left, right, (((0,), (0,)), ((), ())), preferred_element_type=jnp.float32
    )


def signed_buckets(buckets, seq):
    fill = jnp.full((2 * seq - buckets.shape[0],), -1, jnp.int32)
    return jnp.concatenate([fill, buckets])[None, :]


def body(
    encoder_input,
    decoder_input,
    encoder_lengths,
    decoder_lengths,
    encoder_buckets,
    decoder_buckets,
    encoder_attn_gain,
    encoder_query,
    encoder_key,
    encoder_value,
    encoder_output,
    encoder_bias,
    encoder_ffn_gain,
    encoder_ffn_in,
    encoder_ffn_out,
    decoder_attn_gain,
    decoder_query,
    decoder_key,
    decoder_value,
    decoder_output,
    decoder_bias,
    cross_gain,
    cross_query,
    cross_key,
    cross_value,
    cross_output,
    decoder_ffn_gain,
    decoder_ffn_in,
    decoder_ffn_out,
    encoder_cotangent,
    decoder_cotangent,
):
    _, seq, width = encoder_input.shape
    enc_lens, dec_lens = encoder_lengths, decoder_lengths
    enc_bias = (signed_buckets(encoder_buckets, seq), encoder_bias)
    dec_bias = (signed_buckets(decoder_buckets, seq), decoder_bias)
    me = lax.axis_index("mp").astype(jnp.int32).reshape(1)
    core = lax.rem(me, 2)
    x0, y0 = encoder_input[0], decoder_input[0]
    enc_cot, dec_cot = encoder_cotangent[0], decoder_cotangent[0]
    row = lambda gain: gain[None, :]
    encoder_query, encoder_key, encoder_value = encoder_query.T, encoder_key.T, encoder_value.T
    decoder_query, decoder_key, decoder_value = decoder_query.T, decoder_key.T, decoder_value.T
    cross_query, cross_key, cross_value = cross_query.T, cross_key.T, cross_value.T
    chain = Chain()
    tie, mark = chain.tie, chain.mark

    wide_e, wide, e, d, x = [Gather(chain) for _ in range(5)]
    wide_e.put(encoder_output.astype(F32))
    mark(wide_e.own)
    wide_e.sy()
    count = encoder_output.shape[0] // lax.axis_size("dp")
    place = lax.axis_index("dp") * count
    slices = Wire(chain, chip_swap)
    slices.send(
        jnp.concatenate(
            [part(decoder_output, place, count), part(cross_output, place, count)], axis=1
        ).astype(F32)
    )
    enc, out = self_forward(
        enc_lens, tie(x0), row(encoder_attn_gain), encoder_query, encoder_key, encoder_value,
        enc_bias, False, "encoder_attention",
    )
    mark(out)
    e.put(out)
    wide_e.wy()
    slices.wait()
    e.sy()
    e.ss()
    wide.y.value = lax.all_gather(tie(slices.value), "dp", axis=0, tiled=True)
    wide_e.sr()
    wide_e.ss()

    dec, out = self_forward(
        dec_lens, tie(y0), row(decoder_attn_gain), decoder_query, decoder_key, decoder_value,
        dec_bias, True, "decoder_attention",
    )
    mark(out)
    d.put(out)
    e.wy()
    e.sr()
    d.sy()
    e.ws()
    wide_e.ws()
    wide_e.wr()
    e.wr()
    own = jnp.concatenate([decoder_output, cross_output], axis=1).astype(F32)
    wide.put(own)

    ffn = ffn_forward(
        me, tie(x0), e.pieces(), wide_e.pieces(), row(encoder_ffn_gain), encoder_ffn_in,
        encoder_ffn_out,
    )
    mark(ffn[4])
    d.wy()
    d.ss()
    d.sr()
    wide.ss()
    enc_sum = sums(1, parts=[tie(ffn[4])])[0][0]
    mark(enc_sum)
    wide.sr()
    d.ws()
    d.wr()
    wide.ws()
    wide.wr()

    split = lambda i: tuple(value[:, i * width : (i + 1) * width] for value in wide.pieces())
    cross, out = cross_forward(
        me, dec_lens, enc_lens, tie(y0), d.pieces(), split(0), ffn[0], enc_sum, row(cross_gain),
        cross_query, cross_key, cross_value,
    )
    mark(out)
    x.put(out)
    x.sy()
    x.ss()
    x.wy()
    x.sr()
    x.ws()
    x.wr()

    both = ffn_both(
        me, tie(cross[0]), x.pieces(), split(1), row(decoder_ffn_gain), decoder_ffn_in,
        decoder_ffn_out, dec_cot,
    )
    mark(both[4])
    dec_ffn = jnp.concatenate(
        [project_weight(tie(both[1]), both[3]), project_weight(both[2], dec_cot)], axis=0
    )
    mark(dec_ffn)
    dec_ffn = lax.psum(dec_ffn, "dp")
    dn = sums(2, parts=[tie(both[4])])[0][0]
    mark(dn)

    cb, (own_part, memory_part) = attention_back(
        core, dec_lens, enc_lens, dec_cot, both[0], (tie(dn),), row(decoder_ffn_gain),
        cross_output, cross[3:8], cross_query, cross_key, cross_value, None, None, False,
        "cross_back",
    )
    mark(own_part)
    unit_2 = attention_weights((*cb[:2], tie(cb[2]), *cb[3:]), cross[6], cross[1], cross[2])
    mark(unit_2)
    split_units = shares_fit(width)
    totals, nears, shares, _, _, _ = sums(
        3, parts=[tie(memory_part)], near=[own_part], scatter=[unit_2] if split_units else []
    )
    grad_memory, own_near = totals[0], nears[0]
    mark(grad_memory)

    back = ffn_backward(enc_cot, tie(grad_memory), ffn[2], encoder_ffn_in, encoder_ffn_out)
    mark(back[3])
    unit_4a = project_weight(tie(ffn[1]), back[2])
    mark(unit_4a)
    unit_4b = project_weight(tie(ffn[3]), back[1])
    mark(unit_4b)
    totals, _, shares, wholes, _, _ = sums(
        4, parts=[tie(back[3])], scatter=[unit_4a] if split_units else [], gather=shares
    )
    dn = totals[0]
    mark(dn)
    half_4b, half_5 = [Wire(chain, first_swap) for _ in range(2)]
    half_4b.send(first_half(unit_4b))
    own_far, own_beside, own_relay = [
        Wire(chain, swap) for swap in (chip_swap, core_swap, core_swap)
    ]
    own_far.send(own_near)
    own_beside.send(own_near)

    eb, (enc_table, enc_gain, enc_part) = attention_back(
        core, enc_lens, enc_lens, back[0], ffn[0], (tie(dn),), row(encoder_ffn_gain),
        encoder_output, enc[1:6], encoder_query, encoder_key, encoder_value, enc_bias, x0, False,
        "encoder_back",
    )
    mark(enc_part)
    own_beside.wait()
    own_far.wait()
    own_relay.send(own_far.value)
    half_4b.wait()
    dec_ffn = tie(dec_ffn)
    mark(dec_ffn)
    unit_5 = attention_weights((*eb[:2], tie(eb[2]), *eb[3:]), enc[4], enc[0], enc[0])
    mark(unit_5)
    half_5.send(first_half(unit_5))
    own_relay.wait()

    own_pieces = (own_near, own_far.value, own_beside.value, own_relay.value)
    sb, (dec_table, dec_gain, dec_part) = attention_back(
        core, dec_lens, dec_lens, tie(cb[0]), cross[0], own_pieces, row(cross_gain),
        decoder_output, dec[1:6], decoder_query, decoder_key, decoder_value, dec_bias, y0, True,
        "decoder_back",
    )
    mark(dec_part)
    half_5.wait()
    unit_3 = attention_weights(sb, dec[4], dec[0], dec[0])
    tables = []
    for table in (enc_table, dec_table):
        flat = table.reshape(1, -1)
        tables.append(jnp.pad(flat, ((0, 0), (0, width - flat.shape[1]))))
    blank = jnp.zeros((1, width), F32)
    small = jnp.concatenate([enc_gain, dec_gain, eb[5], sb[5], cb[5], *tables, blank], axis=0)
    units = [unit_3, unit_4b, unit_5] if split_units else []
    halves = [half_4b.value, half_5.value] if split_units else []
    totals, _, _, gathered, units, smalls = sums(
        5, parts=[enc_part, dec_part, both[5]], gather=shares, units=units, halves=halves,
        small=small, shared=2
    )
    small = smalls[0]
    if split_units:
        unit_2, unit_4a = wholes[0], gathered[0]
        unit_3, unit_4b, unit_5 = units
    else:
        unit_2, unit_4a, unit_3, unit_4b, unit_5 = lax.psum(
            (unit_2, unit_4a, unit_3, unit_4b, unit_5), "dp"
        )
    enc_grad, dec_grad, result = closing(
        x0, eb[0], row(encoder_attn_gain), totals[0], y0, sb[0], row(decoder_attn_gain), totals[1],
        both[0], totals[2],
    )

    def matrices(stack):
        count = stack.shape[0] // 4
        pieces = [stack[i * count : (i + 1) * count] for i in range(4)]
        return [jnp.transpose(piece) for piece in pieces[:3]] + pieces[3:]

    shape = encoder_bias.shape
    count = shape[0] * shape[1]
    return (
        cross[2][None],
        result[None],
        enc_grad[None],
        dec_grad[None],
        small[0],
        *matrices(unit_5),
        small[5, :count].reshape(shape),
        small[2],
        unit_4a,
        unit_4b,
        small[1],
        *matrices(unit_3),
        small[6, :count].reshape(shape),
        small[3],
        *matrices(unit_2),
        small[4],
        dec_ffn[:width],
        dec_ffn[width:],
    )


def solution(mesh):
    return jax.shard_map(
        body,
        mesh=mesh,
        in_specs=(
            P("dp", None, None),
            P("dp", None, None),
            P("dp", None),
            P("dp", None),
            P(),
            P(),
            P(),
            P(None, "mp"),
            P(None, "mp"),
            P(None, "mp"),
            P("mp", None),
            P(None, "mp"),
            P(),
            P(None, "mp"),
            P("mp", None),
            P(),
            P(None, "mp"),
            P(None, "mp"),
            P(None, "mp"),
            P("mp", None),
            P(None, "mp"),
            P(),
            P(None, "mp"),
            P(None, "mp"),
            P(None, "mp"),
            P("mp", None),
            P(),
            P(None, "mp"),
            P("mp", None),
            P("dp", None, None),
            P("dp", None, None),
        ),
        out_specs=(
            P("dp", None, None),
            P("dp", None, None),
            P("dp", None, None),
            P("dp", None, None),
            P(),
            P(None, "mp"),
            P(None, "mp"),
            P(None, "mp"),
            P("mp", None),
            P(None, "mp"),
            P(),
            P(None, "mp"),
            P("mp", None),
            P(),
            P(None, "mp"),
            P(None, "mp"),
            P(None, "mp"),
            P("mp", None),
            P(None, "mp"),
            P(),
            P(None, "mp"),
            P(None, "mp"),
            P(None, "mp"),
            P("mp", None),
            P(),
            P(None, "mp"),
            P("mp", None),
        ),
        check_vma=False,
    )
```

time: 1600 us -> 726 us (0.45)
  waiting for transfers between devices: 720 us -> 32.2 us
  Pallas kernels: 0 us -> 606 us
  local copies, waits for them, and re-layouts: 501 us -> 39.7 us
  matrix products: 171 us -> 10.3 us
  other arithmetic: 149 us -> 4.99 us
  blocking collectives: 37.7 us -> 0 us
    pallas_call x0 -> x18, Pallas kernels: none -> 606 us  [the longest x5 405 us: sums(): pl.pallas_call(kernel, in_specs=[whole(a.shape) for a in inputs], out_spe...]
    unnamed x402 -> x82, local copies, waits for them, and re-layouts: 337 us -> 11 us
    reduce_scatter x10 -> x0, waiting for transfers between devices: 313 us -> none  [the longest x5 185 us: reduce_branch(): lax.psum_scatter(term(jnp.int32(0), lax.axis_size('mp') * count), 'mp', s...]
    psum x1, waiting for transfers between devices: 212 us -> 0.02 us  [body(): dec_ffn = lax.psum(dec_ffn, 'dp')]
    all_gather x10 -> x1, waiting for transfers between devices: 195 us -> 0.02 us  [body(): wide.y.value = lax.all_gather(tie(slices.value), 'dp', axis=0, tiled=True)]
    dot_general x88 -> x4, matrix products: 171 us -> 10.3 us  [project_weight(): lax.dot_general(left, right, (((0,), (0,)), ((), ())), preferred_element_...]
    reshape x4 -> x2, local copies, waits for them, and re-layouts: 82.3 us -> 0.72 us  [body(): flat = table.reshape(1, -1)]
    reduce_sum x24 -> x0, other arithmetic: 59.9 us -> none  [the longest x4 22.5 us: bias_rows(): tiled = jnp.tile(reverse, (1, count))[:, :count * (length - 1)]]
  transfers between devices with their start and end apart: 21 -> 22, of which waited for: 16 -> 9; matrix products, arithmetic and copies ran while one was open for 35% -> 4% of each run, Pallas kernels for 0% -> 54%
where the time goes in v1:
time: 726 us; the launch traced here: 720 us
  Pallas kernels  606 us (83%)
  local copies, waits for them, and re-layouts  39.7 us (5%)
  waiting for transfers between devices  32.2 us (4%)
  between operations  14.8 us (2%)
  starting transfers between devices  12.4 us (2%)
  matrix products  10.3 us (1%)
    pallas_call x5, Pallas kernels, sums(): pl.pallas_call(kernel, in_specs=[whole(a.shape) for a in inputs], out_spe...  405 us
    pallas_call x13, Pallas kernels, call(): pl.pallas_call(kernel, grid=grid, in_specs=[spec for _, spec in inputs],...  201 us
    ppermute x6, waiting for transfers between devices, chip_swap(): return lax.ppermute(value, 'mp', CHIP_SWAP)  26.8 us
  transfers between devices with their start and end apart: 22, of which 9 were waited for; matrix products, arithmetic and copies ran while one was open for 4% of the time, Pallas kernels for 54%

profile of v1, /device:TPU:0, one launch (start us, length us, event | category | flops | bytes accessed | tf_op | source)
XLA Modules:
  0.0 720.3 jit_solution(11376176345613711985)
XLA Ops:
  8.3 3.0 collective-permute-start.1
  12.3 1.3 broadcast_in_dim.42.refs_2_.egain_ref
  13.6 1.4 copy.66.refs_7_.refs_17_
  15.0 1.4 pad_add_fusion
  16.4 16.6 %encoder_attention.1 = (bf16[1024,768]{1,0:T(8,128)(2,1)}, bf16[1024,192]{1,0:T(8,128)(2,1)}, bf16[1024,192]{1,0:T(8,128)(2,1)}, bf16[1024,192]{1,0:T(8,128)(2,1...) custom-call(s32[1,8]{1,0:T(1,128)} %refs_2_.6, bf16[1024,768]{1,0:T(8,128)(2,1)} %bitcast.59, ...), custom_call_target="tpu_custom_call" | custom-call | flops 1248 | bytes 6 | tf_op jit(solution)/shard_map/encoder_attention/pallas_call | solution.py:534
  34.2 1.9 collective-permute-start.2
  38.1 12.6 %decoder_attention.1 = (bf16[1024,768]{1,0:T(8,128)(2,1)}, bf16[1024,192]{1,0:T(8,128)(2,1)}, bf16[1024,192]{1,0:T(8,128)(2,1)}, bf16[1024,192]{1,0:T(8,128)(2,1...) custom-call(s32[1,8]{1,0:T(1,128)} %refs_2_.7, bf16[1024,768]{1,0:T(8,128)(2,1)} %bitcast.55, ...), custom_call_target="tpu_custom_call" | custom-call | flops 1248 | bytes 6 | tf_op jit(solution)/shard_map/decoder_attention/pallas_call | solution.py:534
  50.7 2.9 collective-permute-done.2.refs_3_
  53.6 1.6 collective-permute-start.7
  58.4 11.9 %ffn_forward.1 = (f32[1024,768]{1,0:T(8,128)}, bf16[1024,768]{1,0:T(8,128)(2,1)}, f32[1024,768]{1,0:T(8,128)}, bf16[1024,768]{1,0:T(8,128)(2,1)}, f32[1024,768]{1,0:T(8,128)}) custom-call(s32[1]{0:T(128)} %bitcast.refs_0_, bf16[1024,768]{1,0:T(8,128)(2,1)} %bitcast.60, f32[192,1024]{1,0:T(8,128)} %get-tuple-element.171.refs_2_, ...), custom_call_target="tpu_custom_call" | custom-call | flops 3456 | bytes 21 | tf_op jit(solution)/shard_map/ffn_forward/pallas_call | solution.py:534
  70.4 3.4 collective-permute-done.7.refs_5_
  74.7 43.6 %sums.5.refs_13_ = f32[1024,768]{1,0:T(8,128)} custom-call(f32[1024,768]{1,0:T(8,128)} %get-tuple-element.186.refs_0_), custom_call_target="tpu_custom_call" | custom-call | flops 1 | bytes 1 | tf_op jit(solution)/shard_map/sums/pallas_call | solution.py:1057
  122.1 1.4 collective-permute-done.11.refs_6_
  123.7 1.2 fusion.7
  126.1 20.9 %cross_forward.1 = (f32[1024,768]{1,0:T(8,128)}, bf16[1024,768]{1,0:T(8,128)(2,1)}, bf16[1024,768]{1,0:T(8,128)(2,1)}, bf16[1024,192]{1,0:T(8,128)(2,1)}, bf16[1...) custom-call(s32[1]{0:T(128)} %bitcast.refs_0_, ...), custom_call_target="tpu_custom_call" | custom-call | flops 2400 | bytes 21 | tf_op jit(solution)/shard_map/cross_forward/pallas_call | solution.py:534
  147.0 1.7 collective-permute-start.12
  148.7 18.4 %collective-permute-done.12.refs_3_ = f32[192,1024]{1,0:T(8,128)S(1)} collective-permute-done((f32[192,1024]{1,0:T(8,128)}, f32[192,1024]{1,0:T(8,128)S(1)}, u32[]{:S(2)}, u32[]{:S(2)}) %collective-permute-start.12) | collective-permute-done | bytes 786464 | tf_op jit(solution)/shard_map/ppermute | solution.py:1103
  167.7 1.6 collective-permute-done.13.refs_5_
  170.3 15.1 %ffn_both.1 = (f32[1024,768]{1,0:T(8,128)}, bf16[1024,768]{1,0:T(8,128)(2,1)}, bf16[1024,768]{1,0:T(8,128)(2,1)}, bf16[1024,768]{1,0:T(8,128)(2,1)}, f32[1024,768]{1,0:T(8,128)}, /*index=5*/f32[1024,768]{1,0:T(8,128)}) custom-call(s32[1]{0:T(128)} %bitcast.refs_0_, f32[1024,768]{1,0:T(8,128)} %get-tuple-element.205.refs_1_.refs_4_, ...), custom_call_target="tpu_custom_call" | custom-call | flops 5760 | bytes 25 | tf_op jit(solution)/shard_map/ffn_both/pallas_call | solution.py:534
  185.4 3.0 fusion
  188.4 1.5 fusion.10
  189.9 2.5 pad_maximum_fusion
  192.4 43.5 %sums.6.refs_5_ = f32[1024,768]{1,0:T(8,128)} custom-call(f32[1024,768]{1,0:T(8,128)} %get-tuple-element.212.refs_0_), custom_call_target="tpu_custom_call" | custom-call | flops 1 | bytes 1 | tf_op jit(solution)/shard_map/sums/pallas_call | solution.py:1057
  236.0 25.7 %cross_back.1 = (f32[1024,768]{1,0:T(8,128)}, bf16[1024,768]{1,0:T(8,128)(2,1)}, bf16[1024,192]{1,0:T(8,128)(2,1)}, bf16[1024,192]{1,0:T(8,128)(2,1)}, bf16[1024...) custom-call(s32[1]{0:T(128)S(6)} %rem.32.refs_0_, s32[1,8]{1,0:T(1,128)} %refs_2_.7, ...), custom_call_target="tpu_custom_call" | custom-call | flops 2112 | bytes 21 | tf_op jit(solution)/shard_map/cross_back/pallas_call | solution.py:534
  261.7 5.8 attention_weights.3.refs_2_
  267.5 61.0 %sums.7 = (f32[1024,768]{1,0:T(8,128)}, f32[512,768]{1,0:T(8,128)}, f32[96,768]{1,0:T(8,128)}) custom-call(f32[1024,768]{1,0:T(8,128)} %get-tuple-element.227.refs_0_, f32[1024,768]{1,0:T(8,128)} %get-tuple-element.221.refs_1_, f32[768,768]{1,0:T(8,128)} %attention_weights.3.refs_2_), custom_call_target="tpu_custom_call" | custom-call | flops 1 | bytes 1 | tf_op jit(solution)/shard_map/sums/pallas_call | solution.py:1057
  328.6 9.7 %ffn_backward.1 = (f32[1024,768]{1,0:T(8,128)}, bf16[1024,768]{1,0:T(8,128)(2,1)}, bf16[1024,768]{1,0:T(8,128)(2,1)}, f32[1024,768]{1,0:T(8,128)}) custom-call(bf16[1024,768]{1,0:T(8,128)(2,1)} %bitcast.67, f32[1024,768]{1,0:T(8,128)} %get-tuple-element.228.sum_ref, f32[1024,768]{1,0:T(8,128)} %get-tuple-element.229.hid_ref, bf16[768,768]{1,0:T(8,128)(2,1)} %wi_ref.1, ...), custom_call_target="tpu_custom_call" | custom-call | flops 2304 | bytes 18 | tf_op jit(solution)/shard_map/ffn_backward/pallas_call | solution.py:534
  338.3 4.4 fusion.11.refs_1_
  342.7 1.4 fusion.12.refs_5_
  344.2 87.8 %sums.8 = (f32[1024,768]{1,0:T(8,128)}, f32[96,768]{1,0:T(8,128)}, f32[768,768]{1,0:T(8,128)}) custom-call(f32[1024,768]{1,0:T(8,128)} %get-tuple-element.238.refs_0_, f32[768,768]{1,0:T(8,128)} %fusion.11.refs_1_, f32[96,768]{1,0:T(8,128)} %get-tuple-element.239.refs_2_), custom_call_target="tpu_custom_call" | custom-call | flops 1 | bytes 1 | tf_op jit(solution)/shard_map/sums/pallas_call | solution.py:1057
  432.0 1.2 collective-permute-start.15
  433.2 1.1 constant_dynamic-slice_fusion.1
  434.9 32.1 %encoder_back.1 = (f32[1024,768]{1,0:T(8,128)}, bf16[1024,768]{1,0:T(8,128)(2,1)}, bf16[1024,192]{1,0:T(8,128)(2,1)}, bf16[1024,192]{1,0:T(8,128)(2,1)}, bf16[10...) custom-call(s32[1]{0:T(128)S(6)} %rem.32.refs_0_, ...), custom_call_target="tpu_custom_call" | custom-call | flops 2112 | bytes 21 | tf_op jit(solution)/shard_map/encoder_back/pallas_call | solution.py:534
  467.1 2.1 collective-permute-done.15.refs_6_
  469.2 6.2 attention_weights.4.refs_6_
  475.4 2.6 constant_dynamic-slice_fusion
  479.3 1.4 fusion.3
  480.7 26.9 %decoder_back.1 = (f32[1024,768]{1,0:T(8,128)}, bf16[1024,768]{1,0:T(8,128)(2,1)}, bf16[1024,192]{1,0:T(8,128)(2,1)}, bf16[1024,192]{1,0:T(8,128)(2,1)}, bf16[10...) custom-call(s32[1]{0:T(128)S(6)} %rem.32.refs_0_, ...), custom_call_target="tpu_custom_call" | custom-call | flops 2112 | bytes 24 | tf_op jit(solution)/shard_map/decoder_back/pallas_call | solution.py:534
  507.7 5.9 attention_weights.5.refs_4_
  514.5 4.9 fusion.2
  520.4 169.1 %sums.9 = (f32[1024,768]{1,0:T(8,128)}, f32[1024,768]{1,0:T(8,128)}, f32[1024,768]{1,0:T(8,128)}, f32[768,768]{1,0:T(8,128)}, f32[768,768]{1,0:T(8,128)}, /*inde...) custom-call(f32[1024,768]{1,0:T(8,128)} %get-tuple-element.248.refs_0_, ...), custom_call_target="tpu_custom_call" | custom-call | flops 1 | bytes 1 | tf_op jit(solution)/shard_map/sums/pallas_call | solution.py:1057
  690.2 1.6 slice_reduce_fusion
  693.3 3.2 fusion.5
  696.5 1.4 fusion.4
  698.0 11.4 %closing.1 = (f32[1024,768]{1,0:T(8,128)}, f32[1024,768]{1,0:T(8,128)}, bf16[1024,768]{1,0:T(8,128)(2,1)}) custom-call(bf16[1024,768]{1,0:T(8,128)(2,1)} %bitcast.62, f32[1024,768]{1,0:T(8,128)} %get-tuple-element.247.eb_ref, f32[1,768]{1,0:T(1,128)} %broadcast_in_dim.42.refs_2_.egain_ref, f32[1024,768]{1,0:T(8,128)} %get-tuple-element.288.z_ref, ...), custom_call_target="tpu_custom_call" | custom-call | flops 15 | bytes 28 | tf_op jit(solution)/shard_map/closing/pallas_call | solution.py:534
  709.4 1.4 copy.79
  710.8 1.1 copy-done.4
  711.9 1.4 copy.80
  (134 shorter events, 22.1 us)
Async XLA Ops:
  7.2 111.1 %all-gather.2.cloned.1.call-start = ((), (), s32[]{:S(2)}) async-start(), calls=%async_computation | async-start | bytes 1327104 | tf_op jit(solution)/shard_map/all_gather | solution.py:1248
  8.3 47.0 %copy-start.2 = (f32[192,768]{1,0:T(8,128)}, f32[192,768]{1,0:T(8,128)S(1)}, u32[]{:S(2)}) copy-start(f32[192,768]{1,0:T(8,128)S(1)} %convert_element_type.13.refs_6_) | copy-start | bytes 1769476
  8.3 27.9 %copy-start.23 = (f32[768]{0:T(1024)S(1)}, f32[768]{0:T(1024)}, u32[]{:S(2)}) copy-start(f32[768]{0:T(1024)} %param.46) | copy-start | bytes 9220
  8.3 28.5 %copy-start.32 = (f32[32,3]{0,1:T(4,128)S(1)}, f32[32,3]{0,1:T(4,128)}, u32[]{:S(2)}) copy-start(f32[32,3]{0,1:T(4,128)} %param.51) | copy-start | bytes 1156
  8.3 29.2 %copy-start.22 = (s32[1024]{0:T(1024)S(1)}, s32[1024]{0:T(1024)}, u32[]{:S(2)}) copy-start(s32[1024]{0:T(1024)} %param.36) | copy-start | bytes 12292
  8.3 24.7 %collective-permute-start.1 = (f32[192,768]{1,0:T(8,128)S(1)}, f32[192,768]{1,0:T(8,128)}, u32[]{:S(2)}, u32[]{:S(2)}) collective-permute-start(f32[192,768]{1,0:T(8,128)S(1)} %convert_element_type.13.refs_6_), channel_id=1, source_target_pairs={{0,2},{2,0},{1,3},{3,1},{4,6},{6,4},{5,7},{7,5},{8,10},{10,8},{9,1... | collective-permute-start | bytes 1769480 | tf_op jit(solution)/shard_map/ppermute | solution.py:1103
  12.1 20.9 %collective-permute-start = (f32[24,1536]{1,0:T(8,128)S(1)}, f32[24,1536]{1,0:T(8,128)S(1)}, u32[]{:S(2)}, u32[]{:S(2)}) collective-permute-start(f32[24,1536]{1,0:T(8,128)S(1)} %maximum_convert_fusion.1), channel_id=1, source_target_pairs={{0,2},{2,0},{1,3},{3,1},{4,6},{6,4},{5,7},{7,5},{8,10},{10,8},{9,1... | collective-permute-start | bytes 442376 | tf_op jit(solution)/shard_map/ppermute | solution.py:1103
  33.0 22.8 %copy-start.24 = (f32[768]{0:T(1024)S(1)}, f32[768]{0:T(1024)}, u32[]{:S(2)}) copy-start(f32[768]{0:T(1024)} %param.43) | copy-start | bytes 9220
  33.0 23.3 %copy-start.7 = (bf16[192,768]{1,0:T(8,128)(2,1)S(1)}, bf16[192,768]{1,0:T(8,128)(2,1)}, u32[]{:S(2)}) copy-start(bf16[192,768]{1,0:T(8,128)(2,1)} %refs_7_.4) | copy-start | bytes 884740
  33.0 23.3 %copy-start.8 = (bf16[192,768]{1,0:T(8,128)(2,1)S(1)}, bf16[192,768]{1,0:T(8,128)(2,1)}, u32[]{:S(2)}) copy-start(bf16[192,768]{1,0:T(8,128)(2,1)} %refs_10_.1) | copy-start | bytes 884740
  33.7 435.5 %all-reduce.5.cloned.1.call-start = ((), (), s32[]{:S(2)}) async-start(), calls=%async_computation.1 | async-start | bytes 9437184 | tf_op jit(solution)/shard_map/psum | solution.py:1308
  34.2 19.4 %collective-permute-start.2 = (f32[192,1024]{1,0:T(8,128)}, f32[192,1024]{1,0:T(8,128)}, u32[]{:S(2)}, u32[]{:S(2)}) collective-permute-start(f32[192,1024]{1,0:T(8,128)} %get-tuple-element.171.refs_2_), channel_id=1, source_target_pairs={{0,2},{2,0},{1,3},{3,1},{4,6},{6,4},{5,7},{7,5},{8,10},{10,8},{9,1... | collective-permute-start | bytes 2359304 | tf_op jit(solution)/shard_map/ppermute | solution.py:1103
  38.1 18.4 %collective-permute-start.6 = (f32[192,1024]{1,0:T(8,128)}, f32[192,1024]{1,0:T(8,128)}, u32[]{:S(2)}, u32[]{:S(2)}) collective-permute-start(f32[192,1024]{1,0:T(8,128)} %get-tuple-element.171.refs_2_), channel_id=1, source_target_pairs={{0,1},{1,0},{2,3},{3,2},{4,5},{5,4},{6,7},{7,6},{8,9},{9,8},{10,11... | collective-permute-start | bytes 2359304 | tf_op jit(solution)/shard_map/ppermute | solution.py:1099
  53.6 4.8 collective-permute-start.3
  53.6 20.2 %collective-permute-start.7 = (f32[192,1024]{1,0:T(8,128)}, f32[192,1024]{1,0:T(8,128)S(1)}, u32[]{:S(2)}, u32[]{:S(2)}) collective-permute-start(f32[192,1024]{1,0:T(8,128)} %get-tuple-element.190.refs_4_), channel_id=1, source_target_pairs={{0,2},{2,0},{1,3},{3,1},{4,6},{6,4},{5,7},{7,5},{8,10},{10,8},{9,1... | collective-permute-start | bytes 2359304 | tf_op jit(solution)/shard_map/ppermute | solution.py:1103
  55.2 2.1 collective-permute-start.5
  55.5 3.0 collective-permute-start.4
  74.7 44.1 %copy-start.12 = (f32[192,1024]{1,0:T(8,128)S(1)}, f32[192,1024]{1,0:T(8,128)}, u32[]{:S(2)}) copy-start(f32[192,1024]{1,0:T(8,128)} %get-tuple-element.190.refs_4_) | copy-start | bytes 2359300
  74.7 44.6 %copy-start.25 = (f32[768]{0:T(1024)S(1)}, f32[768]{0:T(1024)}, u32[]{:S(2)}) copy-start(f32[768]{0:T(1024)} %param.52) | copy-start | bytes 9220
  74.7 49.0 %collective-permute-start.9 = (f32[192,1536]{1,0:T(8,128)S(1)}, f32[192,1536]{1,0:T(8,128)S(1)}, u32[]{:S(2)}, u32[]{:S(2)}) collective-permute-start(f32[192,1536]{1,0:T(8,128)S(1)} %maximum_convert_fusion), channel_id=1, source_target_pairs={{0,1},{1,0},{2,3},{3,2},{4,5},{5,4},{6,7},{7,6},{8,9},{9,8},{10,11... | collective-permute-start | bytes 3538952 | tf_op jit(solution)/shard_map/ppermute | solution.py:1099
  118.3 6.6 collective-permute-start.8
  118.8 4.7 collective-permute-start.11
  118.9 4.8 collective-permute-start.10
  126.0 41.0 %copy-start.26 = (f32[768]{0:T(1024)S(1)}, f32[768]{0:T(1024)}, u32[]{:S(2)}) copy-start(f32[768]{0:T(1024)} %param.57) | copy-start | bytes 9220
  147.0 20.1 %collective-permute-start.12 = (f32[192,1024]{1,0:T(8,128)}, f32[192,1024]{1,0:T(8,128)S(1)}, u32[]{:S(2)}, u32[]{:S(2)}) collective-permute-start(f32[192,1024]{1,0:T(8,128)} %get-tuple-element.200.refs_2_), channel_id=1, source_target_pairs={{0,2},{2,0},{1,3},{3,1},{4,6},{6,4},{5,7},{7,5},{8,10},{10,8},{9,1... | collective-permute-start | bytes 2359304 | tf_op jit(solution)/shard_map/ppermute | solution.py:1103
  148.6 19.1 %collective-permute-start.14 = (f32[192,1024]{1,0:T(8,128)}, f32[192,1024]{1,0:T(8,128)S(1)}, u32[]{:S(2)}, u32[]{:S(2)}) collective-permute-start(f32[192,1024]{1,0:T(8,128)} %get-tuple-element.200.refs_2_), channel_id=1, source_target_pairs={{0,1},{1,0},{2,3},{3,2},{4,5},{5,4},{6,7},{7,6},{8,9},{9,8},{10,11... | collective-permute-start | bytes 2359304 | tf_op jit(solution)/shard_map/ppermute | solution.py:1099
  167.1 2.3 collective-permute-start.13
  170.3 15.1 %copy-start = (bf16[1,1024,768]{2,1,0:T(8,128)(2,1)S(1)}, bf16[1,1024,768]{2,1,0:T(8,128)(2,1)}, u32[]{:S(2)}) copy-start(bf16[1,1024,768]{2,1,0:T(8,128)(2,1)} %param.61) | copy-start | bytes 4718596
  328.6 9.7 %copy-start.34 = (bf16[1024,768]{1,0:T(8,128)(2,1)S(1)}, bf16[1024,768]{1,0:T(8,128)(2,1)}, u32[]{:S(2)}) copy-start(bf16[1024,768]{1,0:T(8,128)(2,1)} %get-tuple-element.234) | copy-start | bytes 4718596
  338.3 4.4 copy-start.33
  338.3 4.4 copy-start.37
  344.2 89.0 %copy-start.1 = (f32[768,768]{1,0:T(8,128)}, f32[768,768]{1,0:T(8,128)S(1)}, u32[]{:S(2)}) copy-start(f32[768,768]{1,0:T(8,128)S(1)} %fusion.12.refs_5_) | copy-start | bytes 7077892
  432.0 35.1 %collective-permute-start.16 = (f32[512,768]{1,0:T(8,128)}, f32[512,768]{1,0:T(8,128)}, u32[]{:S(2)}, u32[]{:S(2)}) collective-permute-start(f32[512,768]{1,0:T(8,128)} %get-tuple-element.251.refs_5_), channel_id=1, source_target_pairs={{0,1},{1,0},{2,3},{3,2},{4,5},{5,4},{6,7},{7,6},{8,9},{9,8},{10,11... | collective-permute-start | bytes 4718600 | tf_op jit(solution)/shard_map/ppermute | solution.py:1099
  432.0 37.1 %collective-permute-start.15 = (f32[512,768]{1,0:T(8,128)}, f32[512,768]{1,0:T(8,128)}, u32[]{:S(2)}, u32[]{:S(2)}) collective-permute-start(f32[512,768]{1,0:T(8,128)} %get-tuple-element.251.refs_5_), channel_id=1, source_target_pairs={{0,2},{2,0},{1,3},{3,1},{4,6},{6,4},{5,7},{7,5},{8,10},{10,8},{9,1... | collective-permute-start | bytes 4718600 | tf_op jit(solution)/shard_map/ppermute | solution.py:1103
  434.3 34.8 %collective-permute-start.18 = (f32[384,768]{1,0:T(8,128)}, f32[384,768]{1,0:T(8,128)S(1)}, u32[]{:S(2)}, u32[]{:S(2)}) collective-permute-start(f32[384,768]{1,0:T(8,128)} %bitcast.18), channel_id=1, source_target_pairs={{0,4},{4,0},{8,12},{12,8},{16,20},{20,16},{24,28},{28,24},{1,5},{5... | collective-permute-start | bytes 3538952 | tf_op jit(solution)/shard_map/ppermute | solution.py:1087
  469.2 11.6 %collective-permute-start.17 = (f32[512,768]{1,0:T(8,128)}, f32[512,768]{1,0:T(8,128)}, u32[]{:S(2)}, u32[]{:S(2)}) collective-permute-start(f32[512,768]{1,0:T(8,128)} %collective-permute-done.15.refs_6_), channel_id=1, source_target_pairs={{0,1},{1,0},{2,3},{3,2},{4,5},{5,4},{6,7},{7,6},{8,9},{9,8},{10,11... | collective-permute-start | bytes 4718600 | tf_op jit(solution)/shard_map/ppermute | solution.py:1099
  469.2 6.3 copy-start.9
  469.2 8.8 %copy-start.20 = (f32[32,3]{1,0:T(8,128)S(1)}, f32[32,3]{1,0:T(8,128)}, u32[]{:S(2)}) copy-start(f32[32,3]{1,0:T(8,128)} %get-tuple-element.284) | copy-start | bytes 1156
  475.4 3.9 copy-start.3
  478.0 41.4 %collective-permute-start.19 = (f32[384,768]{1,0:T(8,128)}, f32[384,768]{1,0:T(8,128)S(1)}, u32[]{:S(2)}, u32[]{:S(2)}) collective-permute-start(f32[384,768]{1,0:T(8,128)} %bitcast.20), channel_id=1, source_target_pairs={{0,4},{4,0},{8,12},{12,8},{16,20},{20,16},{24,28},{28,24},{1,5},{5... | collective-permute-start | bytes 3538952 | tf_op jit(solution)/shard_map/ppermute | solution.py:1087
  507.7 6.0 copy-start.21
  507.7 6.1 copy-start.27
  507.7 6.1 copy-start.28
  507.7 6.1 copy-start.29
  507.7 6.1 copy-start.30
  507.7 6.1 copy-start.31
  693.3 3.2 copy-start.6
  698.0 11.4 %copy-start.5 = (f32[768,768]{1,0:T(8,128)S(1)}, f32[768,768]{1,0:T(8,128)}, u32[]{:S(2)}) copy-start(f32[768,768]{1,0:T(8,128)} %get-tuple-element.424) | copy-start | bytes 7077892
  (12 other events, 23.6 us)
Sparse Core Ops, SparseCore 0:
  33.8 41.2 all-gather.1
  192.5 197.2 all-reduce.4

commit v2 on v1

--- a/solution.py
+++ b/solution.py
@@ -13,7 +13,7 @@
 HIGHEST = lax.Precision.HIGHEST
 TILE = 128
 BQ = 256
-KC = 128
+KC = 256
 SPEEDUP = 1 << 20
 VMEM_BYTES = 60 * 1024 * 1024
 
@@ -588,16 +588,17 @@
     return [pltpu.VMEM((4, width, model), BF16), pltpu.VMEM((4, width, rows), F32)]
 
 
-def piece_inputs(pieces, weights):
+def piece_inputs(pieces, weights, model, half):
     width = pieces[0].shape[0]
-    return [(a, transposed_spec(width)) for a in pieces] + [full(a) for a in weights]
+    spec = pl.BlockSpec((width, model), lambda *_: (0, half), pipeline_mode=pl.Buffered(1))
+    return [(a, transposed_spec(width)) for a in pieces] + [(a, spec) for a in weights]
 
 
 def cross_forward(me, ql, kl, y0, pieces, weights, x1, enc_sum, gain, wq, wk, wv):
     seq, model = y0.shape
     width = wq.shape[0]
     inputs = [(me, SMEM_SPEC), (ql, SMEM_SPEC), (kl, SMEM_SPEC), (y0, rows_spec(model))]
-    inputs += piece_inputs(pieces, weights)
+    inputs += piece_inputs(pieces, weights, model, 0)
     inputs += [full(a) for a in (x1, enc_sum, gain, wq, wk, wv)]
     outputs = [
         ((seq, model), F32, rows_spec(model)),
@@ -625,7 +626,7 @@
 def ffn_forward(me, x, pieces, weights, gain, wi, wo):
     seq, model = x.shape
     units = wi.shape[1]
-    inputs = [(me, SMEM_SPEC), (x, rows_spec(model))] + piece_inputs(pieces, weights)
+    inputs = [(me, SMEM_SPEC), (x, rows_spec(model))] + piece_inputs(pieces, weights, model, 0)
     inputs += [full(a) for a in (gain, wi, wo)]
     outputs = row_outputs(seq, (model, F32), (model, BF16), (units, F32), (units, BF16), (model, F32))
     return call(
@@ -637,7 +638,7 @@
 def ffn_both(me, y, pieces, weights, gain, wi, wo, cot):
     seq, model = y.shape
     units = wi.shape[1]
-    inputs = [(me, SMEM_SPEC), (y, rows_spec(model))] + piece_inputs(pieces, weights)
+    inputs = [(me, SMEM_SPEC), (y, rows_spec(model))] + piece_inputs(pieces, weights, model, 1)
     inputs += [full(a) for a in (gain, wi, wo)] + [(cot, rows_spec(model))]
     outputs = row_outputs(
         seq, (model, F32), (model, BF16), (units, BF16), (units, BF16), (model, F32), (model, F32)
@@ -1282,9 +1283,8 @@
     wide.ws()
     wide.wr()
 
-    split = lambda i: tuple(value[:, i * width : (i + 1) * width] for value in wide.pieces())
     cross, out = cross_forward(
-        me, dec_lens, enc_lens, tie(y0), d.pieces(), split(0), ffn[0], enc_sum, row(cross_gain),
+        me, dec_lens, enc_lens, tie(y0), d.pieces(), wide.pieces(), ffn[0], enc_sum, row(cross_gain),
         cross_query, cross_key, cross_value,
     )
     mark(out)
@@ -1297,15 +1297,10 @@
     x.wr()
 
     both = ffn_both(
-        me, tie(cross[0]), x.pieces(), split(1), row(decoder_ffn_gain), decoder_ffn_in,
+        me, tie(cross[0]), x.pieces(), wide.pieces(), row(decoder_ffn_gain), decoder_ffn_in,
         decoder_ffn_out, dec_cot,
     )
     mark(both[4])
-    dec_ffn = jnp.concatenate(
-        [project_weight(tie(both[1]), both[3]), project_weight(both[2], dec_cot)], axis=0
-    )
-    mark(dec_ffn)
-    dec_ffn = lax.psum(dec_ffn, "dp")
     dn = sums(2, parts=[tie(both[4])])[0][0]
     mark(dn)
 
@@ -1315,12 +1310,15 @@
         "cross_back",
     )
     mark(own_part)
+    unit_1a = project_weight(tie(both[1]), both[3])
+    unit_1b = project_weight(both[2], dec_cot)
     unit_2 = attention_weights((*cb[:2], tie(cb[2]), *cb[3:]), cross[6], cross[1], cross[2])
     mark(unit_2)
+    unit_1a = tie(unit_1a)
+    mark(unit_1a)
+    unit_1a, unit_1b, unit_2 = lax.psum((unit_1a, unit_1b, unit_2), "dp")
     split_units = shares_fit(width)
-    totals, nears, shares, _, _, _ = sums(
-        3, parts=[tie(memory_part)], near=[own_part], scatter=[unit_2] if split_units else []
-    )
+    totals, nears, _, _, _, _ = sums(3, parts=[tie(memory_part)], near=[own_part])
     grad_memory, own_near = totals[0], nears[0]
     mark(grad_memory)
 
@@ -1330,8 +1328,8 @@
     mark(unit_4a)
     unit_4b = project_weight(tie(ffn[3]), back[1])
     mark(unit_4b)
-    totals, _, shares, wholes, _, _ = sums(
-        4, parts=[tie(back[3])], scatter=[unit_4a] if split_units else [], gather=shares
+    totals, _, shares, _, _, _ = sums(
+        4, parts=[tie(back[3])], scatter=[unit_4a] if split_units else []
     )
     dn = totals[0]
     mark(dn)
@@ -1353,8 +1351,6 @@
     own_far.wait()
     own_relay.send(own_far.value)
     half_4b.wait()
-    dec_ffn = tie(dec_ffn)
-    mark(dec_ffn)
     unit_5 = attention_weights((*eb[:2], tie(eb[2]), *eb[3:]), enc[4], enc[0], enc[0])
     mark(unit_5)
     half_5.send(first_half(unit_5))
@@ -1368,7 +1364,7 @@
     )
     mark(dec_part)
     half_5.wait()
-    unit_3 = attention_weights(sb, dec[4], dec[0], dec[0])
+    unit_3 = attention_weights((*sb[:2], tie(sb[2]), *sb[3:]), dec[4], dec[0], dec[0])
     tables = []
     for table in (enc_table, dec_table):
         flat = table.reshape(1, -1)
@@ -1383,12 +1379,10 @@
     )
     small = smalls[0]
     if split_units:
-        unit_2, unit_4a = wholes[0], gathered[0]
+        unit_4a = gathered[0]
         unit_3, unit_4b, unit_5 = units
     else:
-        unit_2, unit_4a, unit_3, unit_4b, unit_5 = lax.psum(
-            (unit_2, unit_4a, unit_3, unit_4b, unit_5), "dp"
-        )
+        unit_4a, unit_3, unit_4b, unit_5 = lax.psum((unit_4a, unit_3, unit_4b, unit_5), "dp")
     enc_grad, dec_grad, result = closing(
         x0, eb[0], row(encoder_attn_gain), totals[0], y0, sb[0], row(decoder_attn_gain), totals[1],
         both[0], totals[2],
@@ -1418,8 +1412,8 @@
         small[3],
         *matrices(unit_2),
         small[4],
-        dec_ffn[:width],
-        dec_ffn[width:],
+        unit_1a,
+        unit_1b,
     )
 
 

time: 726 us -> 716 us (0.986)
  Pallas kernels: 606 us -> 568 us
  waiting for transfers between devices: 32.2 us -> 60.5 us
    pallas_call x13, Pallas kernels: 201 us -> 180 us  [call(): pl.pallas_call(kernel, grid=grid, in_specs=[spec for _, spec in inputs],...]
    pallas_call x5, Pallas kernels: 405 us -> 387 us  [sums(): pl.pallas_call(kernel, in_specs=[whole(a.shape) for a in inputs], out_spe...]
    ppermute x2, waiting for transfers between devices: 0.01 us -> 17 us  [first_swap(): return lax.ppermute(value, 'dp', pairs)]
    slice x5 -> x0, local copies, waits for them, and re-layouts: 9.34 us -> none  [the longest x1 4.86 us: body(): dec_ffn[width:]]
    ppermute x6, waiting for transfers between devices: 26.8 us -> 34.5 us  [chip_swap(): return lax.ppermute(value, 'mp', CHIP_SWAP)]
    unnamed x82 -> x96, local copies, waits for them, and re-layouts: 11 us -> 17.9 us
  transfers between devices with their start and end apart: 22 -> 22, of which waited for: 9 -> 11; matrix products, arithmetic and copies ran while one was open for 4% -> 3% of each run, Pallas kernels for 54% -> 66%
where the time goes in v2:
time: 716 us; the launch traced here: 706 us
  Pallas kernels  568 us (79%)
  waiting for transfers between devices  60.5 us (8%)
  local copies, waits for them, and re-layouts  34.2 us (5%)
  starting transfers between devices  15.1 us (2%)
  between operations  14.8 us (2%)
  matrix products  11.5 us (2%)
    pallas_call x5, Pallas kernels, sums(): pl.pallas_call(kernel, in_specs=[whole(a.shape) for a in inputs], out_spe...  387 us
    pallas_call x13, Pallas kernels, call(): pl.pallas_call(kernel, grid=grid, in_specs=[spec for _, spec in inputs],...  180 us
    ppermute x6, waiting for transfers between devices, chip_swap(): return lax.ppermute(value, 'mp', CHIP_SWAP)  34.5 us
    unnamed x96, local copies, waits for them, and re-layouts  17.9 us
    ppermute x2, waiting for transfers between devices, first_swap(): return lax.ppermute(value, 'dp', pairs)  17 us
  transfers between devices with their start and end apart: 22, of which 11 were waited for; matrix products, arithmetic and copies ran while one was open for 3% of the time, Pallas kernels for 66%

profile of v2, /device:TPU:0, one launch (start us, length us, event | category | flops | bytes accessed | tf_op | source)
XLA Modules:
  0.0 706.1 jit_solution(8103565037739627260)
XLA Ops:
  8.3 3.0 collective-permute-start.1
  12.3 1.3 broadcast_in_dim.42.refs_2_.egain_ref
  13.6 1.4 copy.66.refs_7_.refs_17_
  15.0 1.4 pad_add_fusion
  16.3 12.8 %encoder_attention.1 = (bf16[1024,768]{1,0:T(8,128)(2,1)}, bf16[1024,192]{1,0:T(8,128)(2,1)}, bf16[1024,192]{1,0:T(8,128)(2,1)}, bf16[1024,192]{1,0:T(8,128)(2,1...) custom-call(s32[1,8]{1,0:T(1,128)} %refs_2_.6, bf16[1024,768]{1,0:T(8,128)(2,1)} %bitcast.59, ...), custom_call_target="tpu_custom_call" | custom-call | flops 1248 | bytes 6 | tf_op jit(solution)/shard_map/encoder_attention/pallas_call | solution.py:534
  30.5 1.9 collective-permute-start.2
  34.3 11.1 %decoder_attention.1 = (bf16[1024,768]{1,0:T(8,128)(2,1)}, bf16[1024,192]{1,0:T(8,128)(2,1)}, bf16[1024,192]{1,0:T(8,128)(2,1)}, bf16[1024,192]{1,0:T(8,128)(2,1...) custom-call(s32[1,8]{1,0:T(1,128)} %refs_2_.7, bf16[1024,768]{1,0:T(8,128)(2,1)} %bitcast.55, ...), custom_call_target="tpu_custom_call" | custom-call | flops 1248 | bytes 6 | tf_op jit(solution)/shard_map/decoder_attention/pallas_call | solution.py:534
  45.4 4.5 collective-permute-done.2.refs_3_
  49.8 1.6 collective-permute-start.7
  54.6 12.0 %ffn_forward.1 = (f32[1024,768]{1,0:T(8,128)}, bf16[1024,768]{1,0:T(8,128)(2,1)}, f32[1024,768]{1,0:T(8,128)}, bf16[1024,768]{1,0:T(8,128)(2,1)}, f32[1024,768]{1,0:T(8,128)}) custom-call(s32[1]{0:T(128)} %bitcast.refs_0_, bf16[1024,768]{1,0:T(8,128)(2,1)} %bitcast.60, f32[192,1024]{1,0:T(8,128)} %get-tuple-element.169.refs_2_, ...), custom_call_target="tpu_custom_call" | custom-call | flops 3456 | bytes 21 | tf_op jit(solution)/shard_map/ffn_forward/pallas_call | solution.py:534
  66.6 3.4 collective-permute-done.7.refs_5_
  70.0 43.8 %sums.5.refs_13_ = f32[1024,768]{1,0:T(8,128)} custom-call(f32[1024,768]{1,0:T(8,128)} %get-tuple-element.184.refs_0_), custom_call_target="tpu_custom_call" | custom-call | flops 1 | bytes 1 | tf_op jit(solution)/shard_map/sums/pallas_call | solution.py:1058
  115.5 4.3 collective-permute-done.11.refs_6_
  119.7 1.1 collective-permute-done.10.refs_7_
  122.5 17.8 %cross_forward.1 = (f32[1024,768]{1,0:T(8,128)}, bf16[1024,768]{1,0:T(8,128)(2,1)}, bf16[1024,768]{1,0:T(8,128)(2,1)}, bf16[1024,192]{1,0:T(8,128)(2,1)}, bf16[1...) custom-call(s32[1]{0:T(128)} %bitcast.refs_0_, ...), custom_call_target="tpu_custom_call" | custom-call | flops 2400 | bytes 24 | tf_op jit(solution)/shard_map/cross_forward/pallas_call | solution.py:534
  140.3 1.2 collective-permute-start.12
  141.6 18.9 %collective-permute-done.12.refs_3_ = f32[192,1024]{1,0:T(8,128)S(1)} collective-permute-done((f32[192,1024]{1,0:T(8,128)}, f32[192,1024]{1,0:T(8,128)S(1)}, u32[]{:S(2)}, u32[]{:S(2)}) %collective-permute-start.12) | collective-permute-done | bytes 786464 | tf_op jit(solution)/shard_map/ppermute | solution.py:1104
  161.1 1.6 collective-permute-done.13.refs_5_
  163.6 15.0 %ffn_both.1 = (f32[1024,768]{1,0:T(8,128)}, bf16[1024,768]{1,0:T(8,128)(2,1)}, bf16[1024,768]{1,0:T(8,128)(2,1)}, bf16[1024,768]{1,0:T(8,128)(2,1)}, f32[1024,768]{1,0:T(8,128)}, /*index=5*/f32[1024,768]{1,0:T(8,128)}) custom-call(s32[1]{0:T(128)} %bitcast.refs_0_, f32[1024,768]{1,0:T(8,128)} %get-tuple-element.203.refs_1_.refs_4_, ...), custom_call_target="tpu_custom_call" | custom-call | flops 5760 | bytes 27 | tf_op jit(solution)/shard_map/ffn_both/pallas_call | solution.py:534
  178.7 43.5 %sums.6.refs_5_ = f32[1024,768]{1,0:T(8,128)} custom-call(f32[1024,768]{1,0:T(8,128)} %get-tuple-element.205.refs_0_), custom_call_target="tpu_custom_call" | custom-call | flops 1 | bytes 1 | tf_op jit(solution)/shard_map/sums/pallas_call | solution.py:1058
  222.2 20.6 %cross_back.1 = (f32[1024,768]{1,0:T(8,128)}, bf16[1024,768]{1,0:T(8,128)(2,1)}, bf16[1024,192]{1,0:T(8,128)(2,1)}, bf16[1024,192]{1,0:T(8,128)(2,1)}, bf16[1024...) custom-call(s32[1]{0:T(128)S(6)} %rem.32.refs_0_, s32[1,8]{1,0:T(1,128)} %refs_2_.7, ...), custom_call_target="tpu_custom_call" | custom-call | flops 2112 | bytes 21 | tf_op jit(solution)/shard_map/cross_back/pallas_call | solution.py:534
  242.9 2.9 fusion.5
  245.7 6.0 attention_weights.3
  251.7 2.8 fusion
  254.5 45.1 %sums.7 = (f32[1024,768]{1,0:T(8,128)}, f32[512,768]{1,0:T(8,128)}) custom-call(f32[1024,768]{1,0:T(8,128)} %get-tuple-element.224.refs_0_, f32[1024,768]{1,0:T(8,128)} %get-tuple-element.214.refs_1_), custom_call_target="tpu_custom_call" | custom-call | flops 1 | bytes 1 | tf_op jit(solution)/shard_map/sums/pallas_call | solution.py:1058
  299.7 9.8 %ffn_backward.1 = (f32[1024,768]{1,0:T(8,128)}, bf16[1024,768]{1,0:T(8,128)(2,1)}, bf16[1024,768]{1,0:T(8,128)(2,1)}, f32[1024,768]{1,0:T(8,128)}) custom-call(bf16[1024,768]{1,0:T(8,128)(2,1)} %bitcast.67, f32[1024,768]{1,0:T(8,128)} %get-tuple-element.225.sum_ref, f32[1024,768]{1,0:T(8,128)} %get-tuple-element.226.hid_ref, bf16[768,768]{1,0:T(8,128)(2,1)} %wi_ref.1, ...), custom_call_target="tpu_custom_call" | custom-call | flops 2304 | bytes 18 | tf_op jit(solution)/shard_map/ffn_backward/pallas_call | solution.py:534
  309.5 4.4 fusion.6.refs_1_
  313.9 1.4 fusion.7.refs_5_
  315.4 71.0 %sums.8 = (f32[1024,768]{1,0:T(8,128)}, f32[96,768]{1,0:T(8,128)}) custom-call(f32[1024,768]{1,0:T(8,128)} %get-tuple-element.235.refs_0_, f32[768,768]{1,0:T(8,128)} %fusion.6.refs_1_), custom_call_target="tpu_custom_call" | custom-call | flops 1 | bytes 1 | tf_op jit(solution)/shard_map/sums/pallas_call | solution.py:1058
  386.9 4.4 collective-permute-start.15
  392.3 26.0 %encoder_back.1 = (f32[1024,768]{1,0:T(8,128)}, bf16[1024,768]{1,0:T(8,128)(2,1)}, bf16[1024,192]{1,0:T(8,128)(2,1)}, bf16[1024,192]{1,0:T(8,128)(2,1)}, bf16[10...) custom-call(s32[1]{0:T(128)S(6)} %rem.32.refs_0_, ...), custom_call_target="tpu_custom_call" | custom-call | flops 2112 | bytes 21 | tf_op jit(solution)/shard_map/encoder_back/pallas_call | solution.py:534
  418.4 7.8 %collective-permute-done.15.refs_6_ = f32[512,768]{1,0:T(8,128)} collective-permute-done((f32[512,768]{1,0:T(8,128)}, f32[512,768]{1,0:T(8,128)}, u32[]{:S(2)}, u32[]{:S(2)}) %collective-permute-start.15) | collective-permute-done | bytes 1572896 | tf_op jit(solution)/shard_map/ppermute | solution.py:1104
  426.2 4.3 collective-permute-done.18.refs_8_
  430.5 6.7 attention_weights.4.refs_6_
  437.2 2.4 constant_dynamic-slice_fusion
  439.8 1.1 copy-done.12
  440.9 24.6 %decoder_back.1 = (f32[1024,768]{1,0:T(8,128)}, bf16[1024,768]{1,0:T(8,128)(2,1)}, bf16[1024,192]{1,0:T(8,128)(2,1)}, bf16[1024,192]{1,0:T(8,128)(2,1)}, bf16[10...) custom-call(s32[1]{0:T(128)S(6)} %rem.32.refs_0_, ...), custom_call_target="tpu_custom_call" | custom-call | flops 2112 | bytes 24 | tf_op jit(solution)/shard_map/decoder_back/pallas_call | solution.py:534
  465.5 12.7 %collective-permute-done.19.refs_9_ = f32[384,768]{1,0:T(8,128)S(1)} collective-permute-done((f32[384,768]{1,0:T(8,128)}, f32[384,768]{1,0:T(8,128)S(1)}, u32[]{:S(2)}, u32[]{:S(2)}) %collective-permute-start.19) | collective-permute-done | bytes 1179680 | tf_op jit(solution)/shard_map/ppermute | solution.py:1088
  478.3 6.3 attention_weights.5.refs_4_
  485.4 184.0 %sums.9 = (f32[1024,768]{1,0:T(8,128)}, f32[1024,768]{1,0:T(8,128)}, f32[1024,768]{1,0:T(8,128)}, f32[768,768]{1,0:T(8,128)}, f32[768,768]{1,0:T(8,128)}, /*inde...) custom-call(f32[1024,768]{1,0:T(8,128)} %get-tuple-element.244.refs_0_, ...), custom_call_target="tpu_custom_call" | custom-call | flops 1 | bytes 1 | tf_op jit(solution)/shard_map/sums/pallas_call | solution.py:1058
  669.4 11.4 %closing.1 = (f32[1024,768]{1,0:T(8,128)}, f32[1024,768]{1,0:T(8,128)}, bf16[1024,768]{1,0:T(8,128)(2,1)}) custom-call(bf16[1024,768]{1,0:T(8,128)(2,1)} %bitcast.62, f32[1024,768]{1,0:T(8,128)} %get-tuple-element.243.eb_ref, f32[1,768]{1,0:T(1,128)} %broadcast_in_dim.42.refs_2_.egain_ref, f32[1024,768]{1,0:T(8,128)} %get-tuple-element.284.z_ref, ...), custom_call_target="tpu_custom_call" | custom-call | flops 15 | bytes 28 | tf_op jit(solution)/shard_map/closing/pallas_call | solution.py:534
  683.0 1.4 fusion.4
  685.5 1.4 fusion.3
  687.0 3.2 fusion.2
  690.1 1.4 copy.81
  692.7 1.4 copy.82
  695.2 1.4 copy.83
  697.7 1.4 copy.84
  (142 shorter events, 22.5 us)
Async XLA Ops:
  7.2 107.0 %all-gather.2.cloned.1.call-start = ((), (), s32[]{:S(2)}) async-start(), calls=%async_computation | async-start | bytes 1327104 | tf_op jit(solution)/shard_map/all_gather | solution.py:1249
  8.3 43.2 %copy-start.5 = (f32[192,768]{1,0:T(8,128)}, f32[192,768]{1,0:T(8,128)S(1)}, u32[]{:S(2)}) copy-start(f32[192,768]{1,0:T(8,128)S(1)} %convert_element_type.13.refs_6_) | copy-start | bytes 1769476
  8.3 24.1 %copy-start.28 = (f32[768]{0:T(1024)S(1)}, f32[768]{0:T(1024)}, u32[]{:S(2)}) copy-start(f32[768]{0:T(1024)} %param.46) | copy-start | bytes 9220
  8.3 24.7 %copy-start.37 = (f32[32,3]{0,1:T(4,128)S(1)}, f32[32,3]{0,1:T(4,128)}, u32[]{:S(2)}) copy-start(f32[32,3]{0,1:T(4,128)} %param.51) | copy-start | bytes 1156
  8.3 25.4 %copy-start.27 = (s32[1024]{0:T(1024)S(1)}, s32[1024]{0:T(1024)}, u32[]{:S(2)}) copy-start(s32[1024]{0:T(1024)} %param.36) | copy-start | bytes 12292
  8.3 20.9 %collective-permute-start.1 = (f32[192,768]{1,0:T(8,128)S(1)}, f32[192,768]{1,0:T(8,128)}, u32[]{:S(2)}, u32[]{:S(2)}) collective-permute-start(f32[192,768]{1,0:T(8,128)S(1)} %convert_element_type.13.refs_6_), channel_id=1, source_target_pairs={{0,2},{2,0},{1,3},{3,1},{4,6},{6,4},{5,7},{7,5},{8,10},{10,8},{9,1... | collective-permute-start | bytes 1769480 | tf_op jit(solution)/shard_map/ppermute | solution.py:1104
  12.1 17.0 %collective-permute-start = (f32[24,1536]{1,0:T(8,128)S(1)}, f32[24,1536]{1,0:T(8,128)S(1)}, u32[]{:S(2)}, u32[]{:S(2)}) collective-permute-start(f32[24,1536]{1,0:T(8,128)S(1)} %maximum_convert_fusion.1), channel_id=1, source_target_pairs={{0,2},{2,0},{1,3},{3,1},{4,6},{6,4},{5,7},{7,5},{8,10},{10,8},{9,1... | collective-permute-start | bytes 442376 | tf_op jit(solution)/shard_map/ppermute | solution.py:1104
  29.1 22.8 %copy-start.29 = (f32[768]{0:T(1024)S(1)}, f32[768]{0:T(1024)}, u32[]{:S(2)}) copy-start(f32[768]{0:T(1024)} %param.43) | copy-start | bytes 9220
  29.1 23.4 %copy-start.13 = (bf16[192,768]{1,0:T(8,128)(2,1)S(1)}, bf16[192,768]{1,0:T(8,128)(2,1)}, u32[]{:S(2)}) copy-start(bf16[192,768]{1,0:T(8,128)(2,1)} %refs_7_.4) | copy-start | bytes 884740
  29.2 23.4 %copy-start.14 = (bf16[192,768]{1,0:T(8,128)(2,1)S(1)}, bf16[192,768]{1,0:T(8,128)(2,1)}, u32[]{:S(2)}) copy-start(bf16[192,768]{1,0:T(8,128)(2,1)} %refs_10_.1) | copy-start | bytes 884740
  29.9 657.1 %all-reduce.6.cloned.1.call-start = ((), (), s32[]{:S(2)}) async-start(), calls=%async_computation.1 | async-start | bytes 14155776 | tf_op jit(solution)/shard_map/psum | solution.py:1319
  30.5 19.4 %collective-permute-start.2 = (f32[192,1024]{1,0:T(8,128)}, f32[192,1024]{1,0:T(8,128)}, u32[]{:S(2)}, u32[]{:S(2)}) collective-permute-start(f32[192,1024]{1,0:T(8,128)} %get-tuple-element.169.refs_2_), channel_id=1, source_target_pairs={{0,2},{2,0},{1,3},{3,1},{4,6},{6,4},{5,7},{7,5},{8,10},{10,8},{9,1... | collective-permute-start | bytes 2359304 | tf_op jit(solution)/shard_map/ppermute | solution.py:1104
  34.3 18.4 %collective-permute-start.6 = (f32[192,1024]{1,0:T(8,128)}, f32[192,1024]{1,0:T(8,128)}, u32[]{:S(2)}, u32[]{:S(2)}) collective-permute-start(f32[192,1024]{1,0:T(8,128)} %get-tuple-element.169.refs_2_), channel_id=1, source_target_pairs={{0,1},{1,0},{2,3},{3,2},{4,5},{5,4},{6,7},{7,6},{8,9},{9,8},{10,11... | collective-permute-start | bytes 2359304 | tf_op jit(solution)/shard_map/ppermute | solution.py:1100
  49.8 4.8 collective-permute-start.3
  49.8 20.2 %collective-permute-start.7 = (f32[192,1024]{1,0:T(8,128)}, f32[192,1024]{1,0:T(8,128)S(1)}, u32[]{:S(2)}, u32[]{:S(2)}) collective-permute-start(f32[192,1024]{1,0:T(8,128)} %get-tuple-element.188.refs_4_), channel_id=1, source_target_pairs={{0,2},{2,0},{1,3},{3,1},{4,6},{6,4},{5,7},{7,5},{8,10},{10,8},{9,1... | collective-permute-start | bytes 2359304 | tf_op jit(solution)/shard_map/ppermute | solution.py:1104
  51.4 2.1 collective-permute-start.5
  51.7 3.0 collective-permute-start.4
  52.7 61.1 %copy-start = (f32[192,1536]{1,0:T(8,128)}, f32[192,1536]{1,0:T(8,128)S(1)}, u32[]{:S(2)}) copy-start(f32[192,1536]{1,0:T(8,128)S(1)} %maximum_convert_fusion.refs_8_.refs_6_) | copy-start | bytes 3538948
  70.0 43.8 %copy-start.17 = (f32[192,1024]{1,0:T(8,128)}, f32[192,1024]{1,0:T(8,128)S(1)}, u32[]{:S(2)}) copy-start(f32[192,1024]{1,0:T(8,128)S(1)} %collective-permute-done.7.refs_5_) | copy-start | bytes 2359300
  70.0 44.9 %copy-start.30 = (f32[768]{0:T(1024)S(1)}, f32[768]{0:T(1024)}, u32[]{:S(2)}) copy-start(f32[768]{0:T(1024)} %param.52) | copy-start | bytes 9220
  113.8 7.1 %collective-permute-start.9 = (f32[192,1536]{1,0:T(8,128)S(1)}, f32[192,1536]{1,0:T(8,128)S(1)}, u32[]{:S(2)}, u32[]{:S(2)}) collective-permute-start(f32[192,1536]{1,0:T(8,128)S(1)} %maximum_convert_fusion.refs_8_.refs_6_), channel_id=1, source_target_pairs={{0,1},{1,0},{2,3},{3,2},{4,5},{5,4},{6,7},{7,6},{8,9},{9,8},{10,11... | collective-permute-start | bytes 3538952 | tf_op jit(solution)/shard_map/ppermute | solution.py:1100
  114.2 6.6 collective-permute-start.8
  114.4 5.4 collective-permute-start.11
  114.8 6.1 collective-permute-start.10
  122.5 37.9 %copy-start.31 = (f32[768]{0:T(1024)S(1)}, f32[768]{0:T(1024)}, u32[]{:S(2)}) copy-start(f32[768]{0:T(1024)} %param.57) | copy-start | bytes 9220
  140.3 20.1 %collective-permute-start.12 = (f32[192,1024]{1,0:T(8,128)}, f32[192,1024]{1,0:T(8,128)S(1)}, u32[]{:S(2)}, u32[]{:S(2)}) collective-permute-start(f32[192,1024]{1,0:T(8,128)} %get-tuple-element.198.refs_2_), channel_id=1, source_target_pairs={{0,2},{2,0},{1,3},{3,1},{4,6},{6,4},{5,7},{7,5},{8,10},{10,8},{9,1... | collective-permute-start | bytes 2359304 | tf_op jit(solution)/shard_map/ppermute | solution.py:1104
  141.5 19.6 %collective-permute-start.14 = (f32[192,1024]{1,0:T(8,128)}, f32[192,1024]{1,0:T(8,128)S(1)}, u32[]{:S(2)}, u32[]{:S(2)}) collective-permute-start(f32[192,1024]{1,0:T(8,128)} %get-tuple-element.198.refs_2_), channel_id=1, source_target_pairs={{0,1},{1,0},{2,3},{3,2},{4,5},{5,4},{6,7},{7,6},{8,9},{9,8},{10,11... | collective-permute-start | bytes 2359304 | tf_op jit(solution)/shard_map/ppermute | solution.py:1100
  160.4 2.3 collective-permute-start.13
  222.2 20.6 %copy-start.41 = (bf16[1024,768]{1,0:T(8,128)(2,1)S(1)}, bf16[1024,768]{1,0:T(8,128)(2,1)}, u32[]{:S(2)}) copy-start(bf16[1024,768]{1,0:T(8,128)(2,1)} %get-tuple-element.215) | copy-start | bytes 4718596
  222.2 20.6 %copy-start.42 = (bf16[1024,768]{1,0:T(8,128)(2,1)S(1)}, bf16[1024,768]{1,0:T(8,128)(2,1)}, u32[]{:S(2)}) copy-start(bf16[1024,768]{1,0:T(8,128)(2,1)} %get-tuple-element.216) | copy-start | bytes 4718596
  245.7 6.0 copy-start.40
  299.7 9.8 %copy-start.39 = (bf16[1024,768]{1,0:T(8,128)(2,1)S(1)}, bf16[1024,768]{1,0:T(8,128)(2,1)}, u32[]{:S(2)}) copy-start(bf16[1024,768]{1,0:T(8,128)(2,1)} %get-tuple-element.231) | copy-start | bytes 4718596
  315.4 75.8 %copy-start.2 = (f32[768,768]{1,0:T(8,128)}, f32[768,768]{1,0:T(8,128)S(1)}, u32[]{:S(2)}) copy-start(f32[768,768]{1,0:T(8,128)S(1)} %fusion.7.refs_5_) | copy-start | bytes 7077892
  386.4 32.0 %collective-permute-start.16 = (f32[512,768]{1,0:T(8,128)}, f32[512,768]{1,0:T(8,128)}, u32[]{:S(2)}, u32[]{:S(2)}) collective-permute-start(f32[512,768]{1,0:T(8,128)} %get-tuple-element.247.refs_5_), channel_id=1, source_target_pairs={{0,1},{1,0},{2,3},{3,2},{4,5},{5,4},{6,7},{7,6},{8,9},{9,8},{10,11... | collective-permute-start | bytes 4718600 | tf_op jit(solution)/shard_map/ppermute | solution.py:1100
  386.9 39.3 %collective-permute-start.15 = (f32[512,768]{1,0:T(8,128)}, f32[512,768]{1,0:T(8,128)}, u32[]{:S(2)}, u32[]{:S(2)}) collective-permute-start(f32[512,768]{1,0:T(8,128)} %get-tuple-element.247.refs_5_), channel_id=1, source_target_pairs={{0,2},{2,0},{1,3},{3,1},{4,6},{6,4},{5,7},{7,5},{8,10},{10,8},{9,1... | collective-permute-start | bytes 4718600 | tf_op jit(solution)/shard_map/ppermute | solution.py:1104
  392.3 38.1 %collective-permute-start.18 = (f32[384,768]{1,0:T(8,128)}, f32[384,768]{1,0:T(8,128)S(1)}, u32[]{:S(2)}, u32[]{:S(2)}) collective-permute-start(f32[384,768]{1,0:T(8,128)} %bitcast.18), channel_id=1, source_target_pairs={{0,4},{4,0},{8,12},{12,8},{16,20},{20,16},{24,28},{28,24},{1,5},{5... | collective-permute-start | bytes 3538952 | tf_op jit(solution)/shard_map/ppermute | solution.py:1088
  426.2 13.6 %collective-permute-start.17 = (f32[512,768]{1,0:T(8,128)}, f32[512,768]{1,0:T(8,128)S(1)}, u32[]{:S(2)}, u32[]{:S(2)}) collective-permute-start(f32[512,768]{1,0:T(8,128)} %collective-permute-done.15.refs_6_), channel_id=1, source_target_pairs={{0,1},{1,0},{2,3},{3,2},{4,5},{5,4},{6,7},{7,6},{8,9},{9,8},{10,11... | collective-permute-start | bytes 4718600 | tf_op jit(solution)/shard_map/ppermute | solution.py:1100
  430.5 6.7 copy-start.15
  439.6 38.6 %collective-permute-start.19 = (f32[384,768]{1,0:T(8,128)}, f32[384,768]{1,0:T(8,128)S(1)}, u32[]{:S(2)}, u32[]{:S(2)}) collective-permute-start(f32[384,768]{1,0:T(8,128)} %bitcast.20), channel_id=1, source_target_pairs={{0,4},{4,0},{8,12},{12,8},{16,20},{20,16},{24,28},{28,24},{1,5},{5... | collective-permute-start | bytes 3538952 | tf_op jit(solution)/shard_map/ppermute | solution.py:1088
  478.2 6.3 copy-start.16
  478.2 6.3 copy-start.25
  478.2 6.5 copy-start.32
  478.2 6.5 copy-start.33
  478.2 6.5 copy-start.34
  478.2 6.5 copy-start.35
  478.2 6.5 copy-start.36
  669.4 11.4 %copy-start.26 = (f32[8,768]{1,0:T(8,128)S(1)}, f32[8,768]{1,0:T(8,128)}, u32[]{:S(2)}) copy-start(f32[8,768]{1,0:T(8,128)} %get-tuple-element.291) | copy-start | bytes 73732
  669.4 13.6 %copy-start.11 = (f32[768,768]{1,0:T(8,128)S(1)}, f32[768,768]{1,0:T(8,128)}, u32[]{:S(2)}) copy-start(f32[768,768]{1,0:T(8,128)} %get-tuple-element.292) | copy-start | bytes 7077892
  (18 other events, 42.1 us)
Sparse Core Ops, SparseCore 0:
  30.0 42.6 all-gather.1
  254.7 276.4 all-reduce.5

commit v3 on v2

--- a/solution.py
+++ b/solution.py
@@ -987,8 +987,9 @@
     outputs += [((a.shape[0] * shares, model), F32) for a in gather]
     outputs += [(a.shape, F32) for a in (*units, *smalls)]
     lands = []
+    chunks = 2 * CHUNKS if len(parts) == 1 else CHUNKS
     for a in parts:
-        lands += [pltpu.VMEM((CHUNKS, a.shape[0] // (2 * CHUNKS), model), F32)] * 2
+        lands += [pltpu.VMEM((chunks, a.shape[0] // (2 * chunks), model), F32)] * 2
     for a in near:
         lands.append(pltpu.VMEM((a.shape[0] // 2, model), F32))
     for a in (*scatter, *units):
@@ -996,7 +997,7 @@
     for a in smalls:
         lands += [pltpu.VMEM((2 + len(bits), *a.shape), F32)] * 2
     count, ends = len(inputs), len(inputs) + len(outputs)
-    total = 3 * CHUNKS * len(parts) + len(near) + len(smalls) * (2 + len(bits))
+    total = 3 * chunks * len(parts) + len(near) + len(smalls) * (2 + len(bits))
     total += len(bits) * PIECES * (len(scatter) + len(gather) + 2 * len(units))
 
     def kernel(*refs):
@@ -1006,7 +1007,7 @@
         greet(bits if dp else [])
         copies = Copies(refs[-2], refs[-1])
         for _ in parts:
-            mp_job(copies, ins.pop(0), scratch.pop(0), scratch.pop(0), outs.pop(0), CHUNKS)
+            mp_job(copies, ins.pop(0), scratch.pop(0), scratch.pop(0), outs.pop(0), chunks)
         for _ in near:
             near_job(copies, ins.pop(0), scratch.pop(0), outs.pop(0))
         for a in scatter:
@@ -1328,10 +1329,7 @@
     mark(unit_4a)
     unit_4b = project_weight(tie(ffn[3]), back[1])
     mark(unit_4b)
-    totals, _, shares, _, _, _ = sums(
-        4, parts=[tie(back[3])], scatter=[unit_4a] if split_units else []
-    )
-    dn = totals[0]
+    dn = sums(4, parts=[tie(back[3])])[0][0]
     mark(dn)
     half_4b, half_5 = [Wire(chain, first_swap) for _ in range(2)]
     half_4b.send(first_half(unit_4b))
@@ -1348,11 +1346,11 @@
     )
     mark(enc_part)
     own_beside.wait()
+    unit_5 = attention_weights((*eb[:2], tie(eb[2]), *eb[3:]), enc[4], enc[0], enc[0])
+    mark(unit_5)
     own_far.wait()
     own_relay.send(own_far.value)
     half_4b.wait()
-    unit_5 = attention_weights((*eb[:2], tie(eb[2]), *eb[3:]), enc[4], enc[0], enc[0])
-    mark(unit_5)
     half_5.send(first_half(unit_5))
     own_relay.wait()
 
@@ -1363,24 +1361,24 @@
         "decoder_back",
     )
     mark(dec_part)
+    unit_3 = attention_weights((*sb[:2], tie(sb[2]), *sb[3:]), dec[4], dec[0], dec[0])
+    mark(unit_3)
     half_5.wait()
-    unit_3 = attention_weights((*sb[:2], tie(sb[2]), *sb[3:]), dec[4], dec[0], dec[0])
     tables = []
     for table in (enc_table, dec_table):
         flat = table.reshape(1, -1)
         tables.append(jnp.pad(flat, ((0, 0), (0, width - flat.shape[1]))))
     blank = jnp.zeros((1, width), F32)
     small = jnp.concatenate([enc_gain, dec_gain, eb[5], sb[5], cb[5], *tables, blank], axis=0)
-    units = [unit_3, unit_4b, unit_5] if split_units else []
+    units = [unit_3, unit_4a, unit_4b, unit_5] if split_units else []
     halves = [half_4b.value, half_5.value] if split_units else []
-    totals, _, _, gathered, units, smalls = sums(
-        5, parts=[enc_part, dec_part, both[5]], gather=shares, units=units, halves=halves,
+    totals, _, _, _, units, smalls = sums(
+        5, parts=[enc_part, dec_part, both[5]], units=units, halves=halves,
         small=small, shared=2
     )
     small = smalls[0]
     if split_units:
-        unit_4a = gathered[0]
-        unit_3, unit_4b, unit_5 = units
+        unit_3, unit_4a, unit_4b, unit_5 = units
     else:
         unit_4a, unit_3, unit_4b, unit_5 = lax.psum((unit_4a, unit_3, unit_4b, unit_5), "dp")
     enc_grad, dec_grad, result = closing(

time: 716 us -> 719 us (level)
  Pallas kernels: 568 us -> 588 us
  waiting for transfers between devices: 60.5 us -> 45.8 us
    pallas_call x5, Pallas kernels: 387 us -> 406 us  [sums(): pl.pallas_call(kernel, in_specs=[whole(a.shape) for a in inputs], out_spe...]
    ppermute x6, waiting for transfers between devices: 34.5 us -> 27 us  [chip_swap(): return lax.ppermute(value, 'mp', CHIP_SWAP)]
    ppermute x2, waiting for transfers between devices: 17 us -> 9.77 us  [first_swap(): return lax.ppermute(value, 'dp', pairs)]
    unnamed x96 -> x94, local copies, waits for them, and re-layouts: 17.9 us -> 17.8 us
  transfers between devices with their start and end apart: 22 -> 22, of which waited for: 11 -> 11; matrix products, arithmetic and copies ran while one was open for 3% -> 3% of each run, Pallas kernels for 66% -> 68%
where the time goes in v3:
time: 719 us; the launch traced here: 714 us
  Pallas kernels  588 us (82%)
  waiting for transfers between devices  45.8 us (6%)
  local copies, waits for them, and re-layouts  34.6 us (5%)
  starting transfers between devices  16.5 us (2%)
  between operations  14.8 us (2%)
  matrix products  11.6 us (2%)
    pallas_call x5, Pallas kernels, sums(): pl.pallas_call(kernel, in_specs=[whole(a.shape) for a in inputs], out_spe...  406 us
    pallas_call x13, Pallas kernels, call(): pl.pallas_call(kernel, grid=grid, in_specs=[spec for _, spec in inputs],...  182 us
    ppermute x6, waiting for transfers between devices, chip_swap(): return lax.ppermute(value, 'mp', CHIP_SWAP)  27 us
    unnamed x94, local copies, waits for them, and re-layouts  17.8 us
  transfers between devices with their start and end apart: 22, of which 11 were waited for; matrix products, arithmetic and copies ran while one was open for 3% of the time, Pallas kernels for 68%

profile of v3, /device:TPU:0, one launch (start us, length us, event | category | flops | bytes accessed | tf_op | source)
XLA Modules:
  0.0 714.3 jit_solution(10799437222836424248)
XLA Ops:
  8.3 3.0 collective-permute-start.1
  12.3 1.3 broadcast_in_dim.42.refs_2_.egain_ref
  13.6 1.4 copy.66.refs_7_.refs_17_
  15.0 1.4 pad_add_fusion
  16.3 12.8 %encoder_attention.1 = (bf16[1024,768]{1,0:T(8,128)(2,1)}, bf16[1024,192]{1,0:T(8,128)(2,1)}, bf16[1024,192]{1,0:T(8,128)(2,1)}, bf16[1024,192]{1,0:T(8,128)(2,1...) custom-call(s32[1,8]{1,0:T(1,128)} %refs_2_.6, bf16[1024,768]{1,0:T(8,128)(2,1)} %bitcast.59, ...), custom_call_target="tpu_custom_call" | custom-call | flops 1248 | bytes 6 | tf_op jit(solution)/shard_map/encoder_attention/pallas_call | solution.py:534
  30.2 2.0 collective-permute-start.2
  34.0 11.1 %decoder_attention.1 = (bf16[1024,768]{1,0:T(8,128)(2,1)}, bf16[1024,192]{1,0:T(8,128)(2,1)}, bf16[1024,192]{1,0:T(8,128)(2,1)}, bf16[1024,192]{1,0:T(8,128)(2,1...) custom-call(s32[1,8]{1,0:T(1,128)} %refs_2_.7, bf16[1024,768]{1,0:T(8,128)(2,1)} %bitcast.55, ...), custom_call_target="tpu_custom_call" | custom-call | flops 1248 | bytes 6 | tf_op jit(solution)/shard_map/decoder_attention/pallas_call | solution.py:534
  45.1 4.5 collective-permute-done.2.refs_3_
  49.6 1.6 collective-permute-start.7
  54.4 12.0 %ffn_forward.1 = (f32[1024,768]{1,0:T(8,128)}, bf16[1024,768]{1,0:T(8,128)(2,1)}, f32[1024,768]{1,0:T(8,128)}, bf16[1024,768]{1,0:T(8,128)(2,1)}, f32[1024,768]{1,0:T(8,128)}) custom-call(s32[1]{0:T(128)} %bitcast.refs_0_, bf16[1024,768]{1,0:T(8,128)(2,1)} %bitcast.60, f32[192,1024]{1,0:T(8,128)} %get-tuple-element.167.refs_2_, ...), custom_call_target="tpu_custom_call" | custom-call | flops 3456 | bytes 21 | tf_op jit(solution)/shard_map/ffn_forward/pallas_call | solution.py:534
  66.3 3.4 collective-permute-done.7.refs_5_
  69.8 43.4 %sums.5.refs_13_ = f32[1024,768]{1,0:T(8,128)} custom-call(f32[1024,768]{1,0:T(8,128)} %get-tuple-element.182.refs_0_), custom_call_target="tpu_custom_call" | custom-call | flops 1 | bytes 1 | tf_op jit(solution)/shard_map/sums/pallas_call | solution.py:1059
  114.8 4.3 collective-permute-done.11.refs_6_
  119.1 1.1 collective-permute-done.10.refs_7_
  121.9 18.9 %cross_forward.1 = (f32[1024,768]{1,0:T(8,128)}, bf16[1024,768]{1,0:T(8,128)(2,1)}, bf16[1024,768]{1,0:T(8,128)(2,1)}, bf16[1024,192]{1,0:T(8,128)(2,1)}, bf16[1...) custom-call(s32[1]{0:T(128)} %bitcast.refs_0_, ...), custom_call_target="tpu_custom_call" | custom-call | flops 2400 | bytes 24 | tf_op jit(solution)/shard_map/cross_forward/pallas_call | solution.py:534
  140.8 1.2 collective-permute-start.12
  142.0 18.9 %collective-permute-done.12.refs_3_ = f32[192,1024]{1,0:T(8,128)S(1)} collective-permute-done((f32[192,1024]{1,0:T(8,128)}, f32[192,1024]{1,0:T(8,128)S(1)}, u32[]{:S(2)}, u32[]{:S(2)}) %collective-permute-start.12) | collective-permute-done | bytes 786464 | tf_op jit(solution)/shard_map/ppermute | solution.py:1105
  161.5 1.7 collective-permute-done.13.refs_5_
  164.1 15.4 %ffn_both.1 = (f32[1024,768]{1,0:T(8,128)}, bf16[1024,768]{1,0:T(8,128)(2,1)}, bf16[1024,768]{1,0:T(8,128)(2,1)}, bf16[1024,768]{1,0:T(8,128)(2,1)}, f32[1024,768]{1,0:T(8,128)}, /*index=5*/f32[1024,768]{1,0:T(8,128)}) custom-call(s32[1]{0:T(128)} %bitcast.refs_0_, f32[1024,768]{1,0:T(8,128)} %get-tuple-element.201.refs_1_.refs_4_, ...), custom_call_target="tpu_custom_call" | custom-call | flops 5760 | bytes 27 | tf_op jit(solution)/shard_map/ffn_both/pallas_call | solution.py:534
  179.5 43.2 %sums.6.refs_5_ = f32[1024,768]{1,0:T(8,128)} custom-call(f32[1024,768]{1,0:T(8,128)} %get-tuple-element.203.refs_0_), custom_call_target="tpu_custom_call" | custom-call | flops 1 | bytes 1 | tf_op jit(solution)/shard_map/sums/pallas_call | solution.py:1059
  222.7 22.6 %cross_back.1 = (f32[1024,768]{1,0:T(8,128)}, bf16[1024,768]{1,0:T(8,128)(2,1)}, bf16[1024,192]{1,0:T(8,128)(2,1)}, bf16[1024,192]{1,0:T(8,128)(2,1)}, bf16[1024...) custom-call(s32[1]{0:T(128)S(6)} %rem.32.refs_0_, s32[1,8]{1,0:T(1,128)} %refs_2_.7, ...), custom_call_target="tpu_custom_call" | custom-call | flops 2112 | bytes 21 | tf_op jit(solution)/shard_map/cross_back/pallas_call | solution.py:534
  245.3 2.9 fusion.5
  248.2 6.0 attention_weights.3
  254.2 2.9 fusion
  257.1 44.7 %sums.7 = (f32[1024,768]{1,0:T(8,128)}, f32[512,768]{1,0:T(8,128)}) custom-call(f32[1024,768]{1,0:T(8,128)} %get-tuple-element.222.refs_0_, f32[1024,768]{1,0:T(8,128)} %get-tuple-element.212.refs_1_), custom_call_target="tpu_custom_call" | custom-call | flops 1 | bytes 1 | tf_op jit(solution)/shard_map/sums/pallas_call | solution.py:1059
  301.8 9.9 %ffn_backward.1 = (f32[1024,768]{1,0:T(8,128)}, bf16[1024,768]{1,0:T(8,128)(2,1)}, bf16[1024,768]{1,0:T(8,128)(2,1)}, f32[1024,768]{1,0:T(8,128)}) custom-call(bf16[1024,768]{1,0:T(8,128)(2,1)} %bitcast.67, f32[1024,768]{1,0:T(8,128)} %get-tuple-element.223.sum_ref, f32[1024,768]{1,0:T(8,128)} %get-tuple-element.224.hid_ref, bf16[768,768]{1,0:T(8,128)(2,1)} %wi_ref.1, ...), custom_call_target="tpu_custom_call" | custom-call | flops 2304 | bytes 18 | tf_op jit(solution)/shard_map/ffn_backward/pallas_call | solution.py:534
  311.7 4.4 fusion.6.refs_4_
  316.2 1.4 fusion.7.refs_5_
  317.6 44.0 %sums.8.refs_5_ = f32[1024,768]{1,0:T(8,128)} custom-call(f32[1024,768]{1,0:T(8,128)} %get-tuple-element.233.refs_0_), custom_call_target="tpu_custom_call" | custom-call | flops 1 | bytes 1 | tf_op jit(solution)/shard_map/sums/pallas_call | solution.py:1059
  364.1 2.8 collective-permute-start.18
  366.9 25.8 %encoder_back.1 = (f32[1024,768]{1,0:T(8,128)}, bf16[1024,768]{1,0:T(8,128)(2,1)}, bf16[1024,192]{1,0:T(8,128)(2,1)}, bf16[1024,192]{1,0:T(8,128)(2,1)}, bf16[10...) custom-call(s32[1]{0:T(128)S(6)} %rem.32.refs_0_, ...), custom_call_target="tpu_custom_call" | custom-call | flops 2112 | bytes 21 | tf_op jit(solution)/shard_map/encoder_back/pallas_call | solution.py:534
  392.7 5.8 attention_weights.4.refs_6_
  398.8 5.5 collective-permute-done.18.refs_8_
  404.3 2.8 constant_dynamic-slice_fusion
  407.1 2.4 collective-permute-start.19
  409.6 1.1 copy-done.12
  410.8 24.6 %decoder_back.1 = (f32[1024,768]{1,0:T(8,128)}, bf16[1024,768]{1,0:T(8,128)(2,1)}, bf16[1024,192]{1,0:T(8,128)(2,1)}, bf16[1024,192]{1,0:T(8,128)(2,1)}, bf16[10...) custom-call(s32[1]{0:T(128)S(6)} %rem.32.refs_0_, ...), custom_call_target="tpu_custom_call" | custom-call | flops 2112 | bytes 24 | tf_op jit(solution)/shard_map/decoder_back/pallas_call | solution.py:534
  435.5 5.9 attention_weights.5.refs_3_
  441.5 4.3 collective-permute-done.19.refs_9_
  446.5 231.0 %sums.9 = (f32[1024,768]{1,0:T(8,128)}, f32[1024,768]{1,0:T(8,128)}, f32[1024,768]{1,0:T(8,128)}, f32[768,768]{1,0:T(8,128)}, f32[768,768]{1,0:T(8,128)}, /*inde...) custom-call(f32[1024,768]{1,0:T(8,128)} %get-tuple-element.241.refs_0_, ...), custom_call_target="tpu_custom_call" | custom-call | flops 1 | bytes 1 | tf_op jit(solution)/shard_map/sums/pallas_call | solution.py:1059
  677.5 11.4 %closing.1 = (f32[1024,768]{1,0:T(8,128)}, f32[1024,768]{1,0:T(8,128)}, bf16[1024,768]{1,0:T(8,128)(2,1)}) custom-call(bf16[1024,768]{1,0:T(8,128)(2,1)} %bitcast.62, f32[1024,768]{1,0:T(8,128)} %get-tuple-element.240.eb_ref, f32[1,768]{1,0:T(1,128)} %broadcast_in_dim.42.refs_2_.egain_ref, f32[1024,768]{1,0:T(8,128)} %get-tuple-element.280.z_ref, ...), custom_call_target="tpu_custom_call" | custom-call | flops 15 | bytes 28 | tf_op jit(solution)/shard_map/closing/pallas_call | solution.py:534
  691.1 1.4 fusion.4
  693.6 1.4 fusion.3
  695.1 3.2 fusion.2
  698.3 1.4 copy.81
  700.8 1.4 copy.82
  703.3 1.4 copy.83
  705.8 1.4 copy.84
  (140 shorter events, 23.3 us)
Async XLA Ops:
  7.2 106.4 %all-gather.2.cloned.1.call-start = ((), (), s32[]{:S(2)}) async-start(), calls=%async_computation | async-start | bytes 1327104 | tf_op jit(solution)/shard_map/all_gather | solution.py:1250
  8.3 42.9 %copy-start.5 = (f32[192,768]{1,0:T(8,128)}, f32[192,768]{1,0:T(8,128)S(1)}, u32[]{:S(2)}) copy-start(f32[192,768]{1,0:T(8,128)S(1)} %convert_element_type.13.refs_6_) | copy-start | bytes 1769476
  8.3 23.9 %copy-start.27 = (f32[768]{0:T(1024)S(1)}, f32[768]{0:T(1024)}, u32[]{:S(2)}) copy-start(f32[768]{0:T(1024)} %param.46) | copy-start | bytes 9220
  8.3 24.5 %copy-start.36 = (f32[32,3]{0,1:T(4,128)S(1)}, f32[32,3]{0,1:T(4,128)}, u32[]{:S(2)}) copy-start(f32[32,3]{0,1:T(4,128)} %param.51) | copy-start | bytes 1156
  8.3 25.1 %copy-start.26 = (s32[1024]{0:T(1024)S(1)}, s32[1024]{0:T(1024)}, u32[]{:S(2)}) copy-start(s32[1024]{0:T(1024)} %param.36) | copy-start | bytes 12292
  8.3 20.8 %collective-permute-start.1 = (f32[192,768]{1,0:T(8,128)S(1)}, f32[192,768]{1,0:T(8,128)}, u32[]{:S(2)}, u32[]{:S(2)}) collective-permute-start(f32[192,768]{1,0:T(8,128)S(1)} %convert_element_type.13.refs_6_), channel_id=1, source_target_pairs={{0,2},{2,0},{1,3},{3,1},{4,6},{6,4},{5,7},{7,5},{8,10},{10,8},{9,1... | collective-permute-start | bytes 1769480 | tf_op jit(solution)/shard_map/ppermute | solution.py:1105
  12.1 17.0 %collective-permute-start = (f32[24,1536]{1,0:T(8,128)S(1)}, f32[24,1536]{1,0:T(8,128)S(1)}, u32[]{:S(2)}, u32[]{:S(2)}) collective-permute-start(f32[24,1536]{1,0:T(8,128)S(1)} %maximum_convert_fusion.1), channel_id=1, source_target_pairs={{0,2},{2,0},{1,3},{3,1},{4,6},{6,4},{5,7},{7,5},{8,10},{10,8},{9,1... | collective-permute-start | bytes 442376 | tf_op jit(solution)/shard_map/ppermute | solution.py:1105
  29.1 22.6 %copy-start.28 = (f32[768]{0:T(1024)S(1)}, f32[768]{0:T(1024)}, u32[]{:S(2)}) copy-start(f32[768]{0:T(1024)} %param.43) | copy-start | bytes 9220
  29.1 23.2 %copy-start.13 = (bf16[192,768]{1,0:T(8,128)(2,1)S(1)}, bf16[192,768]{1,0:T(8,128)(2,1)}, u32[]{:S(2)}) copy-start(bf16[192,768]{1,0:T(8,128)(2,1)} %refs_7_.4) | copy-start | bytes 884740
  29.1 23.2 %copy-start.14 = (bf16[192,768]{1,0:T(8,128)(2,1)S(1)}, bf16[192,768]{1,0:T(8,128)(2,1)}, u32[]{:S(2)}) copy-start(bf16[192,768]{1,0:T(8,128)(2,1)} %refs_10_.1) | copy-start | bytes 884740
  29.9 665.2 %all-reduce.6.cloned.1.call-start = ((), (), s32[]{:S(2)}) async-start(), calls=%async_computation.1 | async-start | bytes 14155776 | tf_op jit(solution)/shard_map/psum | solution.py:1320
  30.2 19.4 %collective-permute-start.2 = (f32[192,1024]{1,0:T(8,128)}, f32[192,1024]{1,0:T(8,128)}, u32[]{:S(2)}, u32[]{:S(2)}) collective-permute-start(f32[192,1024]{1,0:T(8,128)} %get-tuple-element.167.refs_2_), channel_id=1, source_target_pairs={{0,2},{2,0},{1,3},{3,1},{4,6},{6,4},{5,7},{7,5},{8,10},{10,8},{9,1... | collective-permute-start | bytes 2359304 | tf_op jit(solution)/shard_map/ppermute | solution.py:1105
  34.0 18.4 %collective-permute-start.6 = (f32[192,1024]{1,0:T(8,128)}, f32[192,1024]{1,0:T(8,128)}, u32[]{:S(2)}, u32[]{:S(2)}) collective-permute-start(f32[192,1024]{1,0:T(8,128)} %get-tuple-element.167.refs_2_), channel_id=1, source_target_pairs={{0,1},{1,0},{2,3},{3,2},{4,5},{5,4},{6,7},{7,6},{8,9},{9,8},{10,11... | collective-permute-start | bytes 2359304 | tf_op jit(solution)/shard_map/ppermute | solution.py:1101
  49.6 4.8 collective-permute-start.3
  49.6 20.2 %collective-permute-start.7 = (f32[192,1024]{1,0:T(8,128)}, f32[192,1024]{1,0:T(8,128)S(1)}, u32[]{:S(2)}, u32[]{:S(2)}) collective-permute-start(f32[192,1024]{1,0:T(8,128)} %get-tuple-element.186.refs_4_), channel_id=1, source_target_pairs={{0,2},{2,0},{1,3},{3,1},{4,6},{6,4},{5,7},{7,5},{8,10},{10,8},{9,1... | collective-permute-start | bytes 2359304 | tf_op jit(solution)/shard_map/ppermute | solution.py:1105
  51.2 2.1 collective-permute-start.5
  51.4 3.0 collective-permute-start.4
  52.4 60.7 %copy-start = (f32[192,1536]{1,0:T(8,128)}, f32[192,1536]{1,0:T(8,128)S(1)}, u32[]{:S(2)}) copy-start(f32[192,1536]{1,0:T(8,128)S(1)} %maximum_convert_fusion.refs_8_.refs_6_) | copy-start | bytes 3538948
  69.8 43.4 %copy-start.16 = (f32[192,1024]{1,0:T(8,128)}, f32[192,1024]{1,0:T(8,128)S(1)}, u32[]{:S(2)}) copy-start(f32[192,1024]{1,0:T(8,128)S(1)} %collective-permute-done.7.refs_5_) | copy-start | bytes 2359300
  69.8 44.5 %copy-start.29 = (f32[768]{0:T(1024)S(1)}, f32[768]{0:T(1024)}, u32[]{:S(2)}) copy-start(f32[768]{0:T(1024)} %param.52) | copy-start | bytes 9220
  113.2 7.1 collective-permute-start.9
  113.6 6.6 collective-permute-start.8
  113.7 5.4 collective-permute-start.11
  114.1 6.1 collective-permute-start.10
  121.9 39.0 %copy-start.30 = (f32[768]{0:T(1024)S(1)}, f32[768]{0:T(1024)}, u32[]{:S(2)}) copy-start(f32[768]{0:T(1024)} %param.57) | copy-start | bytes 9220
  140.8 20.1 %collective-permute-start.12 = (f32[192,1024]{1,0:T(8,128)}, f32[192,1024]{1,0:T(8,128)S(1)}, u32[]{:S(2)}, u32[]{:S(2)}) collective-permute-start(f32[192,1024]{1,0:T(8,128)} %get-tuple-element.196.refs_2_), channel_id=1, source_target_pairs={{0,2},{2,0},{1,3},{3,1},{4,6},{6,4},{5,7},{7,5},{8,10},{10,8},{9,1... | collective-permute-start | bytes 2359304 | tf_op jit(solution)/shard_map/ppermute | solution.py:1105
  142.0 19.6 %collective-permute-start.14 = (f32[192,1024]{1,0:T(8,128)}, f32[192,1024]{1,0:T(8,128)S(1)}, u32[]{:S(2)}, u32[]{:S(2)}) collective-permute-start(f32[192,1024]{1,0:T(8,128)} %get-tuple-element.196.refs_2_), channel_id=1, source_target_pairs={{0,1},{1,0},{2,3},{3,2},{4,5},{5,4},{6,7},{7,6},{8,9},{9,8},{10,11... | collective-permute-start | bytes 2359304 | tf_op jit(solution)/shard_map/ppermute | solution.py:1101
  160.9 2.3 collective-permute-start.13
  222.6 22.6 %copy-start.40 = (bf16[1024,768]{1,0:T(8,128)(2,1)S(1)}, bf16[1024,768]{1,0:T(8,128)(2,1)}, u32[]{:S(2)}) copy-start(bf16[1024,768]{1,0:T(8,128)(2,1)} %get-tuple-element.213) | copy-start | bytes 4718596
  222.6 22.6 %copy-start.41 = (bf16[1024,768]{1,0:T(8,128)(2,1)S(1)}, bf16[1024,768]{1,0:T(8,128)(2,1)}, u32[]{:S(2)}) copy-start(bf16[1024,768]{1,0:T(8,128)(2,1)} %get-tuple-element.214) | copy-start | bytes 4718596
  248.2 6.0 copy-start.1
  248.2 6.0 copy-start.39
  301.8 9.9 %copy-start.38 = (bf16[1024,768]{1,0:T(8,128)(2,1)S(1)}, bf16[1024,768]{1,0:T(8,128)(2,1)}, u32[]{:S(2)}) copy-start(bf16[1024,768]{1,0:T(8,128)(2,1)} %get-tuple-element.229) | copy-start | bytes 4718596
  317.6 45.4 %copy-start.2 = (f32[768,768]{1,0:T(8,128)}, f32[768,768]{1,0:T(8,128)S(1)}, u32[]{:S(2)}) copy-start(f32[768,768]{1,0:T(8,128)S(1)} %fusion.7.refs_5_) | copy-start | bytes 7077892
  361.6 31.1 %collective-permute-start.16 = (f32[512,768]{1,0:T(8,128)}, f32[512,768]{1,0:T(8,128)}, u32[]{:S(2)}, u32[]{:S(2)}) collective-permute-start(f32[512,768]{1,0:T(8,128)} %get-tuple-element.244.refs_5_), channel_id=1, source_target_pairs={{0,1},{1,0},{2,3},{3,2},{4,5},{5,4},{6,7},{7,6},{8,9},{9,8},{10,11... | collective-permute-start | bytes 4718600 | tf_op jit(solution)/shard_map/ppermute | solution.py:1101
  362.1 36.7 %collective-permute-start.15 = (f32[512,768]{1,0:T(8,128)}, f32[512,768]{1,0:T(8,128)}, u32[]{:S(2)}, u32[]{:S(2)}) collective-permute-start(f32[512,768]{1,0:T(8,128)} %get-tuple-element.244.refs_5_), channel_id=1, source_target_pairs={{0,2},{2,0},{1,3},{3,1},{4,6},{6,4},{5,7},{7,5},{8,10},{10,8},{9,1... | collective-permute-start | bytes 4718600 | tf_op jit(solution)/shard_map/ppermute | solution.py:1105
  364.1 40.2 %collective-permute-start.18 = (f32[384,768]{1,0:T(8,128)}, f32[384,768]{1,0:T(8,128)S(1)}, u32[]{:S(2)}, u32[]{:S(2)}) collective-permute-start(f32[384,768]{1,0:T(8,128)} %bitcast.18), channel_id=1, source_target_pairs={{0,4},{4,0},{8,12},{12,8},{16,20},{20,16},{24,28},{28,24},{1,5},{5... | collective-permute-start | bytes 3538952 | tf_op jit(solution)/shard_map/ppermute | solution.py:1089
  398.6 10.9 %copy-start.23 = (f32[32,3]{1,0:T(8,128)S(1)}, f32[32,3]{1,0:T(8,128)}, u32[]{:S(2)}) copy-start(f32[32,3]{1,0:T(8,128)} %get-tuple-element.276) | copy-start | bytes 1156
  398.8 10.8 %collective-permute-start.17 = (f32[512,768]{1,0:T(8,128)}, f32[512,768]{1,0:T(8,128)S(1)}, u32[]{:S(2)}, u32[]{:S(2)}) collective-permute-start(f32[512,768]{1,0:T(8,128)} %collective-permute-done.15.refs_6_), channel_id=1, source_target_pairs={{0,1},{1,0},{2,3},{3,2},{4,5},{5,4},{6,7},{7,6},{8,9},{9,8},{10,11... | collective-permute-start | bytes 4718600 | tf_op jit(solution)/shard_map/ppermute | solution.py:1101
  404.3 31.1 %copy-start.15 = (f32[384,768]{1,0:T(8,128)}, f32[384,768]{1,0:T(8,128)S(1)}, u32[]{:S(2)}) copy-start(f32[384,768]{1,0:T(8,128)S(1)} %collective-permute-done.18.refs_8_) | copy-start | bytes 3538948
  407.1 38.7 %collective-permute-start.19 = (f32[384,768]{1,0:T(8,128)}, f32[384,768]{1,0:T(8,128)}, u32[]{:S(2)}, u32[]{:S(2)}) collective-permute-start(f32[384,768]{1,0:T(8,128)} %bitcast.20), channel_id=1, source_target_pairs={{0,4},{4,0},{8,12},{12,8},{16,20},{20,16},{24,28},{28,24},{1,5},{5... | collective-permute-start | bytes 3538952 | tf_op jit(solution)/shard_map/ppermute | solution.py:1089
  435.4 10.4 %copy-start.31 = (f32[1,768]{1,0:T(1,128)S(1)}, f32[1,768]{1,0:T(1,128)}, u32[]{:S(2)}) copy-start(f32[1,768]{1,0:T(1,128)} %get-tuple-element.275) | copy-start | bytes 9220
  435.4 10.4 %copy-start.32 = (f32[1,768]{1,0:T(1,128)S(1)}, f32[1,768]{1,0:T(1,128)}, u32[]{:S(2)}) copy-start(f32[1,768]{1,0:T(1,128)} %get-tuple-element.273) | copy-start | bytes 9220
  435.5 10.4 %copy-start.33 = (f32[1,768]{1,0:T(1,128)S(1)}, f32[1,768]{1,0:T(1,128)}, u32[]{:S(2)}) copy-start(f32[1,768]{1,0:T(1,128)} %get-tuple-element.271) | copy-start | bytes 9220
  435.5 10.4 %copy-start.34 = (f32[1,768]{1,0:T(1,128)S(1)}, f32[1,768]{1,0:T(1,128)}, u32[]{:S(2)}) copy-start(f32[1,768]{1,0:T(1,128)} %get-tuple-element.274) | copy-start | bytes 9220
  435.5 10.4 %copy-start.35 = (f32[1,768]{1,0:T(1,128)S(1)}, f32[1,768]{1,0:T(1,128)}, u32[]{:S(2)}) copy-start(f32[1,768]{1,0:T(1,128)} %get-tuple-element.272) | copy-start | bytes 9220
  677.5 11.4 %copy-start.25 = (f32[8,768]{1,0:T(8,128)S(1)}, f32[8,768]{1,0:T(8,128)}, u32[]{:S(2)}) copy-start(f32[8,768]{1,0:T(8,128)} %get-tuple-element.287) | copy-start | bytes 73732
  677.5 13.6 %copy-start.11 = (f32[768,768]{1,0:T(8,128)S(1)}, f32[768,768]{1,0:T(8,128)}, u32[]{:S(2)}) copy-start(f32[768,768]{1,0:T(8,128)} %get-tuple-element.288) | copy-start | bytes 7077892
  (17 other events, 39.7 us)
Sparse Core Ops, SparseCore 0:
  30.0 42.8 all-gather.1
  257.2 280.1 all-reduce.5
